TPU v7x, 256 devices: a whole 4x4x8 slice. The times are simulated.
256 devices in a mesh: store: 32 (over x, z), tp: 8 (over y, core).
Axes of the slice: x: 4, y: 4, z: 8, core: 2. Of those that a mesh axis runs over, the one named last changes fastest.
Arguments:
- kv_store: bfloat16 [96, 2, 256, 1024], P('store', None, None, 'tp'), may hold values from -6 to 6
- kv_scale: bfloat16 [96, 2, 8, 2], P('store', None, 'tp'), may hold values from 0.25 to 40
- span_home: int32 [96], replicated, may hold values from 0 to 95, as said below
- doc_ids: int32 [32, 20], P('store'), may hold values from 0 to 95, as said below
- doc_count: int32 [32], P('store'), may hold values from 6 to 20, as said below
- recompute_rows: int32 [32, 4, 128], P('store'), may hold values from 0 to 5119, as said below
- query_len: int32 [32], P('store'), may hold values from 1 to 256, as said below
- hidden: bfloat16 [32, 768, 4096], P('store', None, 'tp'), may hold values from -400 to 400
- norm_gain: bfloat16 [4096], replicated, may hold values from 0.5 to 1.5
- w_q: bfloat16 [4096, 4096], P(None, 'tp'), may hold values from -0.09375 to 0.09375
- w_kv: bfloat16 [4096, 2, 1024], P(None, None, 'tp'), may hold values from -0.09375 to 0.09375
Outputs:
- attn_out: bfloat16 [32, 256, 4096], P('store', None, 'tp')
- context_kv: bfloat16 [32, 2, 5120, 1024], P('store', None, None, 'tp')
Inputs may be any that keep to these rules, and one draw needn't show every extreme that they name: `span_home`: each storage position occurs once; position p lies on index p // 3 of store. `doc_ids`: the 20 ids of a request are distinct; the first doc_count are its documents; a request's ids name at most 2 spans stored on one index of store, and exactly 2 on some index. `doc_count`: some request has 20 documents. `recompute_rows`: distinct within a request and below doc_count * 256. `query_len`: some request has 256 query tokens.
All inputs are finite; a program needn't handle non-finite values.
Results may differ from a plain program's by a relative error of at most 0.015.
The roundings to bfloat16 on the way count: a program that leaves them out, or rounds other values in their place, can miss the bound.
Values may be sent and summed in bfloat16 or wider, within the bound.
No kernel may reach another device: no remote copies, remote signals or barrier semaphores. Data moves between devices by JAX's collectives and lax.ppermute only.
A program may use at most 128 MiB of HBM per device.

v0:
```python
import jax
import jax.numpy as jnp
from jax import lax
from jax.sharding import PartitionSpec as P

SPAN = 256
SB = 128
MAXDOC = 20


rope_base = 500000.0
norm_eps = 1e-05


def rope_angles(positions, head_width):
    halfway = head_width // 2
    exponent = jnp.arange(halfway, dtype=jnp.float32) * (2.0 / head_width)
    inverse_freq = jnp.power(jnp.float32(rope_base), -exponent)
    angles = positions.astype(jnp.float32)[:, None] * inverse_freq[None, :]
    return (jnp.cos(angles), jnp.sin(angles))


def rotate_half(values, cosine, sine_part):
    halfway = values.shape[-1] // 2
    low_half = values[..., :halfway]
    high_half = values[..., halfway:]
    return jnp.concatenate(
        [low_half * cosine - high_half * sine_part, high_half * cosine + low_half * sine_part],
        axis=-1,
    )


def on_device(
    kv_store,
    kv_scale,
    span_home,
    doc_ids,
    doc_count,
    recompute_rows,
    query_len,
    hidden,
    norm_gain,
    w_q,
    w_kv,
):
    peer_count = lax.axis_size("store")
    capacity = max(2, (MAXDOC + peer_count - 1) // peer_count)
    stored = kv_store.shape[0]
    head_width = kv_store.shape[3]
    blocks = kv_scale.shape[3]
    doc_list = doc_ids[0]
    doc_total = doc_count[0]
    span_index = jnp.arange(span_home.shape[0], dtype=jnp.int32)
    position = jnp.sum(
        jnp.where(doc_list[:, None] == span_index[None, :], span_home[None, :], 0), axis=1
    )
    owner_dev = position // stored
    slot_index = position % stored
    slot_range = jnp.arange(MAXDOC)
    before = slot_range[:, None] > slot_range[None, :]
    same_owner = owner_dev[:, None] == owner_dev[None, :]
    copy_rank = jnp.sum(jnp.where(before & same_owner, 1, 0), axis=1)
    mailbox = owner_dev * capacity + copy_rank
    placed = mailbox[:, None] == jnp.arange(peer_count * capacity)[None, :]
    wanted = jnp.sum(jnp.where(placed, slot_index[:, None], 0), axis=0).reshape(
        peer_count, capacity
    )
    asked = lax.all_to_all(wanted, "store", split_axis=0, concat_axis=0, tiled=True)
    asked_flat = asked.reshape(peer_count * capacity)
    send_codes = jnp.take(kv_store, asked_flat, axis=0).reshape(
        peer_count, capacity, 2, SPAN, head_width
    )
    send_scales = jnp.take(kv_scale, asked_flat, axis=0).reshape(peer_count, capacity, 2, blocks)
    got_codes, got_scales = (
        lax.all_to_all(send_codes, "store", split_axis=0, concat_axis=0, tiled=True),
        lax.all_to_all(send_scales, "store", split_axis=0, concat_axis=0, tiled=True),
    )
    codes = jnp.take(got_codes.reshape(peer_count * capacity, 2, SPAN, head_width), mailbox, axis=0)
    scales = jnp.take(got_scales.reshape(peer_count * capacity, 2, blocks), mailbox, axis=0)
    block_scale = jnp.repeat(scales.astype(jnp.float32), SB, axis=2)
    dequant = codes.astype(jnp.float32) * block_scale[..., None]
    shift_cos, shift_sin = rope_angles(jnp.arange(MAXDOC, dtype=jnp.int32) * SPAN, head_width)
    cached_keys = rotate_half(dequant[:, 0], shift_cos[:, None, :], shift_sin[:, None, :])
    context_max = MAXDOC * SPAN
    live_rows = jnp.arange(context_max) < doc_total * SPAN
    cached_keys = jnp.where(
        live_rows[:, None], cached_keys.reshape(context_max, head_width), 0.0
    ).astype(jnp.bfloat16)
    cached_values = jnp.where(
        live_rows[:, None], dequant[:, 1].reshape(context_max, head_width), 0.0
    ).astype(jnp.bfloat16)
    layer_input = lax.all_gather(hidden, "tp", axis=2, tiled=True)[0]
    features = layer_input.astype(jnp.float32)
    inverse_rms = lax.rsqrt(jnp.mean(features * features, axis=-1, keepdims=True) + norm_eps)
    normed = (features * inverse_rms * norm_gain.astype(jnp.float32)).astype(jnp.bfloat16)
    recompute_total = recompute_rows.shape[1] * recompute_rows.shape[2]
    query_rows = layer_input.shape[0] - recompute_total
    query_heads = w_q.shape[1] // head_width
    query_proj = jnp.dot(normed[recompute_total:], w_q, preferred_element_type=jnp.float32)
    kv_proj = jnp.dot(
        normed, w_kv.reshape(w_kv.shape[0], 2 * head_width), preferred_element_type=jnp.float32
    )
    kv_proj = kv_proj.reshape(-1, 2, head_width)
    flat_pos = recompute_rows[0].reshape(recompute_total)
    query_pos = doc_total * SPAN + jnp.arange(query_rows, dtype=jnp.int32)
    row_cos, row_sin = rope_angles(jnp.concatenate([flat_pos, query_pos]), head_width)
    new_keys = rotate_half(kv_proj[:, 0], row_cos, row_sin).astype(jnp.bfloat16)
    new_values = kv_proj[:, 1].astype(jnp.bfloat16)
    queries = rotate_half(
        query_proj.reshape(query_rows, query_heads, head_width),
        row_cos[recompute_total:, None, :],
        row_sin[recompute_total:, None, :],
    ).astype(jnp.bfloat16)
    patched_keys = cached_keys.at[flat_pos].set(new_keys[:recompute_total])
    patched_values = cached_values.at[flat_pos].set(new_values[:recompute_total])
    all_keys = jnp.concatenate([patched_keys, new_keys[recompute_total:]], axis=0)
    all_values = jnp.concatenate([patched_values, new_values[recompute_total:]], axis=0)
    query_matrix = jnp.transpose(queries, (1, 0, 2)).reshape(query_heads * query_rows, head_width)
    scores = lax.dot_general(
        query_matrix, all_keys, (((1,), (1,)), ((), ())), preferred_element_type=jnp.float32
    ) * head_width ** (-0.5)
    query_index = jnp.arange(query_heads * query_rows) % query_rows
    key_index = jnp.arange(context_max + query_rows)
    allowed = jnp.where(
        key_index[None, :] < context_max,
        (key_index < doc_total * SPAN)[None, :],
        key_index[None, :] - context_max <= query_index[:, None],
    )
    scores = jnp.where(allowed, scores, -jnp.inf)
    top_score = jnp.max(scores, axis=-1, keepdims=True)
    exp_terms = jnp.where(allowed, jnp.exp(scores - top_score), 0.0)
    weights = (exp_terms / jnp.sum(exp_terms, axis=-1, keepdims=True)).astype(jnp.bfloat16)
    mixed_rows = jnp.dot(weights, all_values, preferred_element_type=jnp.float32)
    mixed_rows = jnp.where((query_index < query_len[0])[:, None], mixed_rows, 0.0)
    attention = jnp.transpose(mixed_rows.reshape(query_heads, query_rows, head_width), (1, 0, 2))
    attention = attention.reshape(1, query_rows, query_heads * head_width).astype(jnp.bfloat16)
    context_kv = jnp.stack([patched_keys, patched_values], axis=0)[None]
    return (attention, context_kv)


def solution(mesh):
    placed = (
        P("store", None, None, "tp"),
        P("store", None, "tp", None),
        P(),
        P("store", None),
        P("store"),
        P("store", None, None),
        P("store"),
        P("store", None, "tp"),
        P(),
        P(None, "tp"),
        P(None, None, "tp"),
    )
    return jax.shard_map(
        on_device,
        mesh=mesh,
        in_specs=placed,
        out_specs=(P("store", None, "tp"), P("store", None, None, "tp")),
        check_vma=False,
    )
```

profile of v0, /device:TPU:96, one launch (start us, length us, event | category | flops | bytes accessed | tf_op | source)
XLA Modules:
  0.0 298.2 jit_solution(13506042400842713959)
XLA Ops:
  7.2 0.9 select_reduce_fusion.2
  8.4 0.7 all_to_all.12
  9.1 10.3 %all-to-all-start = ((s32[32,1,2]{2,1,0:T(1,128)}), s32[32,1,2]{2,1,0:T(1,128)S(1)}, u32[]{:S(2)}, u32[]{:S(2)}) async-start(s32[32,1,2]{2,1,0:T(1,128)} %bitcast.7), calls=%async_computation | async-start | bytes 32768 | tf_op jit(solution)/shard_map/all_to_all | solution.py:68
  20.1 0.8 copy.66
  20.9 5.3 %all-to-all-done = s32[32,1,2]{2,1,0:T(1,128)S(1)} async-done(((s32[32,1,2]{2,1,0:T(1,128)}), s32[32,1,2]{2,1,0:T(1,128)S(1)}, u32[]{:S(2)}, u32[]{:S(2)}) %all-to-all-start) | async-done | bytes 288 | tf_op jit(solution)/shard_map/all_to_all | solution.py:68
  29.5 6.7 %all-to-all-start.2 = ((bf16[32,2,2,2]{1,3,2,0:T(2,128)(2,1)}), bf16[32,2,2,2]{1,3,2,0:T(2,128)(2,1)S(1)}, u32[]{:S(2)}, u32[]{:S(2)}) async-start(bf16[32,2,2,2]{1,3,2,0:T(2,128)(2,1)} %copy.68), calls=%async_computation.2 | async-start | bytes 65536 | tf_op jit(solution)/shard_map/all_to_all | solution.py:76
  36.3 5.3 %gather_fusion = bf16[64,2,256,128]{3,2,1,0:T(8,128)(2,1)} fusion(bf16[3,2,256,128]{3,2,1,0:T(8,128)(2,1)S(1)} %copy-done, s32[1024]{0:T(1024)S(1)} %pad_clamp_fusion.1), kind=kCustom, calls=%fused_computation | custom fusion | bytes 16777472 | tf_op jit(solution)/shard_map/jit(_take)/gather | solution.py:70
  41.5 7.6 %broadcast_select_fusion = bf16[32,2,2,256,128]{4,3,2,1,0:T(8,128)(2,1)} fusion(bf16[32,2,2,256,128]{4,3,2,1,0:T(8,128)(2,1)} %bitcast.82, pred[32,2]{1,0:T(8,128)(4,1)S(1)} %copy.64), kind=kLoop, calls=%fused_computation.17 | loop fusion | flops 4194304 | bytes 16777280 | tf_op jit(solution)/shard_map/jit(_take)/select_n | solution.py:70
  49.1 10.6 %all-to-all-start.1 = ((bf16[32,2,2,256,128]{4,3,2,1,0:T(8,128)(2,1)}), bf16[32,2,2,256,128]{4,3,2,1,0:T(8,128)(2,1)}, u32[]{:S(2)}, u32[]{:S(2)}) async-start(bf16[32,2,2,256,128]{4,3,2,1,0:T(8,128)(2,1)} %broadcast_select_fusion), calls=%async_computation.1 | async-start | bytes 16777216 | tf_op jit(solution)/shard_map/all_to_all | solution.py:75
  59.7 1.9 copy.88
  61.6 2.9 copy.71
  69.4 0.7 multiply_cosine_fusion.1
  72.1 4.2 %multiply_reduce_fusion = f32[768]{0:T(1024)S(1)} fusion(bf16[1,768,4096]{2,1,0:T(8,128)(2,1)} %all-gather.2.cloned.1.call-done), kind=kLoop, calls=%fused_computation.15 | loop fusion | flops 9436416 | bytes 6294528 | tf_op jit(solution)/shard_map/reduce_sum | solution.py:94
  76.7 3.7 %fusion.44 = (bf16[768,2,128]{0,2,1:T(8,128)(2,1)S(1)}, f32[768,2,128]{0,2,1:T(8,128)S(1)}) fusion(bf16[2,128,4096]{2,1,0:T(8,128)(2,1)} %bitcast.87, bf16[1,768,4096]{2,1,0:T(8,128)(2,1)S(1)} %copy-done.2, f32[4096]{0:T(1024)S(1)} %convert_element_type.81, f32[768]{0:T(1024)S(1)} %add_rsqrt_fusion), kind=kOutput, calls=%fused_computation.112 | convolution fusion | flops 1623392256 | bytes 9587712 | tf_op jit(solution)/shard_map/dot_general | solution.py:100
  80.4 0.7 copy.75
  81.3 4.5 %convert_bitcast_fusion = f32[768,4096]{1,0:T(8,128)S(1)} fusion(bf16[1,768,4096]{2,1,0:T(8,128)(2,1)} %all-gather.2.cloned.1.call-done), kind=kLoop, calls=%fused_computation.12 | loop fusion | flops 3145728 | bytes 18874368 | tf_op jit(solution)/shard_map/convert_element_type | solution.py:93
  85.8 3.5 %fusion.13 = f32[256,512]{1,0:T(8,128)S(1)} fusion(bf16[4096,512]{1,0:T(8,128)(2,1)} %param.20, f32[768,4096]{1,0:T(8,128)S(1)} %convert_bitcast_fusion, f32[4096]{0:T(1024)S(1)} %convert_element_type.81, f32[256]{0:T(256)S(1)} %slice.85), kind=kOutput, calls=%fused_computation.35 | convolution fusion | flops 1076887552 | bytes 8930304 | tf_op jit(solution)/shard_map/dot_general | solution.py:99
  89.5 0.8 subtract_convert_fusion.1
  90.5 0.7 copy.73
  92.1 153.8 %all-to-all-done.1 = bf16[32,2,2,256,128]{4,3,2,1,0:T(8,128)(2,1)} async-done(((bf16[32,2,2,256,128]{4,3,2,1,0:T(8,128)(2,1)}), bf16[32,2,2,256,128]{4,3,2,1,0:T(8,128)(2,1)}, u32[]{:S(2)}, u32[]{:S(2)}) %all-to-all-start.1) | async-done | bytes 8388640 | tf_op jit(solution)/shard_map/all_to_all | solution.py:75
  245.8 4.4 %gather_fusion.1 = bf16[20,2,256,128]{3,2,1,0:T(8,128)(2,1)S(1)} fusion(bf16[64,2,256,128]{3,2,1,0:T(8,128)(2,1)} %bitcast.11, s32[1024]{0:T(1024)S(1)} %pad_clamp_fusion), kind=kCustom, calls=%fused_computation.1 | custom fusion | bytes 5242960 | tf_op jit(solution)/shard_map/jit(_take)/gather | solution.py:78
  250.3 2.7 convert_multiply_fusion.1
  253.7 1.0 multiply_subtract_fusion
  254.7 0.7 pad_maximum_fusion
  255.5 2.9 fusion.12
  258.4 2.5 scatter_fusion.1
  261.0 2.5 scatter_fusion
  263.5 5.6 %fusion = (f32[1024]{0:T(1024)S(1)}, f32[1024,5376]{1,0:T(8,128)S(1)}) fusion(s32[5376]{0:T(1024)S(1)} %copy-done.3, s32[1024]{0:T(1024)S(1)} %copy-done.12, pred[5376]{0:T(1024)(128)(4,1)S(1)} %copy-done.8, pred[5376]{0:T(1024)(128)(4,1)S(1)} %copy-done.9, bf16[1024,128]{1,0:T(8,128)(2,1)S(1)} %bitcast.88, bf16[256,128]{1,0:T(8,128)(2,1)S(1)} %copy-done.6, ...), kind=kOutput, calls=%fused_computation.10 | convolution fusion | flops 1439562752 | bytes 23698944 | tf_op jit(solution)/shard_map/dot_general | solution.py:119
  269.2 10.6 %fusion.42 = f32[1024]{0:T(1024)S(1)} fusion(f32[1024]{0:T(1024)S(1)} %get-tuple-element.23, f32[1024,5376]{1,0:T(8,128)S(1)} %get-tuple-element.24, s32[1024]{0:T(1024)S(1)} %copy-done.12, s32[5376]{0:T(1024)S(1)} %copy-done.3, pred[5376]{0:T(1024)(128)(4,1)S(1)} %copy-done.8, pred[5376]{0:T(1024)(128)(4,1)S(1)} %copy-done.9), kind=kLoop, calls=%fused_computation.110 | loop fusion | flops 38534144 | bytes 22064640 | tf_op jit(solution)/shard_map/reduce_sum | solution.py:132
  279.9 8.4 %fusion.27 = bf16[1024,128]{1,0:T(8,128)(2,1)S(1)} fusion(bf16[256,128]{1,0:T(8,128)(2,1)S(1)} %copy-done.5, bf16[5120,128]{1,0:T(8,128)(2,1)S(1)} %scatter_fusion.1, f32[1024]{0:T(1024)S(1)} %fusion.42, pred[1024]{0:T(1024)(128)(4,1)S(1)} %copy-done.17, f32[1024,5376]{1,0:T(8,128)S(1)} %get-tuple-element.24, f32[1024]{0:T(1024)S(1)} %get-tuple-element.23, ...), kind=kOutput, calls=%fused_computation.47 | convolution fusion | flops 1456340992 | bytes 23704064 | tf_op jit(solution)/shard_map/dot_general | solution.py:133
  288.6 0.8 convert_element_type.96
  289.4 1.7 maximum_bitcast_fusion
  (94 shorter events, 12.5 us)
Async XLA Ops:
  7.2 29.1 %copy-start = (bf16[3,2,256,128]{3,2,1,0:T(8,128)(2,1)S(1)}, bf16[3,2,256,128]{3,2,1,0:T(8,128)(2,1)}, u32[]{:S(2)}) copy-start(bf16[3,2,256,128]{3,2,1,0:T(8,128)(2,1)} %param.11) | copy-start | bytes 1179652
  8.3 62.9 %copy-start.16 = (pred[20]{0:T(512)(128)(4,1)}, pred[20]{0:T(512)(128)(4,1)S(1)}, u32[]{:S(2)}) copy-start(pred[20]{0:T(512)(128)(4,1)S(1)} %get-tuple-element.2) | copy-start | bytes 64
  9.1 17.1 %all-to-all-start = ((s32[32,1,2]{2,1,0:T(1,128)}), s32[32,1,2]{2,1,0:T(1,128)S(1)}, u32[]{:S(2)}, u32[]{:S(2)}) async-start(s32[32,1,2]{2,1,0:T(1,128)} %bitcast.7), calls=%async_computation | async-start | bytes 32768 | tf_op jit(solution)/shard_map/all_to_all | solution.py:68
  19.4 52.7 %all-gather.2.cloned.1.call-start = ((), (), s32[]{:S(2)}) async-start(), calls=%async_computation.3 | async-start | bytes 7077888 | tf_op jit(solution)/shard_map/all_gather | solution.py:92
  29.5 19.6 %all-to-all-start.2 = ((bf16[32,2,2,2]{1,3,2,0:T(2,128)(2,1)}), bf16[32,2,2,2]{1,3,2,0:T(2,128)(2,1)S(1)}, u32[]{:S(2)}, u32[]{:S(2)}) async-start(bf16[32,2,2,2]{1,3,2,0:T(2,128)(2,1)} %copy.68), calls=%async_computation.2 | async-start | bytes 65536 | tf_op jit(solution)/shard_map/all_to_all | solution.py:76
  49.1 196.7 %all-to-all-start.1 = ((bf16[32,2,2,256,128]{4,3,2,1,0:T(8,128)(2,1)}), bf16[32,2,2,256,128]{4,3,2,1,0:T(8,128)(2,1)}, u32[]{:S(2)}, u32[]{:S(2)}) async-start(bf16[32,2,2,256,128]{4,3,2,1,0:T(8,128)(2,1)} %broadcast_select_fusion), calls=%async_computation.1 | async-start | bytes 16777216 | tf_op jit(solution)/shard_map/all_to_all | solution.py:75
  59.7 4.8 %copy-start.14 = (bf16[4096]{0:T(1024)(128)(2,1)S(1)}, bf16[4096]{0:T(1024)(128)(2,1)}, u32[]{:S(2)}) copy-start(bf16[4096]{0:T(1024)(128)(2,1)} %param.19) | copy-start | bytes 24580
  59.7 7.3 %copy-start.15 = (s32[1,4,128]{2,1,0:T(4,128)S(1)}, s32[1,4,128]{2,1,0:T(4,128)}, u32[]{:S(2)}) copy-start(s32[1,4,128]{2,1,0:T(4,128)} %param.16) | copy-start | bytes 6148
  72.1 4.6 %copy-start.2 = (bf16[1,768,4096]{2,1,0:T(8,128)(2,1)S(1)}, bf16[1,768,4096]{2,1,0:T(8,128)(2,1)}, u32[]{:S(2)}) copy-start(bf16[1,768,4096]{2,1,0:T(8,128)(2,1)} %all-gather.2.cloned.1.call-done) | copy-start | bytes 18874372
  253.0 0.7 copy-start.7
  253.7 1.7 copy-start.10
  254.7 3.7 %copy-start.11 = (s32[512,1]{0,1:T(1,128)S(1)}, s32[512,1]{0,1:T(1,128)}, u32[]{:S(2)}) copy-start(s32[512,1]{0,1:T(1,128)} %compare_select_fusion.1) | copy-start | bytes 6148
  255.5 8.0 %copy-start.3 = (s32[5376]{0:T(1024)S(1)}, s32[5376]{0:T(1024)}, u32[]{:S(2)}) copy-start(s32[5376]{0:T(1024)} %iota_add_fusion) | copy-start | bytes 64516
  255.5 8.0 %copy-start.6 = (bf16[256,128]{1,0:T(8,128)(2,1)S(1)}, bf16[256,128]{1,0:T(8,128)(2,1)}, u32[]{:S(2)}) copy-start(bf16[256,128]{1,0:T(8,128)(2,1)} %copy.73) | copy-start | bytes 196612
  255.5 8.0 %copy-start.8 = (pred[5376]{0:T(1024)(128)(4,1)S(1)}, pred[5376]{0:T(1024)(128)(4,1)}, u32[]{:S(2)}) copy-start(pred[5376]{0:T(1024)(128)(4,1)} %get-tuple-element.25) | copy-start | bytes 16132
  255.5 8.0 %copy-start.9 = (pred[5376]{0:T(1024)(128)(4,1)S(1)}, pred[5376]{0:T(1024)(128)(4,1)}, u32[]{:S(2)}) copy-start(pred[5376]{0:T(1024)(128)(4,1)} %get-tuple-element.26) | copy-start | bytes 16132
  255.5 8.0 %copy-start.12 = (s32[1024]{0:T(1024)S(1)}, s32[1024]{0:T(1024)}, u32[]{:S(2)}) copy-start(s32[1024]{0:T(1024)} %add_select_fusion) | copy-start | bytes 12292
  269.2 10.7 %copy-start.4 = (s32[5376]{0:T(1024)S(1)}, s32[5376]{0:T(1024)}, u32[]{:S(2)}) copy-start(s32[5376]{0:T(1024)} %iota_add_fusion) | copy-start | bytes 64516
  269.2 10.7 %copy-start.5 = (bf16[256,128]{1,0:T(8,128)(2,1)S(1)}, bf16[256,128]{1,0:T(8,128)(2,1)}, u32[]{:S(2)}) copy-start(bf16[256,128]{1,0:T(8,128)(2,1)} %copy.75) | copy-start | bytes 196612
  269.2 10.7 %copy-start.13 = (s32[1024]{0:T(1024)S(1)}, s32[1024]{0:T(1024)}, u32[]{:S(2)}) copy-start(s32[1024]{0:T(1024)} %add_select_fusion) | copy-start | bytes 12292
  269.2 10.7 %copy-start.17 = (pred[1024]{0:T(1024)(128)(4,1)S(1)}, pred[1024]{0:T(1024)(128)(4,1)}, u32[]{:S(2)}) copy-start(pred[1024]{0:T(1024)(128)(4,1)} %broadcast_compare_fusion) | copy-start | bytes 3076
  279.9 11.2 %copy-start.1 = (bf16[3,2,256,128]{3,2,1,0:T(8,128)(2,1)S(1)}, bf16[3,2,256,128]{3,2,1,0:T(8,128)(2,1)}, u32[]{:S(2)}) copy-start(bf16[3,2,256,128]{3,2,1,0:T(8,128)(2,1)} %param.11) | copy-start | bytes 1179652
Sparse Core Ops, SparseCore 0:
  22.1 44.8 all-gather.1
where the time goes:
time: 302 us; the launch traced here: 298 us
  waiting for transfers between devices  160 us (53%)
  other arithmetic  43.5 us (14%)
  local copies, waits for them, and re-layouts  30 us (10%)
  starting transfers between devices  27.6 us (9%)
  matrix products  21.2 us (7%)
  between operations  16.1 us (5%)
    all_to_all x1, waiting for transfers between devices, on_device(): lax.all_to_all(send_codes, 'store', split_axis=0, concat_axis=0, tiled=True)  154 us
    reduce_sum x1, other arithmetic, on_device(): jnp.sum(exp_terms, axis=-1, keepdims=True)  10.6 us
    all_to_all x1, starting transfers between devices, on_device(): lax.all_to_all(send_codes, 'store', split_axis=0, concat_axis=0, tiled=True)  10.6 us
    all_to_all x1, starting transfers between devices, on_device(): lax.all_to_all(wanted, 'store', split_axis=0, concat_axis=0, tiled=True)  10.3 us
    dot_general x1, matrix products, on_device(): jnp.dot(weights, all_values, preferred_element_type=jnp.float32)  8.44 us
    select_n x2, other arithmetic, on_device(): jnp.take(kv_store, asked_flat, axis=0)  7.61 us
    all_to_all x1, starting transfers between devices, on_device(): lax.all_to_all(send_scales, 'store', split_axis=0, concat_axis=0, tiled=T...  6.69 us
  transfers between devices with their start and end apart: 4, of which 2 were waited for; matrix products, arithmetic and copies ran while one was open for 16% of the time, Pallas kernels for 0%

commit v1 on v0

v1 whole, which is shorter than its diff:
```python
import functools
import jax
import jax.numpy as jnp
from jax import lax
from jax.experimental import pallas as pl
from jax.experimental.pallas import tpu as pltpu
from jax.sharding import PartitionSpec as P

SPAN = 256
SB = 128
MAXDOC = 20
NX, NZ = 4, 8
HW = 128
LOG2E = 1.4426950408889634
STORED = 3
BLOCK = STORED * SPAN + 16
CUT = BLOCK + 2 * SPAN


rope_base = 500000.0
norm_eps = 1e-05


def rope_angles(positions, head_width):
    halfway = head_width // 2
    exponent = jnp.arange(halfway, dtype=jnp.float32) * (2.0 / head_width)
    inverse_freq = jnp.power(jnp.float32(rope_base), -exponent)
    angles = positions.astype(jnp.float32)[:, None] * inverse_freq[None, :]
    return (jnp.cos(angles), jnp.sin(angles))


def rotate_half(values, cosine, sine_part):
    halfway = values.shape[-1] // 2
    low_half = values[..., :halfway]
    high_half = values[..., halfway:]
    return jnp.concatenate(
        [low_half * cosine - high_half * sine_part, high_half * cosine + low_half * sine_part],
        axis=-1,
    )


def shift(a, dx, dz):
    pairs = [
        (x * NZ + z, ((x + dx) % NX) * NZ + (z + dz) % NZ) for x in range(NX) for z in range(NZ)
    ]
    return lax.ppermute(a, "store", pairs)


HBM = pl.BlockSpec(memory_space=pl.ANY)
VMEM = pl.BlockSpec(memory_space=pltpu.VMEM)
SMEM = pl.BlockSpec(memory_space=pltpu.SMEM)


def pack_kernel(plan, *refs):
    sources, out, sems = refs[:-2], refs[-2], refs[-1]
    copies, at = [], 0
    for n, (source, start, rows) in enumerate(plan):
        copies.append(
            pltpu.make_async_copy(
                sources[source].at[pl.ds(start, rows)], out.at[pl.ds(at, rows)], sems.at[n]
            )
        )
        at += rows
    for copy in copies:
        copy.start()
    for copy in copies:
        copy.wait()


def pack(sources, plan):
    rows = sum(p[2] for p in plan)
    return pl.pallas_call(
        functools.partial(pack_kernel, plan),
        out_shape=jax.ShapeDtypeStruct((rows, HW), jnp.bfloat16),
        in_specs=[HBM] * len(sources),
        out_specs=HBM,
        scratch_shapes=[pltpu.SemaphoreType.DMA((len(plan),))],
        cost_estimate=pl.CostEstimate(
            flops=0, bytes_accessed=4 * rows * HW, transcendentals=0
        ),
    )(*sources)


def project_kernel(hid_ref, gain_ref, wq_ref, wkv_ref, cos_ref, sin_ref, new_ref, qt_ref, nb_ref):
    features = hid_ref.shape[1]
    piece = 512
    total = jnp.zeros((SPAN, 1), jnp.float32)
    for c in range(0, features, piece):
        x = hid_ref[:, c : c + piece].astype(jnp.float32)
        total = total + jnp.sum(x * x, axis=1, keepdims=True)
    inverse = lax.rsqrt(total * (1.0 / features) + norm_eps)
    for c in range(0, features, piece):
        x = hid_ref[:, c : c + piece].astype(jnp.float32)
        gain = gain_ref[:, c : c + piece].astype(jnp.float32)
        nb_ref[:, c : c + piece] = (x * inverse * gain).astype(jnp.bfloat16)
    kv = jnp.dot(nb_ref[...], wkv_ref[...], preferred_element_type=jnp.float32)
    cosine, sine = cos_ref[...], sin_ref[...]
    k = kv[:, :HW]
    new_ref[:, :HW] = (k * cosine + pltpu.roll(k, HW // 2, 1) * sine).astype(jnp.bfloat16)
    new_ref[:, HW : 2 * HW] = kv[:, HW:].astype(jnp.bfloat16)
    new_ref[:, 2 * HW :] = jnp.ones((SPAN, HW), jnp.bfloat16)

    @pl.when(pl.program_id(0) == pl.num_programs(0) - 1)
    def _():
        q = jnp.dot(nb_ref[...], wq_ref[...], preferred_element_type=jnp.float32)
        for h in range(q.shape[1] // HW):
            one = q[:, h * HW : (h + 1) * HW]
            one = one * cosine + pltpu.roll(one, HW // 2, 1) * sine
            qt_ref[:, h * SPAN : (h + 1) * SPAN] = one.T.astype(jnp.bfloat16)


def project(hid, gain, wq, wkv, cosine, sine):
    rows, features = hid.shape
    lanes = wq.shape[1] // HW * SPAN
    return pl.pallas_call(
        project_kernel,
        grid=(rows // SPAN,),
        out_shape=(
            jax.ShapeDtypeStruct((rows, 3 * HW), jnp.bfloat16),
            jax.ShapeDtypeStruct((HW, lanes), jnp.bfloat16),
        ),
        in_specs=[
            pl.BlockSpec((SPAN, features), lambda i: (i, 0)),
            pl.BlockSpec((1, features), lambda i: (0, 0)),
            pl.BlockSpec(wq.shape, lambda i: (0, 0)),
            pl.BlockSpec(wkv.shape, lambda i: (0, 0)),
            pl.BlockSpec((SPAN, HW), lambda i: (i, 0)),
            pl.BlockSpec((SPAN, HW), lambda i: (i, 0)),
        ],
        out_specs=(
            pl.BlockSpec((SPAN, 3 * HW), lambda i: (i, 0)),
            pl.BlockSpec((HW, lanes), lambda i: (0, 0)),
        ),
        scratch_shapes=[pltpu.VMEM((SPAN, features), jnp.bfloat16)],
        compiler_params=pltpu.CompilerParams(vmem_limit_bytes=40 * 1024 * 1024),
        cost_estimate=pl.CostEstimate(
            flops=2 * features * HW * (2 * rows + 4 * SPAN),
            bytes_accessed=2 * features * (rows + 6 * HW),
            transcendentals=0,
        ),
    )(hid, gain, wq, wkv, cosine, sine)


DOC, SLOT, KB, KROW, KSC, VB, VROW, VSC = range(8)


def attend_kernel(first, nk, nv, table, count_ref, pos_ref, shift_ref, new_ref, qt_ref, *refs):
    kbufs, vbufs, refs = refs[:nk], refs[nk : nk + nv], refs[nk + nv :]
    if first:
        ctx_ref, m_ref, l_ref, acc_ref = refs[:4]
        refs = refs[4:]
    else:
        m_in, l_in, acc_in, _, out_ref, ctx_ref, m_ref, l_ref, acc_ref = refs[:9]
        refs = refs[9:]
    kdoc, vdoc, kscale, vscale, zero, ksem, vsem, kssem, vssem, kout, vout = refs
    count = count_ref[2] if first else count_ref[3]
    lanes = qt_ref.shape[1]
    nrec = pos_ref.shape[1]
    factor = HW**-0.5 * LOG2E
    heads = [slice(h, h + SPAN) for h in range(0, lanes, SPAN)]

    def pick(n, low, high, act):
        if high - low == 1:
            act(low)
            return
        mid = (low + high) // 2

        @pl.when(n < mid)
        def _():
            pick(n, low, mid, act)

        @pl.when(n >= mid)
        def _():
            pick(n, mid, high, act)

    def fetch(r, _):
        def keys(b):
            row = pl.multiple_of(table[KROW, r], 16)
            pltpu.make_async_copy(kbufs[b].at[pl.ds(row, SPAN)], kdoc.at[r], ksem.at[r]).start()
            row = pl.multiple_of(table[KSC, r], 16)
            pltpu.make_async_copy(kbufs[b].at[pl.ds(row, 16)], kscale.at[r], kssem.at[r]).start()

        def values(b):
            row = pl.multiple_of(table[VROW, r], 16)
            pltpu.make_async_copy(vbufs[b].at[pl.ds(row, SPAN)], vdoc.at[r], vsem.at[r]).start()
            row = pl.multiple_of(table[VSC, r], 16)
            pltpu.make_async_copy(vbufs[b].at[pl.ds(row, 16)], vscale.at[r], vssem.at[r]).start()

        pick(table[KB, r], 0, nk, keys)
        pick(table[VB, r], 0, nv, values)
        return 0

    lax.fori_loop(0, count, fetch, 0)

    def place(j):
        return pl.ds(pl.multiple_of(j * SPAN, SPAN), SPAN)

    if first:
        docs = count_ref[0]
        zero[...] = jnp.zeros(zero.shape, zero.dtype)

        def blank(j, _):
            pltpu.make_async_copy(zero, ctx_ref.at[0, place(j)], kout.at[j]).start()
            pltpu.make_async_copy(zero, ctx_ref.at[1, place(j)], vout.at[j]).start()
            return 0

        lax.fori_loop(docs, MAXDOC, blank, 0)

        own_keys = new_ref[nrec:, :HW]
        own_values = new_ref[nrec:, HW : 2 * HW]
        for h in heads:
            scores = jnp.dot(own_keys, qt_ref[:, h], preferred_element_type=jnp.float32)
            key_index = lax.broadcasted_iota(jnp.int32, scores.shape, 0)
            query_index = lax.broadcasted_iota(jnp.int32, scores.shape, 1)
            scores = jnp.where(key_index <= query_index, scores, -jnp.inf)
            top = jnp.max(scores, axis=0, keepdims=True)
            terms = jnp.exp2((scores - top) * factor)
            m_ref[:, h] = top
            l_ref[:, h] = jnp.sum(terms, axis=0, keepdims=True)
            acc_ref[:, h] = lax.dot_general(
                own_values,
                terms.astype(jnp.bfloat16),
                (((0,), (0,)), ((), ())),
                preferred_element_type=jnp.float32,
            )
    else:
        m_ref[...] = m_in[...]
        l_ref[...] = l_in[...]
        acc_ref[...] = acc_in[...]

    upper = lax.broadcasted_iota(jnp.int32, (SPAN, HW), 0) >= SB
    row_index = lax.broadcasted_iota(jnp.int32, (SPAN, nrec), 0)
    scale_index = lax.broadcasted_iota(jnp.int32, (16, HW), 0)

    def dequant(codes, scales, slot):
        s = scales.astype(jnp.float32)
        low = jnp.sum(jnp.where(scale_index == 2 * slot, s, 0.0), axis=0, keepdims=True)
        high = jnp.sum(jnp.where(scale_index == 2 * slot + 1, s, 0.0), axis=0, keepdims=True)
        return codes.astype(jnp.float32) * jnp.where(upper, high, low)

    def step(r, _):
        j, slot = table[DOC, r], table[SLOT, r]
        hit = jnp.where(row_index == pos_ref[...] - j * SPAN, 1.0, 0.0).astype(jnp.bfloat16)
        fresh = jnp.dot(hit, new_ref[:nrec], preferred_element_type=jnp.float32)
        replaced = fresh[:, 2 * HW :] > 0.5
        pltpu.make_async_copy(kbufs[0].at[pl.ds(0, SPAN)], kdoc.at[r], ksem.at[r]).wait()
        pltpu.make_async_copy(kbufs[0].at[pl.ds(0, 16)], kscale.at[r], kssem.at[r]).wait()
        pltpu.make_async_copy(vbufs[0].at[pl.ds(0, SPAN)], vdoc.at[r], vsem.at[r]).wait()
        pltpu.make_async_copy(vbufs[0].at[pl.ds(0, 16)], vscale.at[r], vssem.at[r]).wait()
        k = dequant(kdoc[r], kscale[r], slot)
        turn = shift_ref[j]
        k = k * turn[0:1] + pltpu.roll(k, HW // 2, 1) * turn[1:2]
        k = jnp.where(replaced, fresh[:, :HW], k).astype(jnp.bfloat16)
        v = dequant(vdoc[r], vscale[r], slot)
        v = jnp.where(replaced, fresh[:, HW : 2 * HW], v).astype(jnp.bfloat16)
        kdoc[r] = k
        vdoc[r] = v
        pltpu.make_async_copy(kdoc.at[r], ctx_ref.at[0, place(j)], kout.at[r]).start()
        pltpu.make_async_copy(vdoc.at[r], ctx_ref.at[1, place(j)], vout.at[r]).start()
        for h in heads:
            scores = jnp.dot(k, qt_ref[:, h], preferred_element_type=jnp.float32)
            before = m_ref[:, h]
            top = jnp.maximum(before, jnp.max(scores, axis=0, keepdims=True))
            terms = jnp.exp2((scores - top) * factor)
            fade = jnp.exp2((before - top) * factor)
            m_ref[:, h] = top
            l_ref[:, h] = l_ref[:, h] * fade + jnp.sum(terms, axis=0, keepdims=True)
            acc_ref[:, h] = acc_ref[:, h] * fade + lax.dot_general(
                v,
                terms.astype(jnp.bfloat16),
                (((0,), (0,)), ((), ())),
                preferred_element_type=jnp.float32,
            )
        return 0

    lax.fori_loop(0, count, step, 0)

    if not first:
        live = lax.broadcasted_iota(jnp.int32, (1, SPAN), 1) < count_ref[1]
        for n, h in enumerate(heads):
            mixed = jnp.where(live, acc_ref[:, h] / l_ref[:, h], 0.0)
            out_ref[:, n * HW : (n + 1) * HW] = mixed.T.astype(jnp.bfloat16)

    def finish(r, _):
        pltpu.make_async_copy(kdoc.at[0], ctx_ref.at[0, pl.ds(0, SPAN)], kout.at[r]).wait()
        pltpu.make_async_copy(vdoc.at[0], ctx_ref.at[1, pl.ds(0, SPAN)], vout.at[r]).wait()
        return 0

    lax.fori_loop(0, count, finish, 0)
    if first:
        lax.fori_loop(count_ref[0], MAXDOC, finish, 0)


def attend(first, kbufs, vbufs, table, counts, pos, turns, new, qt, state):
    lanes = qt.shape[1]
    context = jax.ShapeDtypeStruct((2, MAXDOC * SPAN, HW), jnp.bfloat16)
    running = [(1, lanes), (1, lanes), (HW, lanes)]
    if first:
        out_shape = (context, *[jax.ShapeDtypeStruct(s, jnp.float32) for s in running])
        out_specs = (HBM, VMEM, VMEM, VMEM)
    else:
        out_shape = (jax.ShapeDtypeStruct((SPAN, lanes // SPAN * HW), jnp.bfloat16), context)
        out_specs = (VMEM, HBM)
    fixed = 6 + len(kbufs) + len(vbufs)
    documents = MAXDOC // 2
    return pl.pallas_call(
        functools.partial(attend_kernel, first, len(kbufs), len(vbufs)),
        out_shape=out_shape,
        in_specs=[SMEM] * 2
        + [VMEM] * 4
        + [HBM] * (len(kbufs) + len(vbufs))
        + ([] if first else [VMEM] * 3 + [HBM]),
        out_specs=out_specs,
        scratch_shapes=([] if first else [pltpu.VMEM(s, jnp.float32) for s in running])
        + [pltpu.VMEM((MAXDOC, SPAN, HW), jnp.bfloat16)] * 2
        + [pltpu.VMEM((MAXDOC, 16, HW), jnp.bfloat16)] * 2
        + [pltpu.VMEM((SPAN, HW), jnp.bfloat16)]
        + [pltpu.SemaphoreType.DMA((MAXDOC,))] * 6,
        input_output_aliases={} if first else {fixed + 3: 1},
        compiler_params=pltpu.CompilerParams(vmem_limit_bytes=32 * 1024 * 1024),
        cost_estimate=pl.CostEstimate(
            flops=4 * lanes * HW * documents * SPAN,
            bytes_accessed=8 * documents * SPAN * HW,
            transcendentals=lanes * documents * SPAN,
        ),
    )(table, counts, pos, turns, new, qt, *kbufs, *vbufs, *state)


def on_device(
    kv_store,
    kv_scale,
    span_home,
    doc_ids,
    doc_count,
    recompute_rows,
    query_len,
    hidden,
    norm_gain,
    w_q,
    w_kv,
):
    tie = lax.optimization_barrier
    me = lax.axis_index("store")
    my_x, my_z = me // NZ, me % NZ

    scale_rows = jnp.transpose(kv_scale[:, :, 0, :], (1, 0, 2)).reshape(2, -1, 1)
    scale_rows = jnp.pad(scale_rows, ((0, 0), (0, 16 - 2 * STORED), (0, 0)))
    own = jnp.concatenate(
        [
            jnp.transpose(kv_store, (1, 0, 2, 3)).reshape(2, STORED * SPAN, HW),
            jnp.broadcast_to(scale_rows, (2, 16, HW)),
        ],
        axis=1,
    ).reshape(2 * BLOCK, HW)

    def keys_of(a):
        return a[:BLOCK]

    def values_of(a):
        return a[BLOCK:]

    def last_hop(a, b, dx, dz):
        left = pack([a], [(0, 0, CUT), (0, 2 * BLOCK - 16, 16)])
        right = pack([b], [(0, CUT, 2 * BLOCK + BLOCK - CUT)])
        return shift(left, dx, dz), shift(right, -dx, -dz)

    z1m, z1p = shift(own, 0, 1), shift(own, 0, -1)
    x1m, x1p = shift(own, 1, 0), shift(own, -1, 0)
    z1m, z1p, x1m, x1p = tie((z1m, z1p, x1m, x1p))
    z2m, z2p = shift(z1m, 0, 1), shift(z1p, 0, -1)
    x2k, x2v = shift(keys_of(x1m), 1, 0), shift(values_of(x1p), -1, 0)
    w0 = pack([x1m, x1p, x2v], [(0, BLOCK, BLOCK), (1, BLOCK, BLOCK), (2, 0, BLOCK)])
    w1m, w1p = shift(w0, 0, 1), shift(w0, 0, -1)
    z3m, z3p = shift(z2m, 0, 1), shift(z2p, 0, -1)
    d1 = pack([z1m, z1p, z2m, z2p], [(n, 0, BLOCK) for n in range(4)])
    d1m, d1p = shift(d1, 1, 0), shift(d1, -1, 0)
    w2m, w2p = shift(w1m, 0, 1), shift(w1p, 0, -1)
    z4k, z4v = shift(keys_of(z3m), 0, 1), shift(values_of(z3p), 0, -1)
    d1a, d1b = shift(d1m[: 2 * BLOCK], 1, 0), shift(d1p[2 * BLOCK :], -1, 0)
    d2 = pack([z3m, z3p, z4k], [(n, 0, BLOCK) for n in range(3)])
    d2m, d2p = shift(d2, 1, 0), shift(d2, -1, 0)

    doc_list = doc_ids[0]
    doc_total = doc_count[0]
    span_index = jnp.arange(span_home.shape[0], dtype=jnp.int32)
    position = jnp.sum(
        jnp.where(doc_list[:, None] == span_index[None, :], span_home[None, :], 0), axis=1
    )
    owner, slot = position // STORED, position % STORED
    dx = (owner // NZ - my_x) % NX
    dz = (owner % NZ - my_z) % NZ
    one_x = jnp.where(dx == 3, 0, dx)
    one_z = jnp.where(dz == 4, 6, jnp.where(dz > 4, 14 - 2 * dz, 2 * dz - 1))

    def split(block):
        second = (block == 2) | ((block == 1) & (slot == 2))
        row = block * BLOCK + slot * SPAN
        scale = jnp.where(block == 1, CUT, block * BLOCK + STORED * SPAN)
        scale_second = block * BLOCK + STORED * SPAN - CUT
        return (
            second.astype(jnp.int32),
            jnp.where(second, row - CUT, row),
            jnp.where(second, scale_second, scale),
        )

    live = jnp.arange(MAXDOC) < doc_total
    axis_buf = jnp.where(dx == 0, jnp.where(dz == 0, 0, 3 + one_z), jnp.where(dx == 2, 9, 1 + one_x))
    straight = (dx == 0) | (dz == 0)
    late = ((dx == 0) & (dz == 4)) | ((dx != 0) & (one_z >= 4))
    key_block = jnp.where(one_z >= 4, one_z - 4, one_z)
    piece, cut_row, cut_scale = split(key_block)
    kb = jnp.where(straight, axis_buf, 10 + one_x)
    row = slot * SPAN
    krow = jnp.where(straight, row, key_block * BLOCK + row)
    far = (~straight) & (dx == 2) & (key_block >= 2)
    kb = jnp.where(far, 13, kb)
    krow = jnp.where(far, krow - 2 * BLOCK, krow)
    ksc = krow - row + STORED * SPAN
    cut = late & (dx == 2)
    kb = jnp.where(late, jnp.where(dx == 0, 0, jnp.where(cut, 3 + piece, 1 + one_x)), kb)
    krow = jnp.where(late, jnp.where(cut, cut_row, jnp.where(dx == 0, row, key_block * BLOCK + row)), krow)
    ksc = jnp.where(late, jnp.where(cut, cut_scale, krow - row + STORED * SPAN), ksc)
    piece, cut_row, cut_scale = split(one_x)
    vb = jnp.where(straight, axis_buf, 10 + one_z)
    vrow = jnp.where(straight, jnp.where((dz == 0) & (dx == 2), row, BLOCK + row), one_x * BLOCK + row)
    vsc = vrow - row + STORED * SPAN
    cut = late & (dx != 0) & (dz == 4)
    vb = jnp.where(late, jnp.where(dx == 0, 0, jnp.where(cut, 3 + piece, one_z - 3)), vb)
    vrow = jnp.where(late, jnp.where(cut, cut_row, jnp.where(dx == 0, row, one_x * BLOCK + row)), vrow)
    vsc = jnp.where(late, jnp.where(cut, cut_scale, vrow - row + STORED * SPAN), vsc)
    facts = jnp.stack([jnp.arange(MAXDOC), slot, kb, krow, ksc, vb, vrow, vsc]).astype(jnp.int32)

    def chosen(flag):
        rank = jnp.sum(jnp.where(jnp.tri(MAXDOC, k=-1, dtype=bool) & flag[None, :], 1, 0), axis=1)
        seat = flag[:, None] & (rank[:, None] == jnp.arange(MAXDOC)[None, :])
        return jnp.sum(jnp.where(seat[None], facts[:, :, None], 0), axis=1)

    early_table, late_table = chosen(live & ~late), chosen(live & late)
    early_count = jnp.sum((live & ~late).astype(jnp.int32))
    counts = jnp.stack([doc_total, query_len[0], early_count, doc_total - early_count]).astype(
        jnp.int32
    )

    shift_cos, shift_sin = rope_angles(jnp.arange(MAXDOC, dtype=jnp.int32) * SPAN, HW)
    turns = jnp.stack(
        [
            jnp.concatenate([shift_cos, shift_cos], axis=1),
            jnp.concatenate([-shift_sin, shift_sin], axis=1),
        ],
        axis=1,
    )

    recompute_total = recompute_rows.shape[1] * recompute_rows.shape[2]
    flat_pos = recompute_rows[0].reshape(recompute_total).astype(jnp.int32)
    query_pos = doc_total * SPAN + jnp.arange(hidden.shape[1] - recompute_total, dtype=jnp.int32)
    row_cos, row_sin = rope_angles(jnp.concatenate([flat_pos, query_pos]), HW)
    layer_input = lax.all_gather(hidden, "tp", axis=2, tiled=True)[0]
    new, qt = project(
        layer_input,
        norm_gain[None],
        w_q,
        w_kv.reshape(w_kv.shape[0], 2 * HW),
        jnp.concatenate([row_cos, row_cos], axis=1),
        jnp.concatenate([-row_sin, row_sin], axis=1),
    )

    w2m, w2p, new, qt = tie((w2m, w2p, new, qt))
    w3m, w3p = shift(w2m, 0, 1), shift(w2p, 0, -1)
    straight_bufs = [own, x1m, x1p, z1m, z1p, z2m, z2p, z3m, z3p]
    common = (counts, flat_pos[None], turns, new, qt)
    context, *state = attend(
        True,
        straight_bufs + [x2k, d1m, d1p, d1a, d1b],
        straight_bufs + [x2v, w1m, w1p, w2m, w2p],
        early_table,
        *common,
        [],
    )
    w3m, w3p, d2m, d2p, state = tie((w3m, w3p, d2m, d2p, state))
    w4a, w4b = last_hop(w3m, w3p, 0, 1)
    d2a, d2b = last_hop(d2m, d2p, 1, 0)
    attention, context = attend(
        False,
        [z4k, d2m, d2p, d2a, d2b],
        [z4v, w3m, w3p, w4a, w4b],
        late_table,
        *common,
        [*state, context],
    )
    return (attention[None], context[None])


def solution(mesh):
    placed = (
        P("store", None, None, "tp"),
        P("store", None, "tp", None),
        P(),
        P("store", None),
        P("store"),
        P("store", None, None),
        P("store"),
        P("store", None, "tp"),
        P(),
        P(None, "tp"),
        P(None, None, "tp"),
    )
    return jax.shard_map(
        on_device,
        mesh=mesh,
        in_specs=placed,
        out_specs=(P("store", None, "tp"), P("store", None, None, "tp")),
        check_vma=False,
    )
```

time: 302 us -> 289 us (0.957)
  the two profiles are of different devices: /device:TPU:96 before, /device:TPU:26 now
where the time goes in v1:
time: 289 us
  Pallas kernels  153 us (53%)
  waiting for transfers between devices  38.8 us (13%)
  starting transfers between devices  38.7 us (13%)
  local copies, waits for them, and re-layouts  30.4 us (11%)
  between operations  16.6 us (6%)
  other arithmetic  11.6 us (4%)
    pallas_call x7, Pallas kernels, pack(): pl.pallas_call(functools.partial(pack_kernel, plan), out_shape=jax.ShapeD...  105 us
    pallas_call x2, Pallas kernels, attend(): pl.pallas_call(functools.partial(attend_kernel, first, len(kbufs), len(vb...  42 us
    ppermute x28, starting transfers between devices, shift(): return lax.ppermute(a, 'store', pairs)  38.7 us
    ppermute x28, waiting for transfers between devices, shift(): return lax.ppermute(a, 'store', pairs)  38.1 us
    unnamed x96, local copies, waits for them, and re-layouts  26.1 us
  transfers between devices with their start and end apart: 29, of which 8 were waited for; matrix products, arithmetic and copies ran while one was open for 6% of the time, Pallas kernels for 43%

profile of v1, /device:TPU:26, one launch (start us, length us, event | category | flops | bytes accessed | tf_op | source)
XLA Modules:
  0.0 289.0 jit_solution(2312493860331347389)
XLA Ops:
  9.9 2.0 collective-permute-start
  11.9 4.0 %collective-permute-start.1 = (bf16[1568,128]{1,0:T(8,128)(2,1)S(1)}, bf16[1568,128]{1,0:T(8,128)(2,1)S(1)}, u32[]{:S(2)}, u32[]{:S(2)}) collective-permute-start(bf16[1568,128]{1,0:T(8,128)(2,1)S(1)} %bitcast.91), channel_id=1, source_target_pairs={{0,56},{8,0},{16,8},{24,16},{32,24},{40,32},{48,40},{56,48},{64,12... | collective-permute-start | bytes 1204232 | tf_op jit(solution)/shard_map/ppermute | solution.py:46
  21.0 2.5 fusion
  23.5 1.6 collective-permute-done.refs_0_.refs_3_.refs_17_
  25.2 1.5 collective-permute-done.2.refs_0_.refs_1_.refs_15_
  28.6 1.7 collective-permute-start.14
  31.2 2.5 collective-permute-done.4.refs_2_.refs_23_
  34.4 19.4 %shard_map.122 = bf16[2352,128]{1,0:T(8,128)(2,1)} custom-call(bf16[1568,128]{1,0:T(8,128)(2,1)} %copy-done.1, bf16[1568,128]{1,0:T(8,128)(2,1)} %copy-done.3, bf16[784,128]{1,0:T(8,128)(2,1)} %copy-done.36), custom_call_target="tpu_custom_call" | custom-call | bytes 1204224 | tf_op jit(solution)/shard_map/pallas_call | solution.py:72
  54.5 3.2 %collective-permute-start.7 = (bf16[2352,128]{1,0:T(8,128)(2,1)}, bf16[2352,128]{1,0:T(8,128)(2,1)}, u32[]{:S(2)}, u32[]{:S(2)}) collective-permute-start(bf16[2352,128]{1,0:T(8,128)(2,1)} %shard_map.122), channel_id=1, source_target_pairs={{0,56},{8,0},{16,8},{24,16},{32,24},{40,32},{48,40},{56,48},{64,12... | collective-permute-start | bytes 1806344 | tf_op jit(solution)/shard_map/ppermute | solution.py:46
  59.2 25.5 %shard_map.125 = bf16[3136,128]{1,0:T(8,128)(2,1)} custom-call(bf16[1568,128]{1,0:T(8,128)(2,1)} %copy-done.10, bf16[1568,128]{1,0:T(8,128)(2,1)} %copy-done.12, bf16[1568,128]{1,0:T(8,128)(2,1)} %copy-done.16, bf16[1568,128]{1,0:T(8,128)(2,1)} %copy-done.14), custom_call_target="tpu_custom_call" | custom-call | bytes 1605632 | tf_op jit(solution)/shard_map/pallas_call | solution.py:72
  87.4 3.1 %collective-permute-start.15 = (bf16[1568,128]{1,0:T(8,128)(2,1)}, bf16[1568,128]{1,0:T(8,128)(2,1)S(1)}, u32[]{:S(2)}, u32[]{:S(2)}) collective-permute-start(bf16[1568,128]{1,0:T(8,128)(2,1)} %copy-done.14), channel_id=1, source_target_pairs={{0,56},{8,0},{16,8},{24,16},{32,24},{40,32},{48,40},{56,48},{64,12... | collective-permute-start | bytes 1204232 | tf_op jit(solution)/shard_map/ppermute | solution.py:46
  91.3 8.8 %collective-permute-done.10.refs_0_.refs_7_.refs_21_ = bf16[1568,128]{1,0:T(8,128)(2,1)S(1)} collective-permute-done((bf16[1568,128]{1,0:T(8,128)(2,1)}, bf16[1568,128]{1,0:T(8,128)(2,1)S(1)}, u32[]{:S(2)}, u32[]{:S(2)}) %collective-permute-start.10) | collective-permute-done | bytes 401440 | tf_op jit(solution)/shard_map/ppermute | solution.py:46
  100.1 2.4 pad_maximum_fusion.1
  102.6 1.9 collective-permute-start.11
  105.4 2.9 %collective-permute-start.21 = (bf16[1568,128]{1,0:T(8,128)(2,1)}, bf16[1568,128]{1,0:T(8,128)(2,1)}, u32[]{:S(2)}, u32[]{:S(2)}) collective-permute-start(bf16[1568,128]{1,0:T(8,128)(2,1)} %slice.25), channel_id=1, source_target_pairs={{0,64},{8,72},{16,80},{24,88},{32,96},{40,104},{48,112},{56,120},{... | collective-permute-start | bytes 1204232 | tf_op jit(solution)/shard_map/ppermute | solution.py:46
  109.5 3.6 %collective-permute-done.11.refs_2_.refs_0_ = bf16[784,128]{1,0:T(8,128)(2,1)S(1)} collective-permute-done((bf16[784,128]{1,0:T(8,128)(2,1)S(1)}, bf16[784,128]{1,0:T(8,128)(2,1)S(1)}, u32[]{:S(2)}, u32[]{:S(2)}) %collective-permute-start.11) | collective-permute-done | bytes 200736 | tf_op jit(solution)/shard_map/ppermute | solution.py:46
  113.1 2.9 %collective-permute-start.18 = (bf16[784,128]{1,0:T(8,128)(2,1)}, bf16[784,128]{1,0:T(8,128)(2,1)}, u32[]{:S(2)}, u32[]{:S(2)}) collective-permute-start(bf16[784,128]{1,0:T(8,128)(2,1)} %slice.20), channel_id=1, source_target_pairs={{0,64},{8,72},{16,80},{24,88},{32,96},{40,104},{48,112},{56,120},{... | collective-permute-start | bytes 602120 | tf_op jit(solution)/shard_map/ppermute | solution.py:46
  116.0 19.4 %shard_map.124 = bf16[2352,128]{1,0:T(8,128)(2,1)} custom-call(bf16[1568,128]{1,0:T(8,128)(2,1)} %copy-done.7, bf16[1568,128]{1,0:T(8,128)(2,1)} %copy-done.5, bf16[784,128]{1,0:T(8,128)(2,1)} %copy-done.38), custom_call_target="tpu_custom_call" | custom-call | bytes 1204224 | tf_op jit(solution)/shard_map/pallas_call | solution.py:72
  135.4 2.8 copy-done
  138.2 2.2 copy-done.9
  142.3 5.6 %shard_map.123 = (bf16[768,384]{1,0:T(8,128)(2,1)S(1)}, bf16[128,1024]{1,0:T(8,128)(2,1)S(1)}) custom-call(bf16[768,4096]{1,0:T(8,128)(2,1)S(1)} %bitcast.89, bf16[1,4096]{1,0:T(2,128)(2,1)S(1)} %broadcast_in_dim.116.gain_ref, bf16[4096,512]{1,0:T(8,128)(2,1)S(1)} %copy-done.9, bf16[4096,256]{1,0:T(8,128)(2,1)S(1)} %bitcast.88, f32[768,128]{1,0:T(8,128)S(1)} %copy-done.31, ...), custom_call_target="tpu_custom_call" | custom-call | flops 2684354560 | bytes 12582912 | tf_op jit(solution)/shard_map/pallas_call | solution.py:115
  151.5 3.2 %collective-permute-start.13 = (bf16[2352,128]{1,0:T(8,128)(2,1)}, bf16[2352,128]{1,0:T(8,128)(2,1)}, u32[]{:S(2)}, u32[]{:S(2)}) collective-permute-start(bf16[2352,128]{1,0:T(8,128)(2,1)} %collective-permute-done.8.refs_27_), channel_id=1, source_target_pairs={{0,56},{8,0},{16,8},{24,16},{32,24},{40,32},{48,40},{56,48},{64,12... | collective-permute-start | bytes 1806344 | tf_op jit(solution)/shard_map/ppermute | solution.py:46
  159.9 10.2 %collective-permute-done.22.refs_13_ = bf16[1568,128]{1,0:T(8,128)(2,1)S(1)} collective-permute-done((bf16[1568,128]{1,0:T(8,128)(2,1)S(1)}, bf16[1568,128]{1,0:T(8,128)(2,1)S(1)}, u32[]{:S(2)}, u32[]{:S(2)}) %collective-permute-start.22) | collective-permute-done | bytes 401440 | tf_op jit(solution)/shard_map/ppermute | solution.py:46
  179.3 25.0 %shard_map.126 = (bf16[2,5120,128]{2,1,0:T(8,128)(2,1)}, f32[1,1024]{1,0:T(1,128)S(1)}, f32[1,1024]{1,0:T(1,128)S(1)}, f32[128,1024]{1,0:T(8,128)S(1)}) custom-call(s32[8,20]{1,0:T(8,128)S(1)} %get-tuple-element.48.table, s32[4]{0:T(128)S(1)} %pad_add_fusion.count_ref, s32[1,512]{1,0:T(1,128)S(1)} %bitcast.97, ...), custom_call_target="tpu_custom_call" | custom-call | flops 1342177280 | bytes 2621440 | tf_op jit(solution)/shard_map/pallas_call | solution.py:306
  206.1 11.3 %shard_map.127 = bf16[1312,128]{1,0:T(8,128)(2,1)} custom-call(bf16[2352,128]{1,0:T(8,128)(2,1)} %copy-done.20), custom_call_target="tpu_custom_call" | custom-call | bytes 671744 | tf_op jit(solution)/shard_map/pallas_call | solution.py:72
  217.5 11.3 %shard_map.129 = bf16[1312,128]{1,0:T(8,128)(2,1)} custom-call(bf16[2352,128]{1,0:T(8,128)(2,1)} %copy-done.22), custom_call_target="tpu_custom_call" | custom-call | bytes 671744 | tf_op jit(solution)/shard_map/pallas_call | solution.py:72
  228.8 3.4 %collective-permute-start.26 = (bf16[1312,128]{1,0:T(8,128)(2,1)}, bf16[1312,128]{1,0:T(8,128)(2,1)S(1)}, u32[]{:S(2)}, u32[]{:S(2)}) collective-permute-start(bf16[1312,128]{1,0:T(8,128)(2,1)} %shard_map.129), channel_id=1, source_target_pairs={{0,8},{8,16},{16,24},{24,32},{32,40},{40,48},{48,56},{56,0},{64,72... | collective-permute-start | bytes 1007624 | tf_op jit(solution)/shard_map/ppermute | solution.py:46
  232.2 9.3 %shard_map.128 = bf16[1056,128]{1,0:T(8,128)(2,1)} custom-call(bf16[2352,128]{1,0:T(8,128)(2,1)} %copy-done.24), custom_call_target="tpu_custom_call" | custom-call | bytes 540672 | tf_op jit(solution)/shard_map/pallas_call | solution.py:72
  241.5 2.1 collective-permute-start.24
  243.6 9.3 %shard_map.130 = bf16[1056,128]{1,0:T(8,128)(2,1)} custom-call(bf16[2352,128]{1,0:T(8,128)(2,1)} %collective-permute-done.13.refs_0_.refs_7_), custom_call_target="tpu_custom_call" | custom-call | bytes 540672 | tf_op jit(solution)/shard_map/pallas_call | solution.py:72
  253.3 8.5 %collective-permute-done.25.refs_5_ = bf16[784,128]{1,0:T(8,128)(2,1)S(1)} collective-permute-done((bf16[784,128]{1,0:T(8,128)(2,1)S(1)}, bf16[784,128]{1,0:T(8,128)(2,1)S(1)}, u32[]{:S(2)}, u32[]{:S(2)}) %collective-permute-start.25) | collective-permute-done | bytes 200736 | tf_op jit(solution)/shard_map/ppermute | solution.py:46
  265.1 17.1 %shard_map.131 = (bf16[256,512]{1,0:T(8,128)(2,1)}, bf16[2,5120,128]{2,1,0:T(8,128)(2,1)}) custom-call(s32[8,20]{1,0:T(8,128)S(1)} %get-tuple-element.49.table, s32[4]{0:T(128)S(1)} %pad_add_fusion.count_ref, s32[1,512]{1,0:T(1,128)S(1)} %bitcast.98, f32[20,2,128]{2,1,0:T(2,128)S(1)} %pad_maximum_fusion.3.shift_ref, ...), custom_call_target="tpu_custom_call", output_to_operand_aliasing={{1}: (19, {})} | custom-call | flops 1342177280 | bytes 2621440 | tf_op jit(solution)/shard_map/pallas_call | solution.py:306
  (171 shorter events, 42.2 us)
Async XLA Ops:
  7.2 128.2 %all-gather.2.cloned.1.call-start = ((), (), s32[]{:S(2)}) async-start(), calls=%async_computation | async-start | bytes 7077888 | tf_op jit(solution)/shard_map/all_gather | solution.py:457
  9.9 15.2 %collective-permute-start = (bf16[1568,128]{1,0:T(8,128)(2,1)S(1)}, bf16[1568,128]{1,0:T(8,128)(2,1)S(1)}, u32[]{:S(2)}, u32[]{:S(2)}) collective-permute-start(bf16[1568,128]{1,0:T(8,128)(2,1)S(1)} %bitcast.90), channel_id=1, source_target_pairs={{0,8},{8,16},{16,24},{24,32},{32,40},{40,48},{48,56},{56,0},{64,72... | collective-permute-start | bytes 1204232 | tf_op jit(solution)/shard_map/ppermute | solution.py:46
  11.9 13.2 %collective-permute-start.1 = (bf16[1568,128]{1,0:T(8,128)(2,1)S(1)}, bf16[1568,128]{1,0:T(8,128)(2,1)S(1)}, u32[]{:S(2)}, u32[]{:S(2)}) collective-permute-start(bf16[1568,128]{1,0:T(8,128)(2,1)S(1)} %bitcast.91), channel_id=1, source_target_pairs={{0,56},{8,0},{16,8},{24,16},{32,24},{40,32},{48,40},{56,48},{64,12... | collective-permute-start | bytes 1204232 | tf_op jit(solution)/shard_map/ppermute | solution.py:46
  15.9 10.8 %collective-permute-start.2 = (bf16[1568,128]{1,0:T(8,128)(2,1)S(1)}, bf16[1568,128]{1,0:T(8,128)(2,1)S(1)}, u32[]{:S(2)}, u32[]{:S(2)}) collective-permute-start(bf16[1568,128]{1,0:T(8,128)(2,1)S(1)} %bitcast.92), channel_id=1, source_target_pairs={{0,64},{8,72},{16,80},{24,88},{32,96},{40,104},{48,112},{56,120},{... | collective-permute-start | bytes 1204232 | tf_op jit(solution)/shard_map/ppermute | solution.py:46
  17.4 10.5 %collective-permute-start.3 = (bf16[1568,128]{1,0:T(8,128)(2,1)S(1)}, bf16[1568,128]{1,0:T(8,128)(2,1)S(1)}, u32[]{:S(2)}, u32[]{:S(2)}) collective-permute-start(bf16[1568,128]{1,0:T(8,128)(2,1)S(1)} %bitcast.93), channel_id=1, source_target_pairs={{0,192},{8,200},{16,208},{24,216},{32,224},{40,232},{48,240},{56,2... | collective-permute-start | bytes 1204232 | tf_op jit(solution)/shard_map/ppermute | solution.py:46
  27.9 5.8 %collective-permute-start.4 = (bf16[784,128]{1,0:T(8,128)(2,1)S(1)}, bf16[784,128]{1,0:T(8,128)(2,1)S(1)}, u32[]{:S(2)}, u32[]{:S(2)}) collective-permute-start(bf16[784,128]{1,0:T(8,128)(2,1)S(1)} %slice.18), channel_id=1, source_target_pairs={{0,192},{8,200},{16,208},{24,216},{32,224},{40,232},{48,240},{56,2... | collective-permute-start | bytes 602120 | tf_op jit(solution)/shard_map/ppermute | solution.py:46
  28.6 29.1 %collective-permute-start.14 = (bf16[1568,128]{1,0:T(8,128)(2,1)S(1)}, bf16[1568,128]{1,0:T(8,128)(2,1)S(1)}, u32[]{:S(2)}, u32[]{:S(2)}) collective-permute-start(bf16[1568,128]{1,0:T(8,128)(2,1)S(1)} %collective-permute-done.1.refs_1_.refs_4_.refs_18_), channel_id=1, source_target_pairs={{0,56},{8,0},{16,8},{24,16},{32,24},{40,32},{48,40},{56,48},{64,12... | collective-permute-start | bytes 1204232 | tf_op jit(solution)/shard_map/ppermute | solution.py:46
  30.2 27.5 %collective-permute-start.9 = (bf16[1568,128]{1,0:T(8,128)(2,1)S(1)}, bf16[1568,128]{1,0:T(8,128)(2,1)S(1)}, u32[]{:S(2)}, u32[]{:S(2)}) collective-permute-start(bf16[1568,128]{1,0:T(8,128)(2,1)S(1)} %collective-permute-done.refs_0_.refs_3_.refs_17_), channel_id=1, source_target_pairs={{0,8},{8,16},{16,24},{24,32},{32,40},{40,48},{48,56},{56,0},{64,72... | collective-permute-start | bytes 1204232 | tf_op jit(solution)/shard_map/ppermute | solution.py:46
  53.8 33.6 %collective-permute-start.5 = (bf16[2352,128]{1,0:T(8,128)(2,1)}, bf16[2352,128]{1,0:T(8,128)(2,1)}, u32[]{:S(2)}, u32[]{:S(2)}) collective-permute-start(bf16[2352,128]{1,0:T(8,128)(2,1)} %shard_map.122), channel_id=1, source_target_pairs={{0,8},{8,16},{16,24},{24,32},{32,40},{40,48},{48,56},{56,0},{64,72... | collective-permute-start | bytes 1806344 | tf_op jit(solution)/shard_map/ppermute | solution.py:46
  54.5 36.8 %collective-permute-start.7 = (bf16[2352,128]{1,0:T(8,128)(2,1)}, bf16[2352,128]{1,0:T(8,128)(2,1)}, u32[]{:S(2)}, u32[]{:S(2)}) collective-permute-start(bf16[2352,128]{1,0:T(8,128)(2,1)} %shard_map.122), channel_id=1, source_target_pairs={{0,56},{8,0},{16,8},{24,16},{32,24},{40,32},{48,40},{56,48},{64,12... | collective-permute-start | bytes 1806344 | tf_op jit(solution)/shard_map/ppermute | solution.py:46
  84.7 17.9 %collective-permute-start.19 = (bf16[3136,128]{1,0:T(8,128)(2,1)}, bf16[3136,128]{1,0:T(8,128)(2,1)S(1)}, u32[]{:S(2)}, u32[]{:S(2)}) collective-permute-start(bf16[3136,128]{1,0:T(8,128)(2,1)} %shard_map.125), channel_id=1, source_target_pairs={{0,64},{8,72},{16,80},{24,88},{32,96},{40,104},{48,112},{56,120},{... | collective-permute-start | bytes 2408456 | tf_op jit(solution)/shard_map/ppermute | solution.py:46
  86.5 13.6 %collective-permute-start.10 = (bf16[1568,128]{1,0:T(8,128)(2,1)}, bf16[1568,128]{1,0:T(8,128)(2,1)S(1)}, u32[]{:S(2)}, u32[]{:S(2)}) collective-permute-start(bf16[1568,128]{1,0:T(8,128)(2,1)} %copy-done.16), channel_id=1, source_target_pairs={{0,8},{8,16},{16,24},{24,32},{32,40},{40,48},{48,56},{56,0},{64,72... | collective-permute-start | bytes 1204232 | tf_op jit(solution)/shard_map/ppermute | solution.py:46
  86.5 65.0 %collective-permute-start.20 = (bf16[3136,128]{1,0:T(8,128)(2,1)}, bf16[3136,128]{1,0:T(8,128)(2,1)}, u32[]{:S(2)}, u32[]{:S(2)}) collective-permute-start(bf16[3136,128]{1,0:T(8,128)(2,1)} %shard_map.125), channel_id=1, source_target_pairs={{0,192},{8,200},{16,208},{24,216},{32,224},{40,232},{48,240},{56,2... | collective-permute-start | bytes 2408456 | tf_op jit(solution)/shard_map/ppermute | solution.py:46
  87.4 18.0 %collective-permute-start.15 = (bf16[1568,128]{1,0:T(8,128)(2,1)}, bf16[1568,128]{1,0:T(8,128)(2,1)S(1)}, u32[]{:S(2)}, u32[]{:S(2)}) collective-permute-start(bf16[1568,128]{1,0:T(8,128)(2,1)} %copy-done.14), channel_id=1, source_target_pairs={{0,56},{8,0},{16,8},{24,16},{32,24},{40,32},{48,40},{56,48},{64,12... | collective-permute-start | bytes 1204232 | tf_op jit(solution)/shard_map/ppermute | solution.py:46
  91.3 58.1 %collective-permute-start.6 = (bf16[2352,128]{1,0:T(8,128)(2,1)}, bf16[2352,128]{1,0:T(8,128)(2,1)}, u32[]{:S(2)}, u32[]{:S(2)}) collective-permute-start(bf16[2352,128]{1,0:T(8,128)(2,1)} %collective-permute-done.5.refs_24_), channel_id=1, source_target_pairs={{0,8},{8,16},{16,24},{24,32},{32,40},{40,48},{48,56},{56,0},{64,72... | collective-permute-start | bytes 1806344 | tf_op jit(solution)/shard_map/ppermute | solution.py:46
  100.1 50.0 %collective-permute-start.8 = (bf16[2352,128]{1,0:T(8,128)(2,1)}, bf16[2352,128]{1,0:T(8,128)(2,1)}, u32[]{:S(2)}, u32[]{:S(2)}) collective-permute-start(bf16[2352,128]{1,0:T(8,128)(2,1)} %collective-permute-done.7.refs_25_), channel_id=1, source_target_pairs={{0,56},{8,0},{16,8},{24,16},{32,24},{40,32},{48,40},{56,48},{64,12... | collective-permute-start | bytes 1806344 | tf_op jit(solution)/shard_map/ppermute | solution.py:46
  102.6 10.4 %collective-permute-start.11 = (bf16[784,128]{1,0:T(8,128)(2,1)S(1)}, bf16[784,128]{1,0:T(8,128)(2,1)S(1)}, u32[]{:S(2)}, u32[]{:S(2)}) collective-permute-start(bf16[784,128]{1,0:T(8,128)(2,1)S(1)} %slice.24), channel_id=1, source_target_pairs={{0,8},{8,16},{16,24},{24,32},{32,40},{40,48},{48,56},{56,0},{64,72... | collective-permute-start | bytes 602120 | tf_op jit(solution)/shard_map/ppermute | solution.py:46
  105.4 52.5 %collective-permute-start.21 = (bf16[1568,128]{1,0:T(8,128)(2,1)}, bf16[1568,128]{1,0:T(8,128)(2,1)}, u32[]{:S(2)}, u32[]{:S(2)}) collective-permute-start(bf16[1568,128]{1,0:T(8,128)(2,1)} %slice.25), channel_id=1, source_target_pairs={{0,64},{8,72},{16,80},{24,88},{32,96},{40,104},{48,112},{56,120},{... | collective-permute-start | bytes 1204232 | tf_op jit(solution)/shard_map/ppermute | solution.py:46
  113.1 38.4 %collective-permute-start.18 = (bf16[784,128]{1,0:T(8,128)(2,1)}, bf16[784,128]{1,0:T(8,128)(2,1)}, u32[]{:S(2)}, u32[]{:S(2)}) collective-permute-start(bf16[784,128]{1,0:T(8,128)(2,1)} %slice.20), channel_id=1, source_target_pairs={{0,64},{8,72},{16,80},{24,88},{32,96},{40,104},{48,112},{56,120},{... | collective-permute-start | bytes 602120 | tf_op jit(solution)/shard_map/ppermute | solution.py:46
  149.5 55.6 %collective-permute-start.16 = (bf16[2352,128]{1,0:T(8,128)(2,1)}, bf16[2352,128]{1,0:T(8,128)(2,1)S(1)}, u32[]{:S(2)}, u32[]{:S(2)}) collective-permute-start(bf16[2352,128]{1,0:T(8,128)(2,1)} %shard_map.124), channel_id=1, source_target_pairs={{0,64},{8,72},{16,80},{24,88},{32,96},{40,104},{48,112},{56,120},{... | collective-permute-start | bytes 1806344 | tf_op jit(solution)/shard_map/ppermute | solution.py:46
  150.1 54.9 %collective-permute-start.17 = (bf16[2352,128]{1,0:T(8,128)(2,1)}, bf16[2352,128]{1,0:T(8,128)(2,1)S(1)}, u32[]{:S(2)}, u32[]{:S(2)}) collective-permute-start(bf16[2352,128]{1,0:T(8,128)(2,1)} %shard_map.124), channel_id=1, source_target_pairs={{0,192},{8,200},{16,208},{24,216},{32,224},{40,232},{48,240},{56,2... | collective-permute-start | bytes 1806344 | tf_op jit(solution)/shard_map/ppermute | solution.py:46
  151.5 53.6 %collective-permute-start.12 = (bf16[2352,128]{1,0:T(8,128)(2,1)}, bf16[2352,128]{1,0:T(8,128)(2,1)S(1)}, u32[]{:S(2)}, u32[]{:S(2)}) collective-permute-start(bf16[2352,128]{1,0:T(8,128)(2,1)} %collective-permute-done.6.refs_26_), channel_id=1, source_target_pairs={{0,8},{8,16},{16,24},{24,32},{32,40},{40,48},{48,56},{56,0},{64,72... | collective-permute-start | bytes 1806344 | tf_op jit(solution)/shard_map/ppermute | solution.py:46
  151.5 53.6 %collective-permute-start.13 = (bf16[2352,128]{1,0:T(8,128)(2,1)}, bf16[2352,128]{1,0:T(8,128)(2,1)}, u32[]{:S(2)}, u32[]{:S(2)}) collective-permute-start(bf16[2352,128]{1,0:T(8,128)(2,1)} %collective-permute-done.8.refs_27_), channel_id=1, source_target_pairs={{0,56},{8,0},{16,8},{24,16},{32,24},{40,32},{48,40},{56,48},{64,12... | collective-permute-start | bytes 1806344 | tf_op jit(solution)/shard_map/ppermute | solution.py:46
  157.9 12.2 %collective-permute-start.22 = (bf16[1568,128]{1,0:T(8,128)(2,1)S(1)}, bf16[1568,128]{1,0:T(8,128)(2,1)S(1)}, u32[]{:S(2)}, u32[]{:S(2)}) collective-permute-start(bf16[1568,128]{1,0:T(8,128)(2,1)S(1)} %slice.26), channel_id=1, source_target_pairs={{0,192},{8,200},{16,208},{24,216},{32,224},{40,232},{48,240},{56,2... | collective-permute-start | bytes 1204232 | tf_op jit(solution)/shard_map/ppermute | solution.py:46
  205.0 56.8 %copy-start.28 = (bf16[768,384]{1,0:T(8,128)(2,1)S(1)}, bf16[768,384]{1,0:T(8,128)(2,1)}, u32[]{:S(2)}) copy-start(bf16[768,384]{1,0:T(8,128)(2,1)} %copy-done.26) | copy-start | bytes 1769476
  205.0 56.8 %copy-start.35 = (bf16[128,1024]{1,0:T(8,128)(2,1)S(1)}, bf16[128,1024]{1,0:T(8,128)(2,1)}, u32[]{:S(2)}) copy-start(bf16[128,1024]{1,0:T(8,128)(2,1)} %copy-done.33) | copy-start | bytes 786436
  205.0 56.8 %copy-start.39 = (bf16[784,128]{1,0:T(8,128)(2,1)S(1)}, bf16[784,128]{1,0:T(8,128)(2,1)}, u32[]{:S(2)}) copy-start(bf16[784,128]{1,0:T(8,128)(2,1)} %copy-done.38) | copy-start | bytes 602116
  217.4 44.4 %collective-permute-start.23 = (bf16[1312,128]{1,0:T(8,128)(2,1)}, bf16[1312,128]{1,0:T(8,128)(2,1)}, u32[]{:S(2)}, u32[]{:S(2)}) collective-permute-start(bf16[1312,128]{1,0:T(8,128)(2,1)} %shard_map.127), channel_id=1, source_target_pairs={{0,64},{8,72},{16,80},{24,88},{32,96},{40,104},{48,112},{56,120},{... | collective-permute-start | bytes 1007624 | tf_op jit(solution)/shard_map/ppermute | solution.py:46
  228.8 33.0 %collective-permute-start.26 = (bf16[1312,128]{1,0:T(8,128)(2,1)}, bf16[1312,128]{1,0:T(8,128)(2,1)S(1)}, u32[]{:S(2)}, u32[]{:S(2)}) collective-permute-start(bf16[1312,128]{1,0:T(8,128)(2,1)} %shard_map.129), channel_id=1, source_target_pairs={{0,8},{8,16},{16,24},{24,32},{32,40},{40,48},{48,56},{56,0},{64,72... | collective-permute-start | bytes 1007624 | tf_op jit(solution)/shard_map/ppermute | solution.py:46
  241.5 20.3 %collective-permute-start.24 = (bf16[1056,128]{1,0:T(8,128)(2,1)}, bf16[1056,128]{1,0:T(8,128)(2,1)S(1)}, u32[]{:S(2)}, u32[]{:S(2)}) collective-permute-start(bf16[1056,128]{1,0:T(8,128)(2,1)} %shard_map.128), channel_id=1, source_target_pairs={{0,192},{8,200},{16,208},{24,216},{32,224},{40,232},{48,240},{56,2... | collective-permute-start | bytes 811016 | tf_op jit(solution)/shard_map/ppermute | solution.py:46
  252.9 8.9 %collective-permute-start.27 = (bf16[1056,128]{1,0:T(8,128)(2,1)}, bf16[1056,128]{1,0:T(8,128)(2,1)S(1)}, u32[]{:S(2)}, u32[]{:S(2)}) collective-permute-start(bf16[1056,128]{1,0:T(8,128)(2,1)} %shard_map.130), channel_id=1, source_target_pairs={{0,56},{8,0},{16,8},{24,16},{32,24},{40,32},{48,40},{56,48},{64,12... | collective-permute-start | bytes 811016 | tf_op jit(solution)/shard_map/ppermute | solution.py:46
  253.0 8.8 %collective-permute-start.25 = (bf16[784,128]{1,0:T(8,128)(2,1)S(1)}, bf16[784,128]{1,0:T(8,128)(2,1)S(1)}, u32[]{:S(2)}, u32[]{:S(2)}) collective-permute-start(bf16[784,128]{1,0:T(8,128)(2,1)S(1)} %slice.27), channel_id=1, source_target_pairs={{0,56},{8,0},{16,8},{24,16},{32,24},{40,32},{48,40},{56,48},{64,12... | collective-permute-start | bytes 602120 | tf_op jit(solution)/shard_map/ppermute | solution.py:46
  (44 other events, 448.4 us)
Sparse Core Ops, SparseCore 0:
  9.8 44.2 all-gather.1

commit v2 on v1

--- a/solution.py
+++ b/solution.py
@@ -15,6 +15,7 @@
 STORED = 3
 BLOCK = STORED * SPAN + 16
 CUT = BLOCK + 2 * SPAN
+ROOM = 20 * 1024 * 1024
 
 
 rope_base = 500000.0
@@ -52,19 +53,11 @@
 
 
 def pack_kernel(plan, *refs):
-    sources, out, sems = refs[:-2], refs[-2], refs[-1]
-    copies, at = [], 0
-    for n, (source, start, rows) in enumerate(plan):
-        copies.append(
-            pltpu.make_async_copy(
-                sources[source].at[pl.ds(start, rows)], out.at[pl.ds(at, rows)], sems.at[n]
-            )
-        )
+    sources, out = refs[:-1], refs[-1]
+    at = 0
+    for source, start, rows in plan:
+        out[at : at + rows] = sources[source][start : start + rows]
         at += rows
-    for copy in copies:
-        copy.start()
-    for copy in copies:
-        copy.wait()
 
 
 def pack(sources, plan):
@@ -72,9 +65,9 @@
     return pl.pallas_call(
         functools.partial(pack_kernel, plan),
         out_shape=jax.ShapeDtypeStruct((rows, HW), jnp.bfloat16),
-        in_specs=[HBM] * len(sources),
-        out_specs=HBM,
-        scratch_shapes=[pltpu.SemaphoreType.DMA((len(plan),))],
+        in_specs=[VMEM] * len(sources),
+        out_specs=VMEM,
+        compiler_params=pltpu.CompilerParams(vmem_limit_bytes=2 * 1024 * 1024),
         cost_estimate=pl.CostEstimate(
             flops=0, bytes_accessed=4 * rows * HW, transcendentals=0
         ),
@@ -122,8 +115,8 @@
         in_specs=[
             pl.BlockSpec((SPAN, features), lambda i: (i, 0)),
             pl.BlockSpec((1, features), lambda i: (0, 0)),
-            pl.BlockSpec(wq.shape, lambda i: (0, 0)),
-            pl.BlockSpec(wkv.shape, lambda i: (0, 0)),
+            pl.BlockSpec(wq.shape, lambda i: (0, 0), pipeline_mode=pl.Buffered(1)),
+            pl.BlockSpec(wkv.shape, lambda i: (0, 0), pipeline_mode=pl.Buffered(1)),
             pl.BlockSpec((SPAN, HW), lambda i: (i, 0)),
             pl.BlockSpec((SPAN, HW), lambda i: (i, 0)),
         ],
@@ -132,7 +125,7 @@
             pl.BlockSpec((HW, lanes), lambda i: (0, 0)),
         ),
         scratch_shapes=[pltpu.VMEM((SPAN, features), jnp.bfloat16)],
-        compiler_params=pltpu.CompilerParams(vmem_limit_bytes=40 * 1024 * 1024),
+        compiler_params=pltpu.CompilerParams(vmem_limit_bytes=ROOM),
         cost_estimate=pl.CostEstimate(
             flops=2 * features * HW * (2 * rows + 4 * SPAN),
             bytes_accessed=2 * features * (rows + 6 * HW),
@@ -317,7 +310,7 @@
         + [pltpu.VMEM((SPAN, HW), jnp.bfloat16)]
         + [pltpu.SemaphoreType.DMA((MAXDOC,))] * 6,
         input_output_aliases={} if first else {fixed + 3: 1},
-        compiler_params=pltpu.CompilerParams(vmem_limit_bytes=32 * 1024 * 1024),
+        compiler_params=pltpu.CompilerParams(vmem_limit_bytes=ROOM),
         cost_estimate=pl.CostEstimate(
             flops=4 * lanes * HW * documents * SPAN,
             bytes_accessed=8 * documents * SPAN * HW,
@@ -354,10 +347,10 @@
     ).reshape(2 * BLOCK, HW)
 
     def keys_of(a):
-        return a[:BLOCK]
+        return pack([a], [(0, 0, BLOCK)])
 
     def values_of(a):
-        return a[BLOCK:]
+        return pack([a], [(0, BLOCK, BLOCK)])
 
     def last_hop(a, b, dx, dz):
         left = pack([a], [(0, 0, CUT), (0, 2 * BLOCK - 16, 16)])
@@ -376,7 +369,8 @@
     d1m, d1p = shift(d1, 1, 0), shift(d1, -1, 0)
     w2m, w2p = shift(w1m, 0, 1), shift(w1p, 0, -1)
     z4k, z4v = shift(keys_of(z3m), 0, 1), shift(values_of(z3p), 0, -1)
-    d1a, d1b = shift(d1m[: 2 * BLOCK], 1, 0), shift(d1p[2 * BLOCK :], -1, 0)
+    d1a = shift(pack([d1m], [(0, 0, 2 * BLOCK)]), 1, 0)
+    d1b = shift(pack([d1p], [(0, 2 * BLOCK, 2 * BLOCK)]), -1, 0)
     d2 = pack([z3m, z3p, z4k], [(n, 0, BLOCK) for n in range(3)])
     d2m, d2p = shift(d2, 1, 0), shift(d2, -1, 0)
 

time: 289 us -> 196 us (0.68)
  the two profiles are of different devices: /device:TPU:26 before, /device:TPU:182 now
where the time goes in v2:
time: 196 us
  waiting for transfers between devices  54.9 us (28%)
  Pallas kernels  50.3 us (26%)
  starting transfers between devices  43.9 us (22%)
  local copies, waits for them, and re-layouts  21.5 us (11%)
  between operations  16.3 us (8%)
  other arithmetic  9.34 us (5%)
    ppermute x28, waiting for transfers between devices, shift(): return lax.ppermute(a, 'store', pairs)  54.2 us
    ppermute x28, starting transfers between devices, shift(): return lax.ppermute(a, 'store', pairs)  43.9 us
    pallas_call x2, Pallas kernels, attend(): pl.pallas_call(functools.partial(attend_kernel, first, len(kbufs), len(vb...  38.9 us
    unnamed x58, local copies, waits for them, and re-layouts  19.7 us
    pallas_call x13, Pallas kernels, pack(): pl.pallas_call(functools.partial(pack_kernel, plan), out_shape=jax.ShapeD...  5.79 us
    pallas_call x1, Pallas kernels, project(): pl.pallas_call(project_kernel, grid=(rows // SPAN,), out_shape=(jax.Shape...  5.57 us
  transfers between devices with their start and end apart: 29, of which 12 were waited for; matrix products, arithmetic and copies ran while one was open for 6% of the time, Pallas kernels for 14%

profile of v2, /device:TPU:182, one launch (start us, length us, event | category | flops | bytes accessed | tf_op | source)
XLA Modules:
  0.0 196.3 jit_solution(4112280151330512865)
XLA Ops:
  9.9 1.1 collective-permute-start
  12.5 1.5 collective-permute-start.3
  17.1 1.4 fusion
  18.6 2.5 %collective-permute-done.refs_0_.refs_3_.refs_17_ = bf16[1568,128]{1,0:T(8,128)(2,1)S(1)} collective-permute-done((bf16[1568,128]{1,0:T(8,128)(2,1)S(1)}, bf16[1568,128]{1,0:T(8,128)(2,1)S(1)}, u32[]{:S(2)}, u32[]{:S(2)}) %collective-permute-start) | collective-permute-done | bytes 401440 | tf_op jit(solution)/shard_map/ppermute | solution.py:47
  22.5 1.4 collective-permute-done.3.refs_0_.refs_1_.refs_2_.refs_16_
  24.4 2.2 %collective-permute-start.14 = (bf16[1568,128]{1,0:T(8,128)(2,1)S(1)}, bf16[1568,128]{1,0:T(8,128)(2,1)S(1)}, u32[]{:S(2)}, u32[]{:S(2)}) collective-permute-start(bf16[1568,128]{1,0:T(8,128)(2,1)S(1)} %collective-permute-done.1.refs_1_.refs_4_.refs_18_), channel_id=1, source_target_pairs={{0,56},{8,0},{16,8},{24,16},{32,24},{40,32},{48,40},{56,48},{64,12... | collective-permute-start | bytes 1204232 | tf_op jit(solution)/shard_map/ppermute | solution.py:47
  27.2 3.7 %collective-permute-done.4.refs_2_.refs_23_ = bf16[784,128]{1,0:T(8,128)(2,1)S(1)} collective-permute-done((bf16[784,128]{1,0:T(8,128)(2,1)S(1)}, bf16[784,128]{1,0:T(8,128)(2,1)S(1)}, u32[]{:S(2)}, u32[]{:S(2)}) %collective-permute-start.4) | collective-permute-done | bytes 200736 | tf_op jit(solution)/shard_map/ppermute | solution.py:47
  32.7 1.2 collective-permute-start.7
  33.9 1.3 collective-permute-done.14.refs_3_.refs_6_.refs_20_
  35.2 3.6 %collective-permute-done.9.refs_2_.refs_5_.refs_19_ = bf16[1568,128]{1,0:T(8,128)(2,1)S(1)} collective-permute-done((bf16[1568,128]{1,0:T(8,128)(2,1)S(1)}, bf16[1568,128]{1,0:T(8,128)(2,1)S(1)}, u32[]{:S(2)}, u32[]{:S(2)}) %collective-permute-start.9) | collective-permute-done | bytes 401440 | tf_op jit(solution)/shard_map/ppermute | solution.py:47
  39.8 2.9 %collective-permute-start.19 = (bf16[3136,128]{1,0:T(8,128)(2,1)}, bf16[3136,128]{1,0:T(8,128)(2,1)S(1)}, u32[]{:S(2)}, u32[]{:S(2)}) collective-permute-start(bf16[3136,128]{1,0:T(8,128)(2,1)} %shard_map.128), channel_id=1, source_target_pairs={{0,64},{8,72},{16,80},{24,88},{32,96},{40,104},{48,112},{56,120},{... | collective-permute-start | bytes 2408456 | tf_op jit(solution)/shard_map/ppermute | solution.py:47
  43.4 8.4 %collective-permute-done.5.refs_24_ = bf16[2352,128]{1,0:T(8,128)(2,1)} collective-permute-done((bf16[2352,128]{1,0:T(8,128)(2,1)S(1)}, bf16[2352,128]{1,0:T(8,128)(2,1)}, u32[]{:S(2)}, u32[]{:S(2)}) %collective-permute-start.5) | collective-permute-done | bytes 602144 | tf_op jit(solution)/shard_map/ppermute | solution.py:47
  51.8 1.8 collective-permute-start.15
  54.6 5.7 %collective-permute-done.10.refs_0_.refs_7_.refs_21_ = bf16[1568,128]{1,0:T(8,128)(2,1)S(1)} collective-permute-done((bf16[1568,128]{1,0:T(8,128)(2,1)S(1)}, bf16[1568,128]{1,0:T(8,128)(2,1)S(1)}, u32[]{:S(2)}, u32[]{:S(2)}) %collective-permute-start.10) | collective-permute-done | bytes 401440 | tf_op jit(solution)/shard_map/ppermute | solution.py:47
  60.3 1.8 collective-permute-start.8
  62.1 1.2 pad_maximum_fusion.1
  64.5 3.0 %collective-permute-start.21 = (bf16[1568,128]{1,0:T(8,128)(2,1)}, bf16[1568,128]{1,0:T(8,128)(2,1)}, u32[]{:S(2)}, u32[]{:S(2)}) collective-permute-start(bf16[1568,128]{1,0:T(8,128)(2,1)} %shard_map.129), channel_id=1, source_target_pairs={{0,64},{8,72},{16,80},{24,88},{32,96},{40,104},{48,112},{56,120},{... | collective-permute-start | bytes 1204232 | tf_op jit(solution)/shard_map/ppermute | solution.py:47
  68.6 5.4 %collective-permute-done.11.refs_2_.refs_0_ = bf16[784,128]{1,0:T(8,128)(2,1)S(1)} collective-permute-done((bf16[784,128]{1,0:T(8,128)(2,1)S(1)}, bf16[784,128]{1,0:T(8,128)(2,1)S(1)}, u32[]{:S(2)}, u32[]{:S(2)}) %collective-permute-start.11) | collective-permute-done | bytes 200736 | tf_op jit(solution)/shard_map/ppermute | solution.py:47
  74.0 2.9 %collective-permute-start.18 = (bf16[784,128]{1,0:T(8,128)(2,1)}, bf16[784,128]{1,0:T(8,128)(2,1)}, u32[]{:S(2)}, u32[]{:S(2)}) collective-permute-start(bf16[784,128]{1,0:T(8,128)(2,1)} %shard_map.127), channel_id=1, source_target_pairs={{0,64},{8,72},{16,80},{24,88},{32,96},{40,104},{48,112},{56,120},{... | collective-permute-start | bytes 602120 | tf_op jit(solution)/shard_map/ppermute | solution.py:47
  78.4 2.8 %copy-done.2 = bf16[1,768,4096]{2,1,0:T(8,128)(2,1)S(1)} copy-done((bf16[1,768,4096]{2,1,0:T(8,128)(2,1)S(1)}, bf16[1,768,4096]{2,1,0:T(8,128)(2,1)}, u32[]{:S(2)}) %copy-start.2) | copy-done | bytes 6291480
  81.2 2.2 %copy-done.3 = bf16[4096,512]{1,0:T(8,128)(2,1)S(1)} copy-done((bf16[4096,512]{1,0:T(8,128)(2,1)S(1)}, bf16[4096,512]{1,0:T(8,128)(2,1)}, u32[]{:S(2)}) %copy-start.3) | copy-done | bytes 4194328
  85.4 5.6 %shard_map.124 = (bf16[768,384]{1,0:T(8,128)(2,1)S(1)}, bf16[128,1024]{1,0:T(8,128)(2,1)S(1)}) custom-call(bf16[768,4096]{1,0:T(8,128)(2,1)S(1)} %bitcast.89, bf16[1,4096]{1,0:T(2,128)(2,1)S(1)} %broadcast_in_dim.116.gain_ref, bf16[4096,512]{1,0:T(8,128)(2,1)S(1)} %copy-done.3, bf16[4096,256]{1,0:T(8,128)(2,1)S(1)} %bitcast.88, f32[768,128]{1,0:T(8,128)S(1)} %copy-done.18, ...), custom_call_target="tpu_custom_call" | custom-call | flops 2684354560 | bytes 12582912 | tf_op jit(solution)/shard_map/pallas_call | solution.py:108
  92.5 2.0 %collective-permute-start.17 = (bf16[2352,128]{1,0:T(8,128)(2,1)}, bf16[2352,128]{1,0:T(8,128)(2,1)S(1)}, u32[]{:S(2)}, u32[]{:S(2)}) collective-permute-start(bf16[2352,128]{1,0:T(8,128)(2,1)} %shard_map.126), channel_id=1, source_target_pairs={{0,192},{8,200},{16,208},{24,216},{32,224},{40,232},{48,240},{56,2... | collective-permute-start | bytes 1806344 | tf_op jit(solution)/shard_map/ppermute | solution.py:47
  94.8 1.8 collective-permute-start.13
  98.7 1.2 shard_map.130
  101.6 12.9 %collective-permute-done.22.refs_13_ = bf16[1568,128]{1,0:T(8,128)(2,1)S(1)} collective-permute-done((bf16[1568,128]{1,0:T(8,128)(2,1)S(1)}, bf16[1568,128]{1,0:T(8,128)(2,1)S(1)}, u32[]{:S(2)}, u32[]{:S(2)}) %collective-permute-start.22) | collective-permute-done | bytes 401440 | tf_op jit(solution)/shard_map/ppermute | solution.py:47
  120.5 1.1 copy-done.15
  123.7 16.0 %shard_map.131 = (bf16[2,5120,128]{2,1,0:T(8,128)(2,1)}, f32[1,1024]{1,0:T(1,128)S(1)}, f32[1,1024]{1,0:T(1,128)S(1)}, f32[128,1024]{1,0:T(8,128)S(1)}) custom-call(s32[8,20]{1,0:T(8,128)S(1)} %get-tuple-element.48.table, s32[4]{0:T(128)S(1)} %pad_add_fusion.count_ref, s32[1,512]{1,0:T(1,128)S(1)} %bitcast.97, ...), custom_call_target="tpu_custom_call" | custom-call | flops 1342177280 | bytes 2621440 | tf_op jit(solution)/shard_map/pallas_call | solution.py:299
  139.9 14.7 %collective-permute-start.26 = (bf16[1312,128]{1,0:T(8,128)(2,1)S(1)}, bf16[1312,128]{1,0:T(8,128)(2,1)S(1)}, u32[]{:S(2)}, u32[]{:S(2)}) collective-permute-start(bf16[1312,128]{1,0:T(8,128)(2,1)S(1)} %shard_map.135), channel_id=1, source_target_pairs={{0,8},{8,16},{16,24},{24,32},{32,40},{40,48},{48,56},{56,0},{64,72... | collective-permute-start | bytes 1007624 | tf_op jit(solution)/shard_map/ppermute | solution.py:47
  154.6 2.1 %collective-permute-start.24 = (bf16[1056,128]{1,0:T(8,128)(2,1)S(1)}, bf16[1056,128]{1,0:T(8,128)(2,1)S(1)}, u32[]{:S(2)}, u32[]{:S(2)}) collective-permute-start(bf16[1056,128]{1,0:T(8,128)(2,1)S(1)} %shard_map.133), channel_id=1, source_target_pairs={{0,192},{8,200},{16,208},{24,216},{32,224},{40,232},{48,240},{56,2... | collective-permute-start | bytes 811016 | tf_op jit(solution)/shard_map/ppermute | solution.py:47
  158.6 7.8 %collective-permute-done.25.refs_5_ = bf16[784,128]{1,0:T(8,128)(2,1)S(1)} collective-permute-done((bf16[784,128]{1,0:T(8,128)(2,1)S(1)}, bf16[784,128]{1,0:T(8,128)(2,1)S(1)}, u32[]{:S(2)}, u32[]{:S(2)}) %collective-permute-start.25) | collective-permute-done | bytes 200736 | tf_op jit(solution)/shard_map/ppermute | solution.py:47
  166.5 22.9 %shard_map.137 = (bf16[256,512]{1,0:T(8,128)(2,1)}, bf16[2,5120,128]{2,1,0:T(8,128)(2,1)}) custom-call(s32[8,20]{1,0:T(8,128)S(1)} %get-tuple-element.49.table, s32[4]{0:T(128)S(1)} %pad_add_fusion.count_ref, s32[1,512]{1,0:T(1,128)S(1)} %bitcast.98, f32[20,2,128]{2,1,0:T(2,128)S(1)} %pad_maximum_fusion.3.shift_ref, ...), custom_call_target="tpu_custom_call", output_to_operand_aliasing={{1}: (19, {})} | custom-call | flops 1342177280 | bytes 2621440 | tf_op jit(solution)/shard_map/pallas_call | solution.py:299
  (133 shorter events, 33.9 us)
Async XLA Ops:
  7.2 71.3 %all-gather.2.cloned.1.call-start = ((), (), s32[]{:S(2)}) async-start(), calls=%async_computation | async-start | bytes 7077888 | tf_op jit(solution)/shard_map/all_gather | solution.py:451
  9.9 11.1 %collective-permute-start = (bf16[1568,128]{1,0:T(8,128)(2,1)S(1)}, bf16[1568,128]{1,0:T(8,128)(2,1)S(1)}, u32[]{:S(2)}, u32[]{:S(2)}) collective-permute-start(bf16[1568,128]{1,0:T(8,128)(2,1)S(1)} %bitcast.90), channel_id=1, source_target_pairs={{0,8},{8,16},{16,24},{24,32},{32,40},{40,48},{48,56},{56,0},{64,72... | collective-permute-start | bytes 1204232 | tf_op jit(solution)/shard_map/ppermute | solution.py:47
  11.0 10.8 %collective-permute-start.1 = (bf16[1568,128]{1,0:T(8,128)(2,1)S(1)}, bf16[1568,128]{1,0:T(8,128)(2,1)S(1)}, u32[]{:S(2)}, u32[]{:S(2)}) collective-permute-start(bf16[1568,128]{1,0:T(8,128)(2,1)S(1)} %bitcast.91), channel_id=1, source_target_pairs={{0,56},{8,0},{16,8},{24,16},{32,24},{40,32},{48,40},{56,48},{64,12... | collective-permute-start | bytes 1204232 | tf_op jit(solution)/shard_map/ppermute | solution.py:47
  12.0 10.5 %collective-permute-start.2 = (bf16[1568,128]{1,0:T(8,128)(2,1)S(1)}, bf16[1568,128]{1,0:T(8,128)(2,1)S(1)}, u32[]{:S(2)}, u32[]{:S(2)}) collective-permute-start(bf16[1568,128]{1,0:T(8,128)(2,1)S(1)} %bitcast.92), channel_id=1, source_target_pairs={{0,64},{8,72},{16,80},{24,88},{32,96},{40,104},{48,112},{56,120},{... | collective-permute-start | bytes 1204232 | tf_op jit(solution)/shard_map/ppermute | solution.py:47
  12.5 11.4 %collective-permute-start.3 = (bf16[1568,128]{1,0:T(8,128)(2,1)S(1)}, bf16[1568,128]{1,0:T(8,128)(2,1)S(1)}, u32[]{:S(2)}, u32[]{:S(2)}) collective-permute-start(bf16[1568,128]{1,0:T(8,128)(2,1)S(1)} %bitcast.93), channel_id=1, source_target_pairs={{0,192},{8,200},{16,208},{24,216},{32,224},{40,232},{48,240},{56,2... | collective-permute-start | bytes 1204232 | tf_op jit(solution)/shard_map/ppermute | solution.py:47
  21.0 42.2 %copy-start.4 = (bf16[1568,128]{1,0:T(8,128)(2,1)}, bf16[1568,128]{1,0:T(8,128)(2,1)S(1)}, u32[]{:S(2)}) copy-start(bf16[1568,128]{1,0:T(8,128)(2,1)S(1)} %collective-permute-done.refs_0_.refs_3_.refs_17_) | copy-start | bytes 1204228
  21.8 41.5 %copy-start.6 = (bf16[1568,128]{1,0:T(8,128)(2,1)}, bf16[1568,128]{1,0:T(8,128)(2,1)S(1)}, u32[]{:S(2)}) copy-start(bf16[1568,128]{1,0:T(8,128)(2,1)S(1)} %collective-permute-done.1.refs_1_.refs_4_.refs_18_) | copy-start | bytes 1204228
  23.9 7.0 %collective-permute-start.4 = (bf16[784,128]{1,0:T(8,128)(2,1)S(1)}, bf16[784,128]{1,0:T(8,128)(2,1)S(1)}, u32[]{:S(2)}, u32[]{:S(2)}) collective-permute-start(bf16[784,128]{1,0:T(8,128)(2,1)S(1)} %shard_map.122), channel_id=1, source_target_pairs={{0,192},{8,200},{16,208},{24,216},{32,224},{40,232},{48,240},{56,2... | collective-permute-start | bytes 602120 | tf_op jit(solution)/shard_map/ppermute | solution.py:47
  24.4 10.9 %collective-permute-start.14 = (bf16[1568,128]{1,0:T(8,128)(2,1)S(1)}, bf16[1568,128]{1,0:T(8,128)(2,1)S(1)}, u32[]{:S(2)}, u32[]{:S(2)}) collective-permute-start(bf16[1568,128]{1,0:T(8,128)(2,1)S(1)} %collective-permute-done.1.refs_1_.refs_4_.refs_18_), channel_id=1, source_target_pairs={{0,56},{8,0},{16,8},{24,16},{32,24},{40,32},{48,40},{56,48},{64,12... | collective-permute-start | bytes 1204232 | tf_op jit(solution)/shard_map/ppermute | solution.py:47
  26.6 12.2 %collective-permute-start.9 = (bf16[1568,128]{1,0:T(8,128)(2,1)S(1)}, bf16[1568,128]{1,0:T(8,128)(2,1)S(1)}, u32[]{:S(2)}, u32[]{:S(2)}) collective-permute-start(bf16[1568,128]{1,0:T(8,128)(2,1)S(1)} %collective-permute-done.refs_0_.refs_3_.refs_17_), channel_id=1, source_target_pairs={{0,8},{8,16},{16,24},{24,32},{32,40},{40,48},{48,56},{56,0},{64,72... | collective-permute-start | bytes 1204232 | tf_op jit(solution)/shard_map/ppermute | solution.py:47
  31.0 20.8 %collective-permute-start.5 = (bf16[2352,128]{1,0:T(8,128)(2,1)S(1)}, bf16[2352,128]{1,0:T(8,128)(2,1)}, u32[]{:S(2)}, u32[]{:S(2)}) collective-permute-start(bf16[2352,128]{1,0:T(8,128)(2,1)S(1)} %shard_map.123), channel_id=1, source_target_pairs={{0,8},{8,16},{16,24},{24,32},{32,40},{40,48},{48,56},{56,0},{64,72... | collective-permute-start | bytes 1806344 | tf_op jit(solution)/shard_map/ppermute | solution.py:47
  32.7 34.9 %copy-start.25 = (bf16[4096,2,128]{2,1,0:T(2,128)(2,1)S(1)}, bf16[4096,2,128]{2,1,0:T(2,128)(2,1)}, u32[]{:S(2)}) copy-start(bf16[4096,2,128]{2,1,0:T(2,128)(2,1)} %param.21) | copy-start | bytes 6291460
  32.7 21.7 %collective-permute-start.7 = (bf16[2352,128]{1,0:T(8,128)(2,1)S(1)}, bf16[2352,128]{1,0:T(8,128)(2,1)}, u32[]{:S(2)}, u32[]{:S(2)}) collective-permute-start(bf16[2352,128]{1,0:T(8,128)(2,1)S(1)} %shard_map.123), channel_id=1, source_target_pairs={{0,56},{8,0},{16,8},{24,16},{32,24},{40,32},{48,40},{56,48},{64,12... | collective-permute-start | bytes 1806344 | tf_op jit(solution)/shard_map/ppermute | solution.py:47
  39.8 23.5 %collective-permute-start.19 = (bf16[3136,128]{1,0:T(8,128)(2,1)}, bf16[3136,128]{1,0:T(8,128)(2,1)S(1)}, u32[]{:S(2)}, u32[]{:S(2)}) collective-permute-start(bf16[3136,128]{1,0:T(8,128)(2,1)} %shard_map.128), channel_id=1, source_target_pairs={{0,64},{8,72},{16,80},{24,88},{32,96},{40,104},{48,112},{56,120},{... | collective-permute-start | bytes 2408456 | tf_op jit(solution)/shard_map/ppermute | solution.py:47
  43.3 17.0 %collective-permute-start.10 = (bf16[1568,128]{1,0:T(8,128)(2,1)S(1)}, bf16[1568,128]{1,0:T(8,128)(2,1)S(1)}, u32[]{:S(2)}, u32[]{:S(2)}) collective-permute-start(bf16[1568,128]{1,0:T(8,128)(2,1)S(1)} %collective-permute-done.9.refs_2_.refs_5_.refs_19_), channel_id=1, source_target_pairs={{0,8},{8,16},{16,24},{24,32},{32,40},{40,48},{48,56},{56,0},{64,72... | collective-permute-start | bytes 1204232 | tf_op jit(solution)/shard_map/ppermute | solution.py:47
  43.3 51.5 %collective-permute-start.20 = (bf16[3136,128]{1,0:T(8,128)(2,1)}, bf16[3136,128]{1,0:T(8,128)(2,1)}, u32[]{:S(2)}, u32[]{:S(2)}) collective-permute-start(bf16[3136,128]{1,0:T(8,128)(2,1)} %shard_map.128), channel_id=1, source_target_pairs={{0,192},{8,200},{16,208},{24,216},{32,224},{40,232},{48,240},{56,2... | collective-permute-start | bytes 2408456 | tf_op jit(solution)/shard_map/ppermute | solution.py:47
  51.8 12.7 %collective-permute-start.15 = (bf16[1568,128]{1,0:T(8,128)(2,1)S(1)}, bf16[1568,128]{1,0:T(8,128)(2,1)S(1)}, u32[]{:S(2)}, u32[]{:S(2)}) collective-permute-start(bf16[1568,128]{1,0:T(8,128)(2,1)S(1)} %collective-permute-done.14.refs_3_.refs_6_.refs_20_), channel_id=1, source_target_pairs={{0,56},{8,0},{16,8},{24,16},{32,24},{40,32},{48,40},{56,48},{64,12... | collective-permute-start | bytes 1204232 | tf_op jit(solution)/shard_map/ppermute | solution.py:47
  54.4 38.1 %collective-permute-start.6 = (bf16[2352,128]{1,0:T(8,128)(2,1)}, bf16[2352,128]{1,0:T(8,128)(2,1)}, u32[]{:S(2)}, u32[]{:S(2)}) collective-permute-start(bf16[2352,128]{1,0:T(8,128)(2,1)} %collective-permute-done.5.refs_24_), channel_id=1, source_target_pairs={{0,8},{8,16},{16,24},{24,32},{32,40},{40,48},{48,56},{56,0},{64,72... | collective-permute-start | bytes 1806344 | tf_op jit(solution)/shard_map/ppermute | solution.py:47
  60.3 32.2 %collective-permute-start.8 = (bf16[2352,128]{1,0:T(8,128)(2,1)}, bf16[2352,128]{1,0:T(8,128)(2,1)}, u32[]{:S(2)}, u32[]{:S(2)}) collective-permute-start(bf16[2352,128]{1,0:T(8,128)(2,1)} %collective-permute-done.7.refs_25_), channel_id=1, source_target_pairs={{0,56},{8,0},{16,8},{24,16},{32,24},{40,32},{48,40},{56,48},{64,12... | collective-permute-start | bytes 1806344 | tf_op jit(solution)/shard_map/ppermute | solution.py:47
  63.3 10.7 %collective-permute-start.11 = (bf16[784,128]{1,0:T(8,128)(2,1)S(1)}, bf16[784,128]{1,0:T(8,128)(2,1)S(1)}, u32[]{:S(2)}, u32[]{:S(2)}) collective-permute-start(bf16[784,128]{1,0:T(8,128)(2,1)S(1)} %shard_map.125), channel_id=1, source_target_pairs={{0,8},{8,16},{16,24},{24,32},{32,40},{40,48},{48,56},{56,0},{64,72... | collective-permute-start | bytes 602120 | tf_op jit(solution)/shard_map/ppermute | solution.py:47
  64.5 35.4 %collective-permute-start.21 = (bf16[1568,128]{1,0:T(8,128)(2,1)}, bf16[1568,128]{1,0:T(8,128)(2,1)}, u32[]{:S(2)}, u32[]{:S(2)}) collective-permute-start(bf16[1568,128]{1,0:T(8,128)(2,1)} %shard_map.129), channel_id=1, source_target_pairs={{0,64},{8,72},{16,80},{24,88},{32,96},{40,104},{48,112},{56,120},{... | collective-permute-start | bytes 1204232 | tf_op jit(solution)/shard_map/ppermute | solution.py:47
  74.0 20.5 %collective-permute-start.18 = (bf16[784,128]{1,0:T(8,128)(2,1)}, bf16[784,128]{1,0:T(8,128)(2,1)}, u32[]{:S(2)}, u32[]{:S(2)}) collective-permute-start(bf16[784,128]{1,0:T(8,128)(2,1)} %shard_map.127), channel_id=1, source_target_pairs={{0,64},{8,72},{16,80},{24,88},{32,96},{40,104},{48,112},{56,120},{... | collective-permute-start | bytes 602120 | tf_op jit(solution)/shard_map/ppermute | solution.py:47
  92.5 47.2 %collective-permute-start.16 = (bf16[2352,128]{1,0:T(8,128)(2,1)}, bf16[2352,128]{1,0:T(8,128)(2,1)S(1)}, u32[]{:S(2)}, u32[]{:S(2)}) collective-permute-start(bf16[2352,128]{1,0:T(8,128)(2,1)} %shard_map.126), channel_id=1, source_target_pairs={{0,64},{8,72},{16,80},{24,88},{32,96},{40,104},{48,112},{56,120},{... | collective-permute-start | bytes 1806344 | tf_op jit(solution)/shard_map/ppermute | solution.py:47
  92.5 47.2 %collective-permute-start.17 = (bf16[2352,128]{1,0:T(8,128)(2,1)}, bf16[2352,128]{1,0:T(8,128)(2,1)S(1)}, u32[]{:S(2)}, u32[]{:S(2)}) collective-permute-start(bf16[2352,128]{1,0:T(8,128)(2,1)} %shard_map.126), channel_id=1, source_target_pairs={{0,192},{8,200},{16,208},{24,216},{32,224},{40,232},{48,240},{56,2... | collective-permute-start | bytes 1806344 | tf_op jit(solution)/shard_map/ppermute | solution.py:47
  94.6 45.2 %collective-permute-start.12 = (bf16[2352,128]{1,0:T(8,128)(2,1)}, bf16[2352,128]{1,0:T(8,128)(2,1)S(1)}, u32[]{:S(2)}, u32[]{:S(2)}) collective-permute-start(bf16[2352,128]{1,0:T(8,128)(2,1)} %collective-permute-done.6.refs_26_), channel_id=1, source_target_pairs={{0,8},{8,16},{16,24},{24,32},{32,40},{40,48},{48,56},{56,0},{64,72... | collective-permute-start | bytes 1806344 | tf_op jit(solution)/shard_map/ppermute | solution.py:47
  94.8 44.9 %collective-permute-start.13 = (bf16[2352,128]{1,0:T(8,128)(2,1)}, bf16[2352,128]{1,0:T(8,128)(2,1)}, u32[]{:S(2)}, u32[]{:S(2)}) collective-permute-start(bf16[2352,128]{1,0:T(8,128)(2,1)} %collective-permute-done.8.refs_27_), channel_id=1, source_target_pairs={{0,56},{8,0},{16,8},{24,16},{32,24},{40,32},{48,40},{56,48},{64,12... | collective-permute-start | bytes 1806344 | tf_op jit(solution)/shard_map/ppermute | solution.py:47
  99.9 14.7 %collective-permute-start.22 = (bf16[1568,128]{1,0:T(8,128)(2,1)S(1)}, bf16[1568,128]{1,0:T(8,128)(2,1)S(1)}, u32[]{:S(2)}, u32[]{:S(2)}) collective-permute-start(bf16[1568,128]{1,0:T(8,128)(2,1)S(1)} %shard_map.130), channel_id=1, source_target_pairs={{0,192},{8,200},{16,208},{24,216},{32,224},{40,232},{48,240},{56,2... | collective-permute-start | bytes 1204232 | tf_op jit(solution)/shard_map/ppermute | solution.py:47
  139.8 26.7 %collective-permute-start.23 = (bf16[1312,128]{1,0:T(8,128)(2,1)S(1)}, bf16[1312,128]{1,0:T(8,128)(2,1)S(1)}, u32[]{:S(2)}, u32[]{:S(2)}) collective-permute-start(bf16[1312,128]{1,0:T(8,128)(2,1)S(1)} %shard_map.132), channel_id=1, source_target_pairs={{0,64},{8,72},{16,80},{24,88},{32,96},{40,104},{48,112},{56,120},{... | collective-permute-start | bytes 1007624 | tf_op jit(solution)/shard_map/ppermute | solution.py:47
  139.9 26.6 %collective-permute-start.26 = (bf16[1312,128]{1,0:T(8,128)(2,1)S(1)}, bf16[1312,128]{1,0:T(8,128)(2,1)S(1)}, u32[]{:S(2)}, u32[]{:S(2)}) collective-permute-start(bf16[1312,128]{1,0:T(8,128)(2,1)S(1)} %shard_map.135), channel_id=1, source_target_pairs={{0,8},{8,16},{16,24},{24,32},{32,40},{40,48},{48,56},{56,0},{64,72... | collective-permute-start | bytes 1007624 | tf_op jit(solution)/shard_map/ppermute | solution.py:47
  154.6 11.9 %collective-permute-start.24 = (bf16[1056,128]{1,0:T(8,128)(2,1)S(1)}, bf16[1056,128]{1,0:T(8,128)(2,1)S(1)}, u32[]{:S(2)}, u32[]{:S(2)}) collective-permute-start(bf16[1056,128]{1,0:T(8,128)(2,1)S(1)} %shard_map.133), channel_id=1, source_target_pairs={{0,192},{8,200},{16,208},{24,216},{32,224},{40,232},{48,240},{56,2... | collective-permute-start | bytes 811016 | tf_op jit(solution)/shard_map/ppermute | solution.py:47
  157.8 8.7 %collective-permute-start.27 = (bf16[1056,128]{1,0:T(8,128)(2,1)S(1)}, bf16[1056,128]{1,0:T(8,128)(2,1)S(1)}, u32[]{:S(2)}, u32[]{:S(2)}) collective-permute-start(bf16[1056,128]{1,0:T(8,128)(2,1)S(1)} %shard_map.136), channel_id=1, source_target_pairs={{0,56},{8,0},{16,8},{24,16},{32,24},{40,32},{48,40},{56,48},{64,12... | collective-permute-start | bytes 811016 | tf_op jit(solution)/shard_map/ppermute | solution.py:47
  157.9 8.6 %collective-permute-start.25 = (bf16[784,128]{1,0:T(8,128)(2,1)S(1)}, bf16[784,128]{1,0:T(8,128)(2,1)S(1)}, u32[]{:S(2)}, u32[]{:S(2)}) collective-permute-start(bf16[784,128]{1,0:T(8,128)(2,1)S(1)} %shard_map.134), channel_id=1, source_target_pairs={{0,56},{8,0},{16,8},{24,16},{32,24},{40,32},{48,40},{56,48},{64,12... | collective-permute-start | bytes 602120 | tf_op jit(solution)/shard_map/ppermute | solution.py:47
  (25 other events, 187.1 us)
Sparse Core Ops, SparseCore 0:
  9.8 43.1 all-gather.1

commit v3 on v2

--- a/solution.py
+++ b/solution.py
@@ -48,6 +48,7 @@
 
 
 HBM = pl.BlockSpec(memory_space=pl.ANY)
+KEPT = pl.BlockSpec(memory_space=pltpu.HBM)
 VMEM = pl.BlockSpec(memory_space=pltpu.VMEM)
 SMEM = pl.BlockSpec(memory_space=pltpu.SMEM)
 
@@ -150,7 +151,7 @@
     lanes = qt_ref.shape[1]
     nrec = pos_ref.shape[1]
     factor = HW**-0.5 * LOG2E
-    heads = [slice(h, h + SPAN) for h in range(0, lanes, SPAN)]
+    heads = [slice(0, lanes)]
 
     def pick(n, low, high, act):
         if high - low == 1:
@@ -204,7 +205,7 @@
         for h in heads:
             scores = jnp.dot(own_keys, qt_ref[:, h], preferred_element_type=jnp.float32)
             key_index = lax.broadcasted_iota(jnp.int32, scores.shape, 0)
-            query_index = lax.broadcasted_iota(jnp.int32, scores.shape, 1)
+            query_index = lax.broadcasted_iota(jnp.int32, scores.shape, 1) & (SPAN - 1)
             scores = jnp.where(key_index <= query_index, scores, -jnp.inf)
             top = jnp.max(scores, axis=0, keepdims=True)
             terms = jnp.exp2((scores - top) * factor)
@@ -270,7 +271,8 @@
 
     if not first:
         live = lax.broadcasted_iota(jnp.int32, (1, SPAN), 1) < count_ref[1]
-        for n, h in enumerate(heads):
+        for n in range(lanes // SPAN):
+            h = slice(n * SPAN, (n + 1) * SPAN)
             mixed = jnp.where(live, acc_ref[:, h] / l_ref[:, h], 0.0)
             out_ref[:, n * HW : (n + 1) * HW] = mixed.T.astype(jnp.bfloat16)
 
@@ -301,7 +303,8 @@
         out_shape=out_shape,
         in_specs=[SMEM] * 2
         + [VMEM] * 4
-        + [HBM] * (len(kbufs) + len(vbufs))
+        + ([KEPT] * 14 + [HBM] * (len(kbufs) - 14) if first else [HBM] * len(kbufs))
+        + ([KEPT] * 14 + [HBM] * (len(vbufs) - 14) if first else [HBM] * len(vbufs))
         + ([] if first else [VMEM] * 3 + [HBM]),
         out_specs=out_specs,
         scratch_shapes=([] if first else [pltpu.VMEM(s, jnp.float32) for s in running])
@@ -400,28 +403,28 @@
     live = jnp.arange(MAXDOC) < doc_total
     axis_buf = jnp.where(dx == 0, jnp.where(dz == 0, 0, 3 + one_z), jnp.where(dx == 2, 9, 1 + one_x))
     straight = (dx == 0) | (dz == 0)
-    late = ((dx == 0) & (dz == 4)) | ((dx != 0) & (one_z >= 4))
-    key_block = jnp.where(one_z >= 4, one_z - 4, one_z)
+    late = (dx != 0) & ((dz == 4) | ((dx == 2) & (one_z >= 4)))
+    far = one_z >= 4
+    row = slot * SPAN
+    key_block = jnp.where(far, one_z - 4, one_z)
     piece, cut_row, cut_scale = split(key_block)
-    kb = jnp.where(straight, axis_buf, 10 + one_x)
-    row = slot * SPAN
-    krow = jnp.where(straight, row, key_block * BLOCK + row)
-    far = (~straight) & (dx == 2) & (key_block >= 2)
-    kb = jnp.where(far, 13, kb)
-    krow = jnp.where(far, krow - 2 * BLOCK, krow)
+    half = (dx == 2) & ~far & (key_block >= 2)
+    kb = jnp.where(far, 15 + one_x, jnp.where(half, 13, 10 + one_x))
+    kb = jnp.where(straight, jnp.where((dx == 0) & (dz == 4), 14, axis_buf), kb)
+    krow = jnp.where(straight, row, (key_block - 2 * half.astype(jnp.int32)) * BLOCK + row)
     ksc = krow - row + STORED * SPAN
-    cut = late & (dx == 2)
-    kb = jnp.where(late, jnp.where(dx == 0, 0, jnp.where(cut, 3 + piece, 1 + one_x)), kb)
-    krow = jnp.where(late, jnp.where(cut, cut_row, jnp.where(dx == 0, row, key_block * BLOCK + row)), krow)
-    ksc = jnp.where(late, jnp.where(cut, cut_scale, krow - row + STORED * SPAN), ksc)
+    kb = jnp.where(late, jnp.where(dx == 2, 2 + piece, one_x), kb)
+    krow = jnp.where(late & (dx == 2), cut_row, krow)
+    ksc = jnp.where(late & (dx == 2), cut_scale, ksc)
     piece, cut_row, cut_scale = split(one_x)
-    vb = jnp.where(straight, axis_buf, 10 + one_z)
-    vrow = jnp.where(straight, jnp.where((dz == 0) & (dx == 2), row, BLOCK + row), one_x * BLOCK + row)
+    vb = jnp.where(far, 11 + one_z, 10 + one_z)
+    vb = jnp.where(straight, jnp.where((dx == 0) & (dz == 4), 14, axis_buf), vb)
+    lone = ((dz == 0) & (dx == 2)) | ((dx == 0) & (dz == 4))
+    vrow = jnp.where(straight, jnp.where(lone, row, BLOCK + row), one_x * BLOCK + row)
     vsc = vrow - row + STORED * SPAN
-    cut = late & (dx != 0) & (dz == 4)
-    vb = jnp.where(late, jnp.where(dx == 0, 0, jnp.where(cut, 3 + piece, one_z - 3)), vb)
-    vrow = jnp.where(late, jnp.where(cut, cut_row, jnp.where(dx == 0, row, one_x * BLOCK + row)), vrow)
-    vsc = jnp.where(late, jnp.where(cut, cut_scale, vrow - row + STORED * SPAN), vsc)
+    vb = jnp.where(late, jnp.where(dz == 4, 2 + piece, one_z - 4), vb)
+    vrow = jnp.where(late & (dz == 4), cut_row, vrow)
+    vsc = jnp.where(late & (dz == 4), cut_scale, vsc)
     facts = jnp.stack([jnp.arange(MAXDOC), slot, kb, krow, ksc, vb, vrow, vsc]).astype(jnp.int32)
 
     def chosen(flag):
@@ -458,25 +461,24 @@
         jnp.concatenate([-row_sin, row_sin], axis=1),
     )
 
-    w2m, w2p, new, qt = tie((w2m, w2p, new, qt))
     w3m, w3p = shift(w2m, 0, 1), shift(w2p, 0, -1)
+    w3m, w3p, d2m, d2p, new, qt = tie((w3m, w3p, d2m, d2p, new, qt))
+    w4a, w4b = last_hop(w3m, w3p, 0, 1)
+    d2a, d2b = last_hop(d2m, d2p, 1, 0)
     straight_bufs = [own, x1m, x1p, z1m, z1p, z2m, z2p, z3m, z3p]
     common = (counts, flat_pos[None], turns, new, qt)
     context, *state = attend(
         True,
-        straight_bufs + [x2k, d1m, d1p, d1a, d1b],
-        straight_bufs + [x2v, w1m, w1p, w2m, w2p],
+        straight_bufs + [x2k, d1m, d1p, d1a, d1b, z4k, d2m, d2p],
+        straight_bufs + [x2v, w1m, w1p, w2m, w2p, z4v, w3m, w3p],
         early_table,
         *common,
         [],
     )
-    w3m, w3p, d2m, d2p, state = tie((w3m, w3p, d2m, d2p, state))
-    w4a, w4b = last_hop(w3m, w3p, 0, 1)
-    d2a, d2b = last_hop(d2m, d2p, 1, 0)
     attention, context = attend(
         False,
-        [z4k, d2m, d2p, d2a, d2b],
-        [z4v, w3m, w3p, w4a, w4b],
+        [d2m, d2p, d2a, d2b],
+        [w3m, w3p, w4a, w4b],
         late_table,
         *common,
         [*state, context],

time: 196 us -> 173 us (0.88)
  the two profiles are of different devices: /device:TPU:182 before, /device:TPU:26 now
where the time goes in v3:
time: 173 us
  Pallas kernels  49.7 us (29%)
  waiting for transfers between devices  40.3 us (23%)
  starting transfers between devices  39.6 us (23%)
  local copies, waits for them, and re-layouts  16.9 us (10%)
  between operations  16.5 us (10%)
  other arithmetic  10.1 us (6%)
    ppermute x28, waiting for transfers between devices, shift(): return lax.ppermute(a, 'store', pairs)  39.6 us
    ppermute x28, starting transfers between devices, shift(): return lax.ppermute(a, 'store', pairs)  39.5 us
    pallas_call x2, Pallas kernels, attend(): pl.pallas_call(functools.partial(attend_kernel, first, len(kbufs), len(vb...  29.7 us
    unnamed x72, local copies, waits for them, and re-layouts  15.8 us
    pallas_call x13, Pallas kernels, pack(): pl.pallas_call(functools.partial(pack_kernel, plan), out_shape=jax.ShapeD...  14.3 us
    pallas_call x1, Pallas kernels, project(): pl.pallas_call(project_kernel, grid=(rows // SPAN,), out_shape=(jax.Shape...  5.72 us
  transfers between devices with their start and end apart: 29, of which 9 were waited for; matrix products, arithmetic and copies ran while one was open for 7% of the time, Pallas kernels for 24%

profile of v3, /device:TPU:26, one launch (start us, length us, event | category | flops | bytes accessed | tf_op | source)
XLA Modules:
  0.0 173.1 jit_solution(13248106934364082658)
XLA Ops:
  9.9 2.0 %collective-permute-start = (bf16[1568,128]{1,0:T(8,128)(2,1)S(1)}, bf16[1568,128]{1,0:T(8,128)(2,1)S(1)}, u32[]{:S(2)}, u32[]{:S(2)}) collective-permute-start(bf16[1568,128]{1,0:T(8,128)(2,1)S(1)} %bitcast.88), channel_id=1, source_target_pairs={{0,8},{8,16},{16,24},{24,32},{32,40},{40,48},{48,56},{56,0},{64,72... | collective-permute-start | bytes 1204232 | tf_op jit(solution)/shard_map/ppermute | solution.py:47
  11.9 4.0 %collective-permute-start.1 = (bf16[1568,128]{1,0:T(8,128)(2,1)S(1)}, bf16[1568,128]{1,0:T(8,128)(2,1)S(1)}, u32[]{:S(2)}, u32[]{:S(2)}) collective-permute-start(bf16[1568,128]{1,0:T(8,128)(2,1)S(1)} %bitcast.89), channel_id=1, source_target_pairs={{0,56},{8,0},{16,8},{24,16},{32,24},{40,32},{48,40},{56,48},{64,12... | collective-permute-start | bytes 1204232 | tf_op jit(solution)/shard_map/ppermute | solution.py:47
  16.0 1.5 collective-permute-start.2
  20.4 4.7 %collective-permute-done.refs_0_.refs_3_.refs_20_ = bf16[1568,128]{1,0:T(8,128)(2,1)S(1)} collective-permute-done((bf16[1568,128]{1,0:T(8,128)(2,1)S(1)}, bf16[1568,128]{1,0:T(8,128)(2,1)S(1)}, u32[]{:S(2)}, u32[]{:S(2)}) %collective-permute-start) | collective-permute-done | bytes 401440 | tf_op jit(solution)/shard_map/ppermute | solution.py:47
  25.2 1.5 collective-permute-done.2.refs_0_.refs_1_.refs_18_
  28.6 3.2 %collective-permute-start.13 = (bf16[1568,128]{1,0:T(8,128)(2,1)S(1)}, bf16[1568,128]{1,0:T(8,128)(2,1)S(1)}, u32[]{:S(2)}, u32[]{:S(2)}) collective-permute-start(bf16[1568,128]{1,0:T(8,128)(2,1)S(1)} %collective-permute-done.1.refs_1_.refs_4_.refs_21_), channel_id=1, source_target_pairs={{0,56},{8,0},{16,8},{24,16},{32,24},{40,32},{48,40},{56,48},{64,12... | collective-permute-start | bytes 1204232 | tf_op jit(solution)/shard_map/ppermute | solution.py:47
  31.9 1.9 %collective-permute-done.4.refs_2_.refs_26_ = bf16[784,128]{1,0:T(8,128)(2,1)S(1)} collective-permute-done((bf16[784,128]{1,0:T(8,128)(2,1)S(1)}, bf16[784,128]{1,0:T(8,128)(2,1)S(1)}, u32[]{:S(2)}, u32[]{:S(2)}) %collective-permute-start.4) | collective-permute-done | bytes 200736 | tf_op jit(solution)/shard_map/ppermute | solution.py:47
  34.6 1.7 collective-permute-start.8
  36.9 4.2 %collective-permute-done.11.refs_2_.refs_5_.refs_22_ = bf16[1568,128]{1,0:T(8,128)(2,1)S(1)} collective-permute-done((bf16[1568,128]{1,0:T(8,128)(2,1)S(1)}, bf16[1568,128]{1,0:T(8,128)(2,1)S(1)}, u32[]{:S(2)}, u32[]{:S(2)}) %collective-permute-start.11) | collective-permute-done | bytes 401440 | tf_op jit(solution)/shard_map/ppermute | solution.py:47
  42.6 1.5 collective-permute-start.23
  44.9 3.5 %collective-permute-start.14 = (bf16[1568,128]{1,0:T(8,128)(2,1)S(1)}, bf16[1568,128]{1,0:T(8,128)(2,1)S(1)}, u32[]{:S(2)}, u32[]{:S(2)}) collective-permute-start(bf16[1568,128]{1,0:T(8,128)(2,1)S(1)} %collective-permute-done.13.refs_3_.refs_6_.refs_23_), channel_id=1, source_target_pairs={{0,56},{8,0},{16,8},{24,16},{32,24},{40,32},{48,40},{56,48},{64,12... | collective-permute-start | bytes 1204232 | tf_op jit(solution)/shard_map/ppermute | solution.py:47
  48.4 6.2 %collective-permute-done.8.refs_28_ = bf16[2352,128]{1,0:T(8,128)(2,1)} collective-permute-done((bf16[2352,128]{1,0:T(8,128)(2,1)}, bf16[2352,128]{1,0:T(8,128)(2,1)}, u32[]{:S(2)}, u32[]{:S(2)}) %collective-permute-start.8) | collective-permute-done | bytes 602144 | tf_op jit(solution)/shard_map/ppermute | solution.py:47
  54.6 3.7 %collective-permute-start.9 = (bf16[2352,128]{1,0:T(8,128)(2,1)}, bf16[2352,128]{1,0:T(8,128)(2,1)}, u32[]{:S(2)}, u32[]{:S(2)}) collective-permute-start(bf16[2352,128]{1,0:T(8,128)(2,1)} %collective-permute-done.8.refs_28_), channel_id=1, source_target_pairs={{0,56},{8,0},{16,8},{24,16},{32,24},{40,32},{48,40},{56,48},{64,12... | collective-permute-start | bytes 1806344 | tf_op jit(solution)/shard_map/ppermute | solution.py:47
  58.9 2.0 %collective-permute-done.12.refs_0_.refs_7_.refs_24_ = bf16[1568,128]{1,0:T(8,128)(2,1)S(1)} collective-permute-done((bf16[1568,128]{1,0:T(8,128)(2,1)S(1)}, bf16[1568,128]{1,0:T(8,128)(2,1)S(1)}, u32[]{:S(2)}, u32[]{:S(2)}) %collective-permute-start.12) | collective-permute-done | bytes 401440 | tf_op jit(solution)/shard_map/ppermute | solution.py:47
  60.9 2.7 %collective-permute-start.24 = (bf16[3136,128]{1,0:T(8,128)(2,1)}, bf16[3136,128]{1,0:T(8,128)(2,1)S(1)}, u32[]{:S(2)}, u32[]{:S(2)}) collective-permute-start(bf16[3136,128]{1,0:T(8,128)(2,1)} %shard_map.132), channel_id=1, source_target_pairs={{0,192},{8,200},{16,208},{24,216},{32,224},{40,232},{48,240},{56,2... | collective-permute-start | bytes 2408456 | tf_op jit(solution)/shard_map/ppermute | solution.py:47
  64.4 17.4 %collective-permute-done.15.refs_2_.refs_14_ = bf16[784,128]{1,0:T(8,128)(2,1)S(1)} collective-permute-done((bf16[784,128]{1,0:T(8,128)(2,1)S(1)}, bf16[784,128]{1,0:T(8,128)(2,1)S(1)}, u32[]{:S(2)}, u32[]{:S(2)}) %collective-permute-start.15) | collective-permute-done | bytes 200736 | tf_op jit(solution)/shard_map/ppermute | solution.py:47
  82.8 1.9 %collective-permute-start.17 = (bf16[2352,128]{1,0:T(8,128)(2,1)}, bf16[2352,128]{1,0:T(8,128)(2,1)}, u32[]{:S(2)}, u32[]{:S(2)}) collective-permute-start(bf16[2352,128]{1,0:T(8,128)(2,1)} %shard_map.125), channel_id=1, source_target_pairs={{0,192},{8,200},{16,208},{24,216},{32,224},{40,232},{48,240},{56,2... | collective-permute-start | bytes 1806344 | tf_op jit(solution)/shard_map/ppermute | solution.py:47
  84.7 2.6 %fusion = (f32[768,64]{1,0:T(8,128)}, f32[768,64]{1,0:T(8,128)}, f32[768,64]{1,0:T(8,128)}) fusion(f32[64]{0:T(128)S(1)} %negate_power_fusion, f32[768]{0:T(1024)S(1)} %add_convert_fusion), kind=kLoop, calls=%fused_computation.6 | loop fusion | flops 98304 | bytes 593152 | tf_op jit(solution)/shard_map/neg | solution.py:461
  87.4 2.1 %collective-permute-start.7 = (bf16[2352,128]{1,0:T(8,128)(2,1)}, bf16[2352,128]{1,0:T(8,128)(2,1)}, u32[]{:S(2)}, u32[]{:S(2)}) collective-permute-start(bf16[2352,128]{1,0:T(8,128)(2,1)} %collective-permute-done.6.refs_29_), channel_id=1, source_target_pairs={{0,8},{8,16},{16,24},{24,32},{32,40},{40,48},{48,56},{56,0},{64,72... | collective-permute-start | bytes 1806344 | tf_op jit(solution)/shard_map/ppermute | solution.py:47
  89.6 1.9 %shard_map.133 = bf16[1568,128]{1,0:T(8,128)(2,1)} custom-call(bf16[3136,128]{1,0:T(8,128)(2,1)} %collective-permute-done.23.refs_0_.refs_10_), custom_call_target="tpu_custom_call" | custom-call | bytes 802816 | tf_op jit(solution)/shard_map/pallas_call | solution.py:66
  94.2 2.6 %pad_maximum_fusion.1 = (f32[768,128]{1,0:T(8,128)}, f32[768,128]{1,0:T(8,128)}) fusion(f32[768,64]{1,0:T(8,128)} %get-tuple-element.55, f32[768,64]{1,0:T(8,128)} %get-tuple-element.54, f32[768,64]{1,0:T(8,128)} %get-tuple-element.53), kind=kLoop, calls=%fused_computation.4 | loop fusion | flops 196608 | bytes 1376256 | tf_op jit(solution)/shard_map/concatenate | solution.py:460
  102.3 2.8 %copy-done.3 = bf16[1,768,4096]{2,1,0:T(8,128)(2,1)S(1)} copy-done((bf16[1,768,4096]{2,1,0:T(8,128)(2,1)S(1)}, bf16[1,768,4096]{2,1,0:T(8,128)(2,1)}, u32[]{:S(2)}) %copy-start.3) | copy-done | bytes 6291480
  105.1 2.2 %copy-done.4 = bf16[4096,512]{1,0:T(8,128)(2,1)S(1)} copy-done((bf16[4096,512]{1,0:T(8,128)(2,1)S(1)}, bf16[4096,512]{1,0:T(8,128)(2,1)}, u32[]{:S(2)}) %copy-start.4) | copy-done | bytes 4194328
  109.2 5.7 %shard_map.126 = (bf16[768,384]{1,0:T(8,128)(2,1)S(1)}, bf16[128,1024]{1,0:T(8,128)(2,1)S(1)}) custom-call(bf16[768,4096]{1,0:T(8,128)(2,1)S(1)} %bitcast.87, bf16[1,4096]{1,0:T(2,128)(2,1)S(1)} %broadcast_in_dim.116.gain_ref, bf16[4096,512]{1,0:T(8,128)(2,1)S(1)} %copy-done.4, bf16[4096,256]{1,0:T(8,128)(2,1)S(1)} %bitcast.86, f32[768,128]{1,0:T(8,128)S(1)} %copy-done.20, ...), custom_call_target="tpu_custom_call" | custom-call | flops 2684354560 | bytes 12582912 | tf_op jit(solution)/shard_map/pallas_call | solution.py:109
  116.6 2.0 %shard_map.127 = bf16[1312,128]{1,0:T(8,128)(2,1)} custom-call(bf16[2352,128]{1,0:T(8,128)(2,1)} %collective-permute-done.16.refs_0_.refs_15_), custom_call_target="tpu_custom_call" | custom-call | bytes 671744 | tf_op jit(solution)/shard_map/pallas_call | solution.py:66
  118.5 2.0 %collective-permute-start.18 = (bf16[1312,128]{1,0:T(8,128)(2,1)}, bf16[1312,128]{1,0:T(8,128)(2,1)}, u32[]{:S(2)}, u32[]{:S(2)}) collective-permute-start(bf16[1312,128]{1,0:T(8,128)(2,1)} %shard_map.127), channel_id=1, source_target_pairs={{0,64},{8,72},{16,80},{24,88},{32,96},{40,104},{48,112},{56,120},{... | collective-permute-start | bytes 1007624 | tf_op jit(solution)/shard_map/ppermute | solution.py:47
  120.6 1.8 %shard_map.129 = bf16[1312,128]{1,0:T(8,128)(2,1)} custom-call(bf16[2352,128]{1,0:T(8,128)(2,1)} %collective-permute-done.7.refs_0_.refs_32_.refs_4_), custom_call_target="tpu_custom_call" | custom-call | bytes 671744 | tf_op jit(solution)/shard_map/pallas_call | solution.py:66
  122.4 1.8 %shard_map.128 = bf16[1056,128]{1,0:T(8,128)(2,1)} custom-call(bf16[2352,128]{1,0:T(8,128)(2,1)} %collective-permute-done.17.refs_0_.refs_16_.refs_1_), custom_call_target="tpu_custom_call" | custom-call | bytes 540672 | tf_op jit(solution)/shard_map/pallas_call | solution.py:66
  124.2 1.8 %shard_map.130 = bf16[1056,128]{1,0:T(8,128)(2,1)} custom-call(bf16[2352,128]{1,0:T(8,128)(2,1)} %collective-permute-done.10.refs_0_.refs_33_.refs_5_), custom_call_target="tpu_custom_call" | custom-call | bytes 540672 | tf_op jit(solution)/shard_map/pallas_call | solution.py:66
  127.9 2.4 %collective-permute-start.21 = (bf16[1056,128]{1,0:T(8,128)(2,1)}, bf16[1056,128]{1,0:T(8,128)(2,1)}, u32[]{:S(2)}, u32[]{:S(2)}) collective-permute-start(bf16[1056,128]{1,0:T(8,128)(2,1)} %shard_map.130), channel_id=1, source_target_pairs={{0,56},{8,0},{16,8},{24,16},{32,24},{40,32},{48,40},{56,48},{64,12... | collective-permute-start | bytes 811016 | tf_op jit(solution)/shard_map/ppermute | solution.py:47
  136.5 21.9 %shard_map.136 = (bf16[2,5120,128]{2,1,0:T(8,128)(2,1)}, f32[1,1024]{1,0:T(1,128)S(1)}, f32[1,1024]{1,0:T(1,128)S(1)}, f32[128,1024]{1,0:T(8,128)S(1)}) custom-call(s32[8,20]{1,0:T(8,128)S(1)} %get-tuple-element.38.table, s32[4]{0:T(128)S(1)} %pad_add_fusion.count_ref, s32[1,512]{1,0:T(1,128)S(1)} %bitcast.95, ...), custom_call_target="tpu_custom_call" | custom-call | flops 1342177280 | bytes 2621440 | tf_op jit(solution)/shard_map/pallas_call | solution.py:301
  158.4 7.8 %shard_map.137 = (bf16[256,512]{1,0:T(8,128)(2,1)}, bf16[2,5120,128]{2,1,0:T(8,128)(2,1)}) custom-call(s32[8,20]{1,0:T(8,128)S(1)} %get-tuple-element.39.table, s32[4]{0:T(128)S(1)} %pad_add_fusion.count_ref, s32[1,512]{1,0:T(1,128)S(1)} %bitcast.96, f32[20,2,128]{2,1,0:T(2,128)S(1)} %pad_maximum_fusion.3.shift_ref, ...), custom_call_target="tpu_custom_call", output_to_operand_aliasing={{1}: (17, {})} | custom-call | flops 1342177280 | bytes 2621440 | tf_op jit(solution)/shard_map/pallas_call | solution.py:301
  (147 shorter events, 31.5 us)
Async XLA Ops:
  7.2 95.1 %all-gather.2.cloned.1.call-start = ((), (), s32[]{:S(2)}) async-start(), calls=%async_computation | async-start | bytes 7077888 | tf_op jit(solution)/shard_map/all_gather | solution.py:454
  9.9 53.7 %copy-start.26 = (s32[1,4,128]{2,1,0:T(4,128)S(1)}, s32[1,4,128]{2,1,0:T(4,128)}, u32[]{:S(2)}) copy-start(s32[1,4,128]{2,1,0:T(4,128)} %param.16) | copy-start | bytes 6148
  9.9 15.2 %collective-permute-start = (bf16[1568,128]{1,0:T(8,128)(2,1)S(1)}, bf16[1568,128]{1,0:T(8,128)(2,1)S(1)}, u32[]{:S(2)}, u32[]{:S(2)}) collective-permute-start(bf16[1568,128]{1,0:T(8,128)(2,1)S(1)} %bitcast.88), channel_id=1, source_target_pairs={{0,8},{8,16},{16,24},{24,32},{32,40},{40,48},{48,56},{56,0},{64,72... | collective-permute-start | bytes 1204232 | tf_op jit(solution)/shard_map/ppermute | solution.py:47
  11.9 13.2 %collective-permute-start.1 = (bf16[1568,128]{1,0:T(8,128)(2,1)S(1)}, bf16[1568,128]{1,0:T(8,128)(2,1)S(1)}, u32[]{:S(2)}, u32[]{:S(2)}) collective-permute-start(bf16[1568,128]{1,0:T(8,128)(2,1)S(1)} %bitcast.89), channel_id=1, source_target_pairs={{0,56},{8,0},{16,8},{24,16},{32,24},{40,32},{48,40},{56,48},{64,12... | collective-permute-start | bytes 1204232 | tf_op jit(solution)/shard_map/ppermute | solution.py:47
  16.0 10.8 %collective-permute-start.2 = (bf16[1568,128]{1,0:T(8,128)(2,1)S(1)}, bf16[1568,128]{1,0:T(8,128)(2,1)S(1)}, u32[]{:S(2)}, u32[]{:S(2)}) collective-permute-start(bf16[1568,128]{1,0:T(8,128)(2,1)S(1)} %bitcast.90), channel_id=1, source_target_pairs={{0,64},{8,72},{16,80},{24,88},{32,96},{40,104},{48,112},{56,120},{... | collective-permute-start | bytes 1204232 | tf_op jit(solution)/shard_map/ppermute | solution.py:47
  17.4 10.5 %collective-permute-start.3 = (bf16[1568,128]{1,0:T(8,128)(2,1)S(1)}, bf16[1568,128]{1,0:T(8,128)(2,1)S(1)}, u32[]{:S(2)}, u32[]{:S(2)}) collective-permute-start(bf16[1568,128]{1,0:T(8,128)(2,1)S(1)} %bitcast.91), channel_id=1, source_target_pairs={{0,192},{8,200},{16,208},{24,216},{32,224},{40,232},{48,240},{56,2... | collective-permute-start | bytes 1204232 | tf_op jit(solution)/shard_map/ppermute | solution.py:47
  27.9 5.8 %collective-permute-start.4 = (bf16[784,128]{1,0:T(8,128)(2,1)S(1)}, bf16[784,128]{1,0:T(8,128)(2,1)S(1)}, u32[]{:S(2)}, u32[]{:S(2)}) collective-permute-start(bf16[784,128]{1,0:T(8,128)(2,1)S(1)} %shard_map.122), channel_id=1, source_target_pairs={{0,192},{8,200},{16,208},{24,216},{32,224},{40,232},{48,240},{56,2... | collective-permute-start | bytes 602120 | tf_op jit(solution)/shard_map/ppermute | solution.py:47
  28.6 12.6 %collective-permute-start.11 = (bf16[1568,128]{1,0:T(8,128)(2,1)S(1)}, bf16[1568,128]{1,0:T(8,128)(2,1)S(1)}, u32[]{:S(2)}, u32[]{:S(2)}) collective-permute-start(bf16[1568,128]{1,0:T(8,128)(2,1)S(1)} %collective-permute-done.refs_0_.refs_3_.refs_20_), channel_id=1, source_target_pairs={{0,8},{8,16},{16,24},{24,32},{32,40},{40,48},{48,56},{56,0},{64,72... | collective-permute-start | bytes 1204232 | tf_op jit(solution)/shard_map/ppermute | solution.py:47
  28.6 13.0 %collective-permute-start.13 = (bf16[1568,128]{1,0:T(8,128)(2,1)S(1)}, bf16[1568,128]{1,0:T(8,128)(2,1)S(1)}, u32[]{:S(2)}, u32[]{:S(2)}) collective-permute-start(bf16[1568,128]{1,0:T(8,128)(2,1)S(1)} %collective-permute-done.1.refs_1_.refs_4_.refs_21_), channel_id=1, source_target_pairs={{0,56},{8,0},{16,8},{24,16},{32,24},{40,32},{48,40},{56,48},{64,12... | collective-permute-start | bytes 1204232 | tf_op jit(solution)/shard_map/ppermute | solution.py:47
  34.6 20.0 %collective-permute-start.8 = (bf16[2352,128]{1,0:T(8,128)(2,1)}, bf16[2352,128]{1,0:T(8,128)(2,1)}, u32[]{:S(2)}, u32[]{:S(2)}) collective-permute-start(bf16[2352,128]{1,0:T(8,128)(2,1)} %shard_map.123), channel_id=1, source_target_pairs={{0,56},{8,0},{16,8},{24,16},{32,24},{40,32},{48,40},{56,48},{64,12... | collective-permute-start | bytes 1806344 | tf_op jit(solution)/shard_map/ppermute | solution.py:47
  36.4 27.1 %collective-permute-start.5 = (bf16[2352,128]{1,0:T(8,128)(2,1)}, bf16[2352,128]{1,0:T(8,128)(2,1)}, u32[]{:S(2)}, u32[]{:S(2)}) collective-permute-start(bf16[2352,128]{1,0:T(8,128)(2,1)} %shard_map.123), channel_id=1, source_target_pairs={{0,8},{8,16},{16,24},{24,32},{32,40},{40,48},{48,56},{56,0},{64,72... | collective-permute-start | bytes 1806344 | tf_op jit(solution)/shard_map/ppermute | solution.py:47
  41.2 46.2 %copy-start.9 = (bf16[1568,128]{1,0:T(8,128)(2,1)}, bf16[1568,128]{1,0:T(8,128)(2,1)S(1)}, u32[]{:S(2)}) copy-start(bf16[1568,128]{1,0:T(8,128)(2,1)S(1)} %collective-permute-done.11.refs_2_.refs_5_.refs_22_) | copy-start | bytes 1204228
  41.6 45.8 %copy-start.11 = (bf16[1568,128]{1,0:T(8,128)(2,1)}, bf16[1568,128]{1,0:T(8,128)(2,1)S(1)}, u32[]{:S(2)}) copy-start(bf16[1568,128]{1,0:T(8,128)(2,1)S(1)} %collective-permute-done.13.refs_3_.refs_6_.refs_23_) | copy-start | bytes 1204228
  42.6 40.1 %collective-permute-start.23 = (bf16[3136,128]{1,0:T(8,128)(2,1)}, bf16[3136,128]{1,0:T(8,128)(2,1)}, u32[]{:S(2)}, u32[]{:S(2)}) collective-permute-start(bf16[3136,128]{1,0:T(8,128)(2,1)} %shard_map.132), channel_id=1, source_target_pairs={{0,64},{8,72},{16,80},{24,88},{32,96},{40,104},{48,112},{56,120},{... | collective-permute-start | bytes 2408456 | tf_op jit(solution)/shard_map/ppermute | solution.py:47
  44.1 16.8 %collective-permute-start.12 = (bf16[1568,128]{1,0:T(8,128)(2,1)S(1)}, bf16[1568,128]{1,0:T(8,128)(2,1)S(1)}, u32[]{:S(2)}, u32[]{:S(2)}) collective-permute-start(bf16[1568,128]{1,0:T(8,128)(2,1)S(1)} %collective-permute-done.11.refs_2_.refs_5_.refs_22_), channel_id=1, source_target_pairs={{0,8},{8,16},{16,24},{24,32},{32,40},{40,48},{48,56},{56,0},{64,72... | collective-permute-start | bytes 1204232 | tf_op jit(solution)/shard_map/ppermute | solution.py:47
  44.9 18.7 %collective-permute-start.14 = (bf16[1568,128]{1,0:T(8,128)(2,1)S(1)}, bf16[1568,128]{1,0:T(8,128)(2,1)S(1)}, u32[]{:S(2)}, u32[]{:S(2)}) collective-permute-start(bf16[1568,128]{1,0:T(8,128)(2,1)S(1)} %collective-permute-done.13.refs_3_.refs_6_.refs_23_), channel_id=1, source_target_pairs={{0,56},{8,0},{16,8},{24,16},{32,24},{40,32},{48,40},{56,48},{64,12... | collective-permute-start | bytes 1204232 | tf_op jit(solution)/shard_map/ppermute | solution.py:47
  54.6 30.1 %collective-permute-start.9 = (bf16[2352,128]{1,0:T(8,128)(2,1)}, bf16[2352,128]{1,0:T(8,128)(2,1)}, u32[]{:S(2)}, u32[]{:S(2)}) collective-permute-start(bf16[2352,128]{1,0:T(8,128)(2,1)} %collective-permute-done.8.refs_28_), channel_id=1, source_target_pairs={{0,56},{8,0},{16,8},{24,16},{32,24},{40,32},{48,40},{56,48},{64,12... | collective-permute-start | bytes 1806344 | tf_op jit(solution)/shard_map/ppermute | solution.py:47
  60.9 30.6 %collective-permute-start.24 = (bf16[3136,128]{1,0:T(8,128)(2,1)}, bf16[3136,128]{1,0:T(8,128)(2,1)S(1)}, u32[]{:S(2)}, u32[]{:S(2)}) collective-permute-start(bf16[3136,128]{1,0:T(8,128)(2,1)} %shard_map.132), channel_id=1, source_target_pairs={{0,192},{8,200},{16,208},{24,216},{32,224},{40,232},{48,240},{56,2... | collective-permute-start | bytes 2408456 | tf_op jit(solution)/shard_map/ppermute | solution.py:47
  63.6 23.8 %collective-permute-start.6 = (bf16[2352,128]{1,0:T(8,128)(2,1)}, bf16[2352,128]{1,0:T(8,128)(2,1)}, u32[]{:S(2)}, u32[]{:S(2)}) collective-permute-start(bf16[2352,128]{1,0:T(8,128)(2,1)} %collective-permute-done.5.refs_27_), channel_id=1, source_target_pairs={{0,8},{8,16},{16,24},{24,32},{32,40},{40,48},{48,56},{56,0},{64,72... | collective-permute-start | bytes 1806344 | tf_op jit(solution)/shard_map/ppermute | solution.py:47
  63.7 18.1 %collective-permute-start.15 = (bf16[784,128]{1,0:T(8,128)(2,1)S(1)}, bf16[784,128]{1,0:T(8,128)(2,1)S(1)}, u32[]{:S(2)}, u32[]{:S(2)}) collective-permute-start(bf16[784,128]{1,0:T(8,128)(2,1)S(1)} %shard_map.124), channel_id=1, source_target_pairs={{0,8},{8,16},{16,24},{24,32},{32,40},{40,48},{48,56},{56,0},{64,72... | collective-permute-start | bytes 602120 | tf_op jit(solution)/shard_map/ppermute | solution.py:47
  82.7 16.3 %collective-permute-start.16 = (bf16[2352,128]{1,0:T(8,128)(2,1)}, bf16[2352,128]{1,0:T(8,128)(2,1)}, u32[]{:S(2)}, u32[]{:S(2)}) collective-permute-start(bf16[2352,128]{1,0:T(8,128)(2,1)} %shard_map.125), channel_id=1, source_target_pairs={{0,64},{8,72},{16,80},{24,88},{32,96},{40,104},{48,112},{56,120},{... | collective-permute-start | bytes 1806344 | tf_op jit(solution)/shard_map/ppermute | solution.py:47
  82.8 17.4 %collective-permute-start.17 = (bf16[2352,128]{1,0:T(8,128)(2,1)}, bf16[2352,128]{1,0:T(8,128)(2,1)}, u32[]{:S(2)}, u32[]{:S(2)}) collective-permute-start(bf16[2352,128]{1,0:T(8,128)(2,1)} %shard_map.125), channel_id=1, source_target_pairs={{0,192},{8,200},{16,208},{24,216},{32,224},{40,232},{48,240},{56,2... | collective-permute-start | bytes 1806344 | tf_op jit(solution)/shard_map/ppermute | solution.py:47
  84.7 16.7 %collective-permute-start.10 = (bf16[2352,128]{1,0:T(8,128)(2,1)}, bf16[2352,128]{1,0:T(8,128)(2,1)}, u32[]{:S(2)}, u32[]{:S(2)}) collective-permute-start(bf16[2352,128]{1,0:T(8,128)(2,1)} %collective-permute-done.9.refs_30_), channel_id=1, source_target_pairs={{0,56},{8,0},{16,8},{24,16},{32,24},{40,32},{48,40},{56,48},{64,12... | collective-permute-start | bytes 1806344 | tf_op jit(solution)/shard_map/ppermute | solution.py:47
  87.4 29.2 %collective-permute-start.7 = (bf16[2352,128]{1,0:T(8,128)(2,1)}, bf16[2352,128]{1,0:T(8,128)(2,1)}, u32[]{:S(2)}, u32[]{:S(2)}) collective-permute-start(bf16[2352,128]{1,0:T(8,128)(2,1)} %collective-permute-done.6.refs_29_), channel_id=1, source_target_pairs={{0,8},{8,16},{16,24},{24,32},{32,40},{40,48},{48,56},{56,0},{64,72... | collective-permute-start | bytes 1806344 | tf_op jit(solution)/shard_map/ppermute | solution.py:47
  92.4 35.5 %collective-permute-start.25 = (bf16[1568,128]{1,0:T(8,128)(2,1)}, bf16[1568,128]{1,0:T(8,128)(2,1)}, u32[]{:S(2)}, u32[]{:S(2)}) collective-permute-start(bf16[1568,128]{1,0:T(8,128)(2,1)} %shard_map.133), channel_id=1, source_target_pairs={{0,64},{8,72},{16,80},{24,88},{32,96},{40,104},{48,112},{56,120},{... | collective-permute-start | bytes 1204232 | tf_op jit(solution)/shard_map/ppermute | solution.py:47
  99.0 27.0 %collective-permute-start.22 = (bf16[784,128]{1,0:T(8,128)(2,1)}, bf16[784,128]{1,0:T(8,128)(2,1)}, u32[]{:S(2)}, u32[]{:S(2)}) collective-permute-start(bf16[784,128]{1,0:T(8,128)(2,1)} %shard_map.131), channel_id=1, source_target_pairs={{0,64},{8,72},{16,80},{24,88},{32,96},{40,104},{48,112},{56,120},{... | collective-permute-start | bytes 602120 | tf_op jit(solution)/shard_map/ppermute | solution.py:47
  100.2 26.6 %collective-permute-start.27 = (bf16[784,128]{1,0:T(8,128)(2,1)}, bf16[784,128]{1,0:T(8,128)(2,1)}, u32[]{:S(2)}, u32[]{:S(2)}) collective-permute-start(bf16[784,128]{1,0:T(8,128)(2,1)} %shard_map.135), channel_id=1, source_target_pairs={{0,56},{8,0},{16,8},{24,16},{32,24},{40,32},{48,40},{56,48},{64,12... | collective-permute-start | bytes 602120 | tf_op jit(solution)/shard_map/ppermute | solution.py:47
  101.4 29.9 %collective-permute-start.26 = (bf16[1568,128]{1,0:T(8,128)(2,1)}, bf16[1568,128]{1,0:T(8,128)(2,1)}, u32[]{:S(2)}, u32[]{:S(2)}) collective-permute-start(bf16[1568,128]{1,0:T(8,128)(2,1)} %shard_map.134), channel_id=1, source_target_pairs={{0,192},{8,200},{16,208},{24,216},{32,224},{40,232},{48,240},{56,2... | collective-permute-start | bytes 1204232 | tf_op jit(solution)/shard_map/ppermute | solution.py:47
  118.5 39.9 %collective-permute-start.18 = (bf16[1312,128]{1,0:T(8,128)(2,1)}, bf16[1312,128]{1,0:T(8,128)(2,1)}, u32[]{:S(2)}, u32[]{:S(2)}) collective-permute-start(bf16[1312,128]{1,0:T(8,128)(2,1)} %shard_map.127), channel_id=1, source_target_pairs={{0,64},{8,72},{16,80},{24,88},{32,96},{40,104},{48,112},{56,120},{... | collective-permute-start | bytes 1007624 | tf_op jit(solution)/shard_map/ppermute | solution.py:47
  126.0 32.4 %collective-permute-start.20 = (bf16[1312,128]{1,0:T(8,128)(2,1)}, bf16[1312,128]{1,0:T(8,128)(2,1)}, u32[]{:S(2)}, u32[]{:S(2)}) collective-permute-start(bf16[1312,128]{1,0:T(8,128)(2,1)} %shard_map.129), channel_id=1, source_target_pairs={{0,8},{8,16},{16,24},{24,32},{32,40},{40,48},{48,56},{56,0},{64,72... | collective-permute-start | bytes 1007624 | tf_op jit(solution)/shard_map/ppermute | solution.py:47
  126.8 31.6 %collective-permute-start.19 = (bf16[1056,128]{1,0:T(8,128)(2,1)}, bf16[1056,128]{1,0:T(8,128)(2,1)}, u32[]{:S(2)}, u32[]{:S(2)}) collective-permute-start(bf16[1056,128]{1,0:T(8,128)(2,1)} %shard_map.128), channel_id=1, source_target_pairs={{0,192},{8,200},{16,208},{24,216},{32,224},{40,232},{48,240},{56,2... | collective-permute-start | bytes 811016 | tf_op jit(solution)/shard_map/ppermute | solution.py:47
  127.9 30.5 %collective-permute-start.21 = (bf16[1056,128]{1,0:T(8,128)(2,1)}, bf16[1056,128]{1,0:T(8,128)(2,1)}, u32[]{:S(2)}, u32[]{:S(2)}) collective-permute-start(bf16[1056,128]{1,0:T(8,128)(2,1)} %shard_map.130), channel_id=1, source_target_pairs={{0,56},{8,0},{16,8},{24,16},{32,24},{40,32},{48,40},{56,48},{64,12... | collective-permute-start | bytes 811016 | tf_op jit(solution)/shard_map/ppermute | solution.py:47
  (32 other events, 336.6 us)
Sparse Core Ops, SparseCore 0:
  9.8 44.2 all-gather.1

commit v4 on v3

--- a/solution.py
+++ b/solution.py
@@ -73,6 +73,28 @@
             flops=0, bytes_accessed=4 * rows * HW, transcendentals=0
         ),
     )(*sources)
+
+
+def halves_kernel(*refs):
+    for n in range(0, 4, 2):
+        a, b, left, right = refs[n], refs[n + 1], refs[n + 4], refs[n + 5]
+        left[:CUT] = a[:CUT]
+        left[CUT:] = a[2 * BLOCK - 16 : 2 * BLOCK]
+        right[...] = b[CUT:]
+
+
+def halves(*pairs):
+    shapes = [(CUT + 16, HW), (3 * BLOCK - CUT, HW)] * 2
+    return pl.pallas_call(
+        halves_kernel,
+        out_shape=[jax.ShapeDtypeStruct(shape, jnp.bfloat16) for shape in shapes],
+        in_specs=[VMEM] * 4,
+        out_specs=[VMEM] * 4,
+        compiler_params=pltpu.CompilerParams(vmem_limit_bytes=2 * 1024 * 1024),
+        cost_estimate=pl.CostEstimate(
+            flops=0, bytes_accessed=24 * BLOCK * HW, transcendentals=0
+        ),
+    )(*pairs)
 
 
 def project_kernel(hid_ref, gain_ref, wq_ref, wkv_ref, cos_ref, sin_ref, new_ref, qt_ref, nb_ref):
@@ -232,7 +254,7 @@
         high = jnp.sum(jnp.where(scale_index == 2 * slot + 1, s, 0.0), axis=0, keepdims=True)
         return codes.astype(jnp.float32) * jnp.where(upper, high, low)
 
-    def step(r, _):
+    def ready(r):
         j, slot = table[DOC, r], table[SLOT, r]
         hit = jnp.where(row_index == pos_ref[...] - j * SPAN, 1.0, 0.0).astype(jnp.bfloat16)
         fresh = jnp.dot(hit, new_ref[:nrec], preferred_element_type=jnp.float32)
@@ -251,23 +273,34 @@
         vdoc[r] = v
         pltpu.make_async_copy(kdoc.at[r], ctx_ref.at[0, place(j)], kout.at[r]).start()
         pltpu.make_async_copy(vdoc.at[r], ctx_ref.at[1, place(j)], vout.at[r]).start()
-        for h in heads:
-            scores = jnp.dot(k, qt_ref[:, h], preferred_element_type=jnp.float32)
-            before = m_ref[:, h]
-            top = jnp.maximum(before, jnp.max(scores, axis=0, keepdims=True))
-            terms = jnp.exp2((scores - top) * factor)
-            fade = jnp.exp2((before - top) * factor)
-            m_ref[:, h] = top
-            l_ref[:, h] = l_ref[:, h] * fade + jnp.sum(terms, axis=0, keepdims=True)
-            acc_ref[:, h] = acc_ref[:, h] * fade + lax.dot_general(
-                v,
-                terms.astype(jnp.bfloat16),
-                (((0,), (0,)), ((), ())),
-                preferred_element_type=jnp.float32,
-            )
+        return k, v
+
+    def absorb(k, v):
+        scores = jnp.dot(k, qt_ref[...], preferred_element_type=jnp.float32)
+        before = m_ref[...]
+        top = jnp.maximum(before, jnp.max(scores, axis=0, keepdims=True))
+        terms = jnp.exp2((scores - top) * factor)
+        fade = jnp.exp2((before - top) * factor)
+        m_ref[...] = top
+        l_ref[...] = l_ref[...] * fade + jnp.sum(terms, axis=0, keepdims=True)
+        acc_ref[...] = acc_ref[...] * fade + lax.dot_general(
+            v,
+            terms.astype(jnp.bfloat16),
+            (((0,), (0,)), ((), ())),
+            preferred_element_type=jnp.float32,
+        )
+
+    def pair(n, _):
+        k0, v0 = ready(2 * n)
+        k1, v1 = ready(2 * n + 1)
+        absorb(jnp.concatenate([k0, k1], axis=0), jnp.concatenate([v0, v1], axis=0))
         return 0
 
-    lax.fori_loop(0, count, step, 0)
+    lax.fori_loop(0, count // 2, pair, 0)
+
+    @pl.when(count % 2 == 1)
+    def _():
+        absorb(*ready(count - 1))
 
     if not first:
         live = lax.broadcasted_iota(jnp.int32, (1, SPAN), 1) < count_ref[1]
@@ -303,8 +336,7 @@
         out_shape=out_shape,
         in_specs=[SMEM] * 2
         + [VMEM] * 4
-        + ([KEPT] * 14 + [HBM] * (len(kbufs) - 14) if first else [HBM] * len(kbufs))
-        + ([KEPT] * 14 + [HBM] * (len(vbufs) - 14) if first else [HBM] * len(vbufs))
+        + [KEPT if first else HBM] * (len(kbufs) + len(vbufs))
         + ([] if first else [VMEM] * 3 + [HBM]),
         out_specs=out_specs,
         scratch_shapes=([] if first else [pltpu.VMEM(s, jnp.float32) for s in running])
@@ -355,11 +387,6 @@
     def values_of(a):
         return pack([a], [(0, BLOCK, BLOCK)])
 
-    def last_hop(a, b, dx, dz):
-        left = pack([a], [(0, 0, CUT), (0, 2 * BLOCK - 16, 16)])
-        right = pack([b], [(0, CUT, 2 * BLOCK + BLOCK - CUT)])
-        return shift(left, dx, dz), shift(right, -dx, -dz)
-
     z1m, z1p = shift(own, 0, 1), shift(own, 0, -1)
     x1m, x1p = shift(own, 1, 0), shift(own, -1, 0)
     z1m, z1p, x1m, x1p = tie((z1m, z1p, x1m, x1p))
@@ -374,8 +401,6 @@
     z4k, z4v = shift(keys_of(z3m), 0, 1), shift(values_of(z3p), 0, -1)
     d1a = shift(pack([d1m], [(0, 0, 2 * BLOCK)]), 1, 0)
     d1b = shift(pack([d1p], [(0, 2 * BLOCK, 2 * BLOCK)]), -1, 0)
-    d2 = pack([z3m, z3p, z4k], [(n, 0, BLOCK) for n in range(3)])
-    d2m, d2p = shift(d2, 1, 0), shift(d2, -1, 0)
 
     doc_list = doc_ids[0]
     doc_total = doc_count[0]
@@ -461,10 +486,14 @@
         jnp.concatenate([-row_sin, row_sin], axis=1),
     )
 
+    z4k, new, qt = tie((z4k, new, qt))
+    d2 = pack([z3m, z3p, z4k], [(n, 0, BLOCK) for n in range(3)])
+    d2m, d2p = shift(d2, 1, 0), shift(d2, -1, 0)
     w3m, w3p = shift(w2m, 0, 1), shift(w2p, 0, -1)
     w3m, w3p, d2m, d2p, new, qt = tie((w3m, w3p, d2m, d2p, new, qt))
-    w4a, w4b = last_hop(w3m, w3p, 0, 1)
-    d2a, d2b = last_hop(d2m, d2p, 1, 0)
+    w_left, w_right, d_left, d_right = halves(w3m, w3p, d2m, d2p)
+    w4a, w4b = shift(w_left, 0, 1), shift(w_right, 0, -1)
+    d2a, d2b = shift(d_left, 1, 0), shift(d_right, -1, 0)
     straight_bufs = [own, x1m, x1p, z1m, z1p, z2m, z2p, z3m, z3p]
     common = (counts, flat_pos[None], turns, new, qt)
     context, *state = attend(

time: 173 us -> 169 us (0.977); the launches traced: 173 us -> 166 us
  Pallas kernels: 49.7 us -> 39.1 us
  local copies, waits for them, and re-layouts: 16.9 us -> 24 us
  waiting for transfers between devices: 40.3 us -> 35.2 us
  starting transfers between devices: 39.6 us -> 43.4 us
  other arithmetic: 10.1 us -> 8.1 us
    unnamed x72 -> x70, local copies, waits for them, and re-layouts: 15.8 us -> 22.2 us
    pallas_call x2, Pallas kernels: 29.7 us -> 23.3 us  [attend(): pl.pallas_call(functools.partial(attend_kernel, first, len(kbufs), len(vb...]
    pallas_call x13 -> x9, Pallas kernels: 14.3 us -> 7.98 us  [pack(): pl.pallas_call(functools.partial(pack_kernel, plan), out_shape=jax.ShapeD...]
    ppermute x28, waiting for transfers between devices: 39.6 us -> 34.5 us  [shift(): return lax.ppermute(a, 'store', pairs)]
    ppermute x28, starting transfers between devices: 39.5 us -> 43.4 us  [shift(): return lax.ppermute(a, 'store', pairs)]
    pallas_call x0 -> x1, Pallas kernels: none -> 2.2 us  [halves(): pl.pallas_call(halves_kernel, out_shape=[jax.ShapeDtypeStruct(shape, jnp....]
  transfers between devices with their start and end apart: 29 -> 29, of which waited for: 9 -> 8; matrix products, arithmetic and copies ran while one was open for 7% -> 7% of each run, Pallas kernels for 24% -> 22%
where the time goes in v4:
time: 169 us; the launch traced here: 166 us
  starting transfers between devices  43.4 us (26%)
  Pallas kernels  39.1 us (23%)
  waiting for transfers between devices  35.2 us (21%)
  local copies, waits for them, and re-layouts  24 us (14%)
  between operations  16.4 us (10%)
  other arithmetic  8.1 us (5%)
    ppermute x28, starting transfers between devices, shift(): return lax.ppermute(a, 'store', pairs)  43.4 us
    ppermute x28, waiting for transfers between devices, shift(): return lax.ppermute(a, 'store', pairs)  34.5 us
    pallas_call x2, Pallas kernels, attend(): pl.pallas_call(functools.partial(attend_kernel, first, len(kbufs), len(vb...  23.3 us
    unnamed x70, local copies, waits for them, and re-layouts  22.2 us
    pallas_call x9, Pallas kernels, pack(): pl.pallas_call(functools.partial(pack_kernel, plan), out_shape=jax.ShapeD...  7.98 us
    pallas_call x1, Pallas kernels, project(): pl.pallas_call(project_kernel, grid=(rows // SPAN,), out_shape=(jax.Shape...  5.59 us
  transfers between devices with their start and end apart: 29, of which 8 were waited for; matrix products, arithmetic and copies ran while one was open for 7% of the time, Pallas kernels for 22%

profile of v4, /device:TPU:26, one launch (start us, length us, event | category | flops | bytes accessed | tf_op | source)
XLA Modules:
  0.0 166.2 jit_solution(7145334535410594097)
XLA Ops:
  9.9 2.0 %collective-permute-start = (bf16[1568,128]{1,0:T(8,128)(2,1)S(1)}, bf16[1568,128]{1,0:T(8,128)(2,1)S(1)}, u32[]{:S(2)}, u32[]{:S(2)}) collective-permute-start(bf16[1568,128]{1,0:T(8,128)(2,1)S(1)} %bitcast.88), channel_id=1, source_target_pairs={{0,8},{8,16},{16,24},{24,32},{32,40},{40,48},{48,56},{56,0},{64,72... | collective-permute-start | bytes 1204232 | tf_op jit(solution)/shard_map/ppermute | solution.py:47
  11.9 4.0 %collective-permute-start.1 = (bf16[1568,128]{1,0:T(8,128)(2,1)S(1)}, bf16[1568,128]{1,0:T(8,128)(2,1)S(1)}, u32[]{:S(2)}, u32[]{:S(2)}) collective-permute-start(bf16[1568,128]{1,0:T(8,128)(2,1)S(1)} %bitcast.89), channel_id=1, source_target_pairs={{0,56},{8,0},{16,8},{24,16},{32,24},{40,32},{48,40},{56,48},{64,12... | collective-permute-start | bytes 1204232 | tf_op jit(solution)/shard_map/ppermute | solution.py:47
  15.9 1.5 collective-permute-start.2
  22.2 2.9 %collective-permute-done.refs_0_.refs_3_.refs_20_ = bf16[1568,128]{1,0:T(8,128)(2,1)S(1)} collective-permute-done((bf16[1568,128]{1,0:T(8,128)(2,1)S(1)}, bf16[1568,128]{1,0:T(8,128)(2,1)S(1)}, u32[]{:S(2)}, u32[]{:S(2)}) %collective-permute-start) | collective-permute-done | bytes 401440 | tf_op jit(solution)/shard_map/ppermute | solution.py:47
  25.2 1.5 collective-permute-done.2.refs_0_.refs_1_.refs_18_
  28.6 5.2 %collective-permute-done.4.refs_2_.refs_26_ = bf16[784,128]{1,0:T(8,128)(2,1)S(1)} collective-permute-done((bf16[784,128]{1,0:T(8,128)(2,1)S(1)}, bf16[784,128]{1,0:T(8,128)(2,1)S(1)}, u32[]{:S(2)}, u32[]{:S(2)}) %collective-permute-start.4) | collective-permute-done | bytes 200736 | tf_op jit(solution)/shard_map/ppermute | solution.py:47
  33.8 3.3 %collective-permute-start.8 = (bf16[2352,128]{1,0:T(8,128)(2,1)S(1)}, bf16[2352,128]{1,0:T(8,128)(2,1)}, u32[]{:S(2)}, u32[]{:S(2)}) collective-permute-start(bf16[2352,128]{1,0:T(8,128)(2,1)S(1)} %shard_map.123), channel_id=1, source_target_pairs={{0,56},{8,0},{16,8},{24,16},{32,24},{40,32},{48,40},{56,48},{64,12... | collective-permute-start | bytes 1806344 | tf_op jit(solution)/shard_map/ppermute | solution.py:47
  37.1 3.3 %collective-permute-start.13 = (bf16[1568,128]{1,0:T(8,128)(2,1)S(1)}, bf16[1568,128]{1,0:T(8,128)(2,1)}, u32[]{:S(2)}, u32[]{:S(2)}) collective-permute-start(bf16[1568,128]{1,0:T(8,128)(2,1)S(1)} %collective-permute-done.1.refs_1_.refs_4_.refs_21_), channel_id=1, source_target_pairs={{0,56},{8,0},{16,8},{24,16},{32,24},{40,32},{48,40},{56,48},{64,12... | collective-permute-start | bytes 1204232 | tf_op jit(solution)/shard_map/ppermute | solution.py:47
  40.6 1.4 fusion
  42.1 13.9 %collective-permute-done.13.refs_3_.refs_6_.refs_23_ = bf16[1568,128]{1,0:T(8,128)(2,1)} collective-permute-done((bf16[1568,128]{1,0:T(8,128)(2,1)S(1)}, bf16[1568,128]{1,0:T(8,128)(2,1)}, u32[]{:S(2)}, u32[]{:S(2)}) %collective-permute-start.13) | collective-permute-done | bytes 401440 | tf_op jit(solution)/shard_map/ppermute | solution.py:47
  56.0 1.9 %shard_map.129 = bf16[3136,128]{1,0:T(8,128)(2,1)} custom-call(bf16[1568,128]{1,0:T(8,128)(2,1)S(1)} %collective-permute-done.refs_0_.refs_3_.refs_20_, bf16[1568,128]{1,0:T(8,128)(2,1)S(1)} %collective-permute-done.1.refs_1_.refs_4_.refs_21_, bf16[1568,128]{1,0:T(8,128)(2,1)S(1)} %collective-permute-done.11.refs_2_.refs_5_.refs_22_, ...), custom_call_target="tpu_custom_call" | custom-call | bytes 1605632 | tf_op jit(solution)/shard_map/pallas_call | solution.py:66
  59.2 3.8 %collective-permute-start.14 = (bf16[1568,128]{1,0:T(8,128)(2,1)}, bf16[1568,128]{1,0:T(8,128)(2,1)}, u32[]{:S(2)}, u32[]{:S(2)}) collective-permute-start(bf16[1568,128]{1,0:T(8,128)(2,1)} %collective-permute-done.13.refs_3_.refs_6_.refs_23_), channel_id=1, source_target_pairs={{0,56},{8,0},{16,8},{24,16},{32,24},{40,32},{48,40},{56,48},{64,12... | collective-permute-start | bytes 1204232 | tf_op jit(solution)/shard_map/ppermute | solution.py:47
  63.3 3.2 %collective-permute-start.9 = (bf16[2352,128]{1,0:T(8,128)(2,1)}, bf16[2352,128]{1,0:T(8,128)(2,1)}, u32[]{:S(2)}, u32[]{:S(2)}) collective-permute-start(bf16[2352,128]{1,0:T(8,128)(2,1)} %collective-permute-done.8.refs_28_), channel_id=1, source_target_pairs={{0,56},{8,0},{16,8},{24,16},{32,24},{40,32},{48,40},{56,48},{64,12... | collective-permute-start | bytes 1806344 | tf_op jit(solution)/shard_map/ppermute | solution.py:47
  68.1 4.3 %collective-permute-done.15.refs_2_.refs_14_ = bf16[784,128]{1,0:T(8,128)(2,1)S(1)} collective-permute-done((bf16[784,128]{1,0:T(8,128)(2,1)S(1)}, bf16[784,128]{1,0:T(8,128)(2,1)S(1)}, u32[]{:S(2)}, u32[]{:S(2)}) %collective-permute-start.15) | collective-permute-done | bytes 200736 | tf_op jit(solution)/shard_map/ppermute | solution.py:47
  73.9 2.8 %copy-done = bf16[1,768,4096]{2,1,0:T(8,128)(2,1)S(1)} copy-done((bf16[1,768,4096]{2,1,0:T(8,128)(2,1)S(1)}, bf16[1,768,4096]{2,1,0:T(8,128)(2,1)}, u32[]{:S(2)}) %copy-start) | copy-done | bytes 6291480
  76.7 2.2 %copy-done.1 = bf16[4096,512]{1,0:T(8,128)(2,1)S(1)} copy-done((bf16[4096,512]{1,0:T(8,128)(2,1)S(1)}, bf16[4096,512]{1,0:T(8,128)(2,1)}, u32[]{:S(2)}) %copy-start.1) | copy-done | bytes 4194328
  80.9 5.6 %shard_map.125 = (bf16[768,384]{1,0:T(8,128)(2,1)S(1)}, bf16[128,1024]{1,0:T(8,128)(2,1)S(1)}) custom-call(bf16[768,4096]{1,0:T(8,128)(2,1)S(1)} %bitcast.87, bf16[1,4096]{1,0:T(2,128)(2,1)S(1)} %broadcast_in_dim.116.gain_ref, bf16[4096,512]{1,0:T(8,128)(2,1)S(1)} %copy-done.1, bf16[4096,256]{1,0:T(8,128)(2,1)S(1)} %bitcast.86, f32[768,128]{1,0:T(8,128)S(1)} %copy-done.12, ...), custom_call_target="tpu_custom_call" | custom-call | flops 2684354560 | bytes 12582912 | tf_op jit(solution)/shard_map/pallas_call | solution.py:131
  88.1 2.0 %collective-permute-start.7 = (bf16[2352,128]{1,0:T(8,128)(2,1)}, bf16[2352,128]{1,0:T(8,128)(2,1)S(1)}, u32[]{:S(2)}, u32[]{:S(2)}) collective-permute-start(bf16[2352,128]{1,0:T(8,128)(2,1)} %collective-permute-done.6.refs_29_), channel_id=1, source_target_pairs={{0,8},{8,16},{16,24},{24,32},{32,40},{40,48},{48,56},{56,0},{64,72... | collective-permute-start | bytes 1806344 | tf_op jit(solution)/shard_map/ppermute | solution.py:47
  90.1 1.9 %shard_map.126 = bf16[2352,128]{1,0:T(8,128)(2,1)} custom-call(bf16[1568,128]{1,0:T(8,128)(2,1)S(1)} %collective-permute-done.12.refs_0_.refs_7_.refs_24_, bf16[1568,128]{1,0:T(8,128)(2,1)} %collective-permute-done.14.refs_1_.refs_0_.refs_8_.refs_25_, bf16[784,128]{1,0:T(8,128)(2,1)S(1)} %copy-done.17), custom_call_target="tpu_custom_call" | custom-call | bytes 1204224 | tf_op jit(solution)/shard_map/pallas_call | solution.py:66
  92.0 2.1 %collective-permute-start.16 = (bf16[2352,128]{1,0:T(8,128)(2,1)}, bf16[2352,128]{1,0:T(8,128)(2,1)S(1)}, u32[]{:S(2)}, u32[]{:S(2)}) collective-permute-start(bf16[2352,128]{1,0:T(8,128)(2,1)} %shard_map.126), channel_id=1, source_target_pairs={{0,64},{8,72},{16,80},{24,88},{32,96},{40,104},{48,112},{56,120},{... | collective-permute-start | bytes 1806344 | tf_op jit(solution)/shard_map/ppermute | solution.py:47
  98.2 1.4 collective-permute-start.25
  101.3 1.9 %shard_map.131 = bf16[1568,128]{1,0:T(8,128)(2,1)} custom-call(bf16[3136,128]{1,0:T(8,128)(2,1)} %collective-permute-done.24.refs_0_.refs_11_), custom_call_target="tpu_custom_call" | custom-call | bytes 802816 | tf_op jit(solution)/shard_map/pallas_call | solution.py:66
  103.2 2.0 %collective-permute-start.22 = (bf16[784,128]{1,0:T(8,128)(2,1)S(1)}, bf16[784,128]{1,0:T(8,128)(2,1)S(1)}, u32[]{:S(2)}, u32[]{:S(2)}) collective-permute-start(bf16[784,128]{1,0:T(8,128)(2,1)S(1)} %shard_map.128), channel_id=1, source_target_pairs={{0,64},{8,72},{16,80},{24,88},{32,96},{40,104},{48,112},{56,120},{... | collective-permute-start | bytes 602120 | tf_op jit(solution)/shard_map/ppermute | solution.py:47
  105.2 1.3 collective-permute-start.27
  106.5 2.6 %collective-permute-done.16.refs_2_.refs_15_.refs_0_ = bf16[2352,128]{1,0:T(8,128)(2,1)S(1)} collective-permute-done((bf16[2352,128]{1,0:T(8,128)(2,1)}, bf16[2352,128]{1,0:T(8,128)(2,1)S(1)}, u32[]{:S(2)}, u32[]{:S(2)}) %collective-permute-start.16) | collective-permute-done | bytes 602144 | tf_op jit(solution)/shard_map/ppermute | solution.py:47
  109.1 3.0 %collective-permute-start.26 = (bf16[1568,128]{1,0:T(8,128)(2,1)}, bf16[1568,128]{1,0:T(8,128)(2,1)}, u32[]{:S(2)}, u32[]{:S(2)}) collective-permute-start(bf16[1568,128]{1,0:T(8,128)(2,1)} %shard_map.131), channel_id=1, source_target_pairs={{0,192},{8,200},{16,208},{24,216},{32,224},{40,232},{48,240},{56,2... | collective-permute-start | bytes 1204232 | tf_op jit(solution)/shard_map/ppermute | solution.py:47
  112.1 2.2 %shard_map.127 = (bf16[1312,128]{1,0:T(8,128)(2,1)}, bf16[1056,128]{1,0:T(8,128)(2,1)}, bf16[1312,128]{1,0:T(8,128)(2,1)}, bf16[1056,128]{1,0:T(8,128)(2,1)}) custom-call(bf16[2352,128]{1,0:T(8,128)(2,1)S(1)} %collective-permute-done.7.refs_0_.refs_32_.refs_4_, bf16[2352,128]{1,0:T(8,128)(2,1)S(1)} %collective-permute-done.10.refs_1_.refs_33_.refs_5_, ...), custom_call_target="tpu_custom_call" | custom-call | bytes 2408448 | tf_op jit(solution)/shard_map/pallas_call | solution.py:88
  114.3 2.8 %collective-permute-done.22.refs_9_ = bf16[784,128]{1,0:T(8,128)(2,1)S(1)} collective-permute-done((bf16[784,128]{1,0:T(8,128)(2,1)S(1)}, bf16[784,128]{1,0:T(8,128)(2,1)S(1)}, u32[]{:S(2)}, u32[]{:S(2)}) %collective-permute-start.22) | collective-permute-done | bytes 200736 | tf_op jit(solution)/shard_map/ppermute | solution.py:47
  118.7 3.0 %collective-permute-start.19 = (bf16[1056,128]{1,0:T(8,128)(2,1)}, bf16[1056,128]{1,0:T(8,128)(2,1)}, u32[]{:S(2)}, u32[]{:S(2)}) collective-permute-start(bf16[1056,128]{1,0:T(8,128)(2,1)} %get-tuple-element.43), channel_id=1, source_target_pairs={{0,192},{8,200},{16,208},{24,216},{32,224},{40,232},{48,240},{56,2... | collective-permute-start | bytes 811016 | tf_op jit(solution)/shard_map/ppermute | solution.py:47
  122.5 2.9 %collective-permute-start.21 = (bf16[1056,128]{1,0:T(8,128)(2,1)}, bf16[1056,128]{1,0:T(8,128)(2,1)}, u32[]{:S(2)}, u32[]{:S(2)}) collective-permute-start(bf16[1056,128]{1,0:T(8,128)(2,1)} %get-tuple-element.45), channel_id=1, source_target_pairs={{0,56},{8,0},{16,8},{24,16},{32,24},{40,32},{48,40},{56,48},{64,12... | collective-permute-start | bytes 811016 | tf_op jit(solution)/shard_map/ppermute | solution.py:47
  135.9 20.7 %shard_map.133 = (bf16[2,5120,128]{2,1,0:T(8,128)(2,1)}, f32[1,1024]{1,0:T(1,128)S(1)}, f32[1,1024]{1,0:T(1,128)S(1)}, f32[128,1024]{1,0:T(8,128)S(1)}) custom-call(s32[8,20]{1,0:T(8,128)S(1)} %get-tuple-element.52.table, s32[4]{0:T(128)S(1)} %pad_add_fusion.count_ref, s32[1,512]{1,0:T(1,128)S(1)} %bitcast.95, ...), custom_call_target="tpu_custom_call" | custom-call | flops 1342177280 | bytes 2621440 | tf_op jit(solution)/shard_map/pallas_call | solution.py:334
  156.7 2.6 %shard_map.134 = (bf16[256,512]{1,0:T(8,128)(2,1)}, bf16[2,5120,128]{2,1,0:T(8,128)(2,1)}) custom-call(s32[8,20]{1,0:T(8,128)S(1)} %get-tuple-element.53.table, s32[4]{0:T(128)S(1)} %pad_add_fusion.count_ref, s32[1,512]{1,0:T(1,128)S(1)} %bitcast.96, f32[20,2,128]{2,1,0:T(2,128)S(1)} %pad_maximum_fusion.3.shift_ref, ...), custom_call_target="tpu_custom_call", output_to_operand_aliasing={{1}: (17, {})} | custom-call | flops 1342177280 | bytes 2621440 | tf_op jit(solution)/shard_map/pallas_call | solution.py:334
  (142 shorter events, 34.5 us)
Async XLA Ops:
  7.2 66.8 %all-gather.2.cloned.1.call-start = ((), (), s32[]{:S(2)}) async-start(), calls=%async_computation | async-start | bytes 7077888 | tf_op jit(solution)/shard_map/all_gather | solution.py:479
  9.9 15.2 %collective-permute-start = (bf16[1568,128]{1,0:T(8,128)(2,1)S(1)}, bf16[1568,128]{1,0:T(8,128)(2,1)S(1)}, u32[]{:S(2)}, u32[]{:S(2)}) collective-permute-start(bf16[1568,128]{1,0:T(8,128)(2,1)S(1)} %bitcast.88), channel_id=1, source_target_pairs={{0,8},{8,16},{16,24},{24,32},{32,40},{40,48},{48,56},{56,0},{64,72... | collective-permute-start | bytes 1204232 | tf_op jit(solution)/shard_map/ppermute | solution.py:47
  11.9 13.2 %collective-permute-start.1 = (bf16[1568,128]{1,0:T(8,128)(2,1)S(1)}, bf16[1568,128]{1,0:T(8,128)(2,1)S(1)}, u32[]{:S(2)}, u32[]{:S(2)}) collective-permute-start(bf16[1568,128]{1,0:T(8,128)(2,1)S(1)} %bitcast.89), channel_id=1, source_target_pairs={{0,56},{8,0},{16,8},{24,16},{32,24},{40,32},{48,40},{56,48},{64,12... | collective-permute-start | bytes 1204232 | tf_op jit(solution)/shard_map/ppermute | solution.py:47
  15.9 10.8 %collective-permute-start.2 = (bf16[1568,128]{1,0:T(8,128)(2,1)S(1)}, bf16[1568,128]{1,0:T(8,128)(2,1)S(1)}, u32[]{:S(2)}, u32[]{:S(2)}) collective-permute-start(bf16[1568,128]{1,0:T(8,128)(2,1)S(1)} %bitcast.90), channel_id=1, source_target_pairs={{0,64},{8,72},{16,80},{24,88},{32,96},{40,104},{48,112},{56,120},{... | collective-permute-start | bytes 1204232 | tf_op jit(solution)/shard_map/ppermute | solution.py:47
  17.4 10.5 %collective-permute-start.3 = (bf16[1568,128]{1,0:T(8,128)(2,1)S(1)}, bf16[1568,128]{1,0:T(8,128)(2,1)S(1)}, u32[]{:S(2)}, u32[]{:S(2)}) collective-permute-start(bf16[1568,128]{1,0:T(8,128)(2,1)S(1)} %bitcast.91), channel_id=1, source_target_pairs={{0,192},{8,200},{16,208},{24,216},{32,224},{40,232},{48,240},{56,2... | collective-permute-start | bytes 1204232 | tf_op jit(solution)/shard_map/ppermute | solution.py:47
  25.1 32.8 %copy-start.2 = (bf16[1568,128]{1,0:T(8,128)(2,1)}, bf16[1568,128]{1,0:T(8,128)(2,1)S(1)}, u32[]{:S(2)}) copy-start(bf16[1568,128]{1,0:T(8,128)(2,1)S(1)} %collective-permute-done.refs_0_.refs_3_.refs_20_) | copy-start | bytes 1204228
  25.2 32.8 %copy-start.4 = (bf16[1568,128]{1,0:T(8,128)(2,1)}, bf16[1568,128]{1,0:T(8,128)(2,1)S(1)}, u32[]{:S(2)}) copy-start(bf16[1568,128]{1,0:T(8,128)(2,1)S(1)} %collective-permute-done.1.refs_1_.refs_4_.refs_21_) | copy-start | bytes 1204228
  27.9 12.5 %collective-permute-start.11 = (bf16[1568,128]{1,0:T(8,128)(2,1)S(1)}, bf16[1568,128]{1,0:T(8,128)(2,1)S(1)}, u32[]{:S(2)}, u32[]{:S(2)}) collective-permute-start(bf16[1568,128]{1,0:T(8,128)(2,1)S(1)} %collective-permute-done.refs_0_.refs_3_.refs_20_), channel_id=1, source_target_pairs={{0,8},{8,16},{16,24},{24,32},{32,40},{40,48},{48,56},{56,0},{64,72... | collective-permute-start | bytes 1204232 | tf_op jit(solution)/shard_map/ppermute | solution.py:47
  27.9 5.8 %collective-permute-start.4 = (bf16[784,128]{1,0:T(8,128)(2,1)S(1)}, bf16[784,128]{1,0:T(8,128)(2,1)S(1)}, u32[]{:S(2)}, u32[]{:S(2)}) collective-permute-start(bf16[784,128]{1,0:T(8,128)(2,1)S(1)} %shard_map.122), channel_id=1, source_target_pairs={{0,192},{8,200},{16,208},{24,216},{32,224},{40,232},{48,240},{56,2... | collective-permute-start | bytes 602120 | tf_op jit(solution)/shard_map/ppermute | solution.py:47
  28.6 38.1 %copy-start.26 = (bf16[4096,2,128]{2,1,0:T(2,128)(2,1)S(1)}, bf16[4096,2,128]{2,1,0:T(2,128)(2,1)}, u32[]{:S(2)}) copy-start(bf16[4096,2,128]{2,1,0:T(2,128)(2,1)} %param.21) | copy-start | bytes 6291460
  33.8 29.5 %collective-permute-start.8 = (bf16[2352,128]{1,0:T(8,128)(2,1)S(1)}, bf16[2352,128]{1,0:T(8,128)(2,1)}, u32[]{:S(2)}, u32[]{:S(2)}) collective-permute-start(bf16[2352,128]{1,0:T(8,128)(2,1)S(1)} %shard_map.123), channel_id=1, source_target_pairs={{0,56},{8,0},{16,8},{24,16},{32,24},{40,32},{48,40},{56,48},{64,12... | collective-permute-start | bytes 1806344 | tf_op jit(solution)/shard_map/ppermute | solution.py:47
  37.1 29.5 %collective-permute-start.5 = (bf16[2352,128]{1,0:T(8,128)(2,1)S(1)}, bf16[2352,128]{1,0:T(8,128)(2,1)}, u32[]{:S(2)}, u32[]{:S(2)}) collective-permute-start(bf16[2352,128]{1,0:T(8,128)(2,1)S(1)} %shard_map.123), channel_id=1, source_target_pairs={{0,8},{8,16},{16,24},{24,32},{32,40},{40,48},{48,56},{56,0},{64,72... | collective-permute-start | bytes 1806344 | tf_op jit(solution)/shard_map/ppermute | solution.py:47
  37.1 18.9 %collective-permute-start.13 = (bf16[1568,128]{1,0:T(8,128)(2,1)S(1)}, bf16[1568,128]{1,0:T(8,128)(2,1)}, u32[]{:S(2)}, u32[]{:S(2)}) collective-permute-start(bf16[1568,128]{1,0:T(8,128)(2,1)S(1)} %collective-permute-done.1.refs_1_.refs_4_.refs_21_), channel_id=1, source_target_pairs={{0,56},{8,0},{16,8},{24,16},{32,24},{40,32},{48,40},{56,48},{64,12... | collective-permute-start | bytes 1204232 | tf_op jit(solution)/shard_map/ppermute | solution.py:47
  40.4 22.6 %collective-permute-start.12 = (bf16[1568,128]{1,0:T(8,128)(2,1)S(1)}, bf16[1568,128]{1,0:T(8,128)(2,1)S(1)}, u32[]{:S(2)}, u32[]{:S(2)}) collective-permute-start(bf16[1568,128]{1,0:T(8,128)(2,1)S(1)} %collective-permute-done.11.refs_2_.refs_5_.refs_22_), channel_id=1, source_target_pairs={{0,8},{8,16},{16,24},{24,32},{32,40},{40,48},{48,56},{56,0},{64,72... | collective-permute-start | bytes 1204232 | tf_op jit(solution)/shard_map/ppermute | solution.py:47
  58.0 36.8 %collective-permute-start.23 = (bf16[3136,128]{1,0:T(8,128)(2,1)}, bf16[3136,128]{1,0:T(8,128)(2,1)}, u32[]{:S(2)}, u32[]{:S(2)}) collective-permute-start(bf16[3136,128]{1,0:T(8,128)(2,1)} %shard_map.129), channel_id=1, source_target_pairs={{0,64},{8,72},{16,80},{24,88},{32,96},{40,104},{48,112},{56,120},{... | collective-permute-start | bytes 2408456 | tf_op jit(solution)/shard_map/ppermute | solution.py:47
  59.2 30.9 %collective-permute-start.14 = (bf16[1568,128]{1,0:T(8,128)(2,1)}, bf16[1568,128]{1,0:T(8,128)(2,1)}, u32[]{:S(2)}, u32[]{:S(2)}) collective-permute-start(bf16[1568,128]{1,0:T(8,128)(2,1)} %collective-permute-done.13.refs_3_.refs_6_.refs_23_), channel_id=1, source_target_pairs={{0,56},{8,0},{16,8},{24,16},{32,24},{40,32},{48,40},{56,48},{64,12... | collective-permute-start | bytes 1204232 | tf_op jit(solution)/shard_map/ppermute | solution.py:47
  63.0 9.4 %collective-permute-start.15 = (bf16[784,128]{1,0:T(8,128)(2,1)S(1)}, bf16[784,128]{1,0:T(8,128)(2,1)S(1)}, u32[]{:S(2)}, u32[]{:S(2)}) collective-permute-start(bf16[784,128]{1,0:T(8,128)(2,1)S(1)} %shard_map.124), channel_id=1, source_target_pairs={{0,8},{8,16},{16,24},{24,32},{32,40},{40,48},{48,56},{56,0},{64,72... | collective-permute-start | bytes 602120 | tf_op jit(solution)/shard_map/ppermute | solution.py:47
  63.3 24.7 %collective-permute-start.9 = (bf16[2352,128]{1,0:T(8,128)(2,1)}, bf16[2352,128]{1,0:T(8,128)(2,1)}, u32[]{:S(2)}, u32[]{:S(2)}) collective-permute-start(bf16[2352,128]{1,0:T(8,128)(2,1)} %collective-permute-done.8.refs_28_), channel_id=1, source_target_pairs={{0,56},{8,0},{16,8},{24,16},{32,24},{40,32},{48,40},{56,48},{64,12... | collective-permute-start | bytes 1806344 | tf_op jit(solution)/shard_map/ppermute | solution.py:47
  66.5 21.5 %collective-permute-start.6 = (bf16[2352,128]{1,0:T(8,128)(2,1)}, bf16[2352,128]{1,0:T(8,128)(2,1)}, u32[]{:S(2)}, u32[]{:S(2)}) collective-permute-start(bf16[2352,128]{1,0:T(8,128)(2,1)} %collective-permute-done.5.refs_27_), channel_id=1, source_target_pairs={{0,8},{8,16},{16,24},{24,32},{32,40},{40,48},{48,56},{56,0},{64,72... | collective-permute-start | bytes 1806344 | tf_op jit(solution)/shard_map/ppermute | solution.py:47
  73.1 25.0 %collective-permute-start.24 = (bf16[3136,128]{1,0:T(8,128)(2,1)}, bf16[3136,128]{1,0:T(8,128)(2,1)}, u32[]{:S(2)}, u32[]{:S(2)}) collective-permute-start(bf16[3136,128]{1,0:T(8,128)(2,1)} %shard_map.129), channel_id=1, source_target_pairs={{0,192},{8,200},{16,208},{24,216},{32,224},{40,232},{48,240},{56,2... | collective-permute-start | bytes 2408456 | tf_op jit(solution)/shard_map/ppermute | solution.py:47
  88.0 15.2 %collective-permute-start.10 = (bf16[2352,128]{1,0:T(8,128)(2,1)}, bf16[2352,128]{1,0:T(8,128)(2,1)S(1)}, u32[]{:S(2)}, u32[]{:S(2)}) collective-permute-start(bf16[2352,128]{1,0:T(8,128)(2,1)} %collective-permute-done.9.refs_30_), channel_id=1, source_target_pairs={{0,56},{8,0},{16,8},{24,16},{32,24},{40,32},{48,40},{56,48},{64,12... | collective-permute-start | bytes 1806344 | tf_op jit(solution)/shard_map/ppermute | solution.py:47
  88.1 17.2 %collective-permute-start.7 = (bf16[2352,128]{1,0:T(8,128)(2,1)}, bf16[2352,128]{1,0:T(8,128)(2,1)S(1)}, u32[]{:S(2)}, u32[]{:S(2)}) collective-permute-start(bf16[2352,128]{1,0:T(8,128)(2,1)} %collective-permute-done.6.refs_29_), channel_id=1, source_target_pairs={{0,8},{8,16},{16,24},{24,32},{32,40},{40,48},{48,56},{56,0},{64,72... | collective-permute-start | bytes 1806344 | tf_op jit(solution)/shard_map/ppermute | solution.py:47
  92.0 17.2 %collective-permute-start.16 = (bf16[2352,128]{1,0:T(8,128)(2,1)}, bf16[2352,128]{1,0:T(8,128)(2,1)S(1)}, u32[]{:S(2)}, u32[]{:S(2)}) collective-permute-start(bf16[2352,128]{1,0:T(8,128)(2,1)} %shard_map.126), channel_id=1, source_target_pairs={{0,64},{8,72},{16,80},{24,88},{32,96},{40,104},{48,112},{56,120},{... | collective-permute-start | bytes 1806344 | tf_op jit(solution)/shard_map/ppermute | solution.py:47
  94.7 17.4 %collective-permute-start.17 = (bf16[2352,128]{1,0:T(8,128)(2,1)}, bf16[2352,128]{1,0:T(8,128)(2,1)}, u32[]{:S(2)}, u32[]{:S(2)}) collective-permute-start(bf16[2352,128]{1,0:T(8,128)(2,1)} %shard_map.126), channel_id=1, source_target_pairs={{0,192},{8,200},{16,208},{24,216},{32,224},{40,232},{48,240},{56,2... | collective-permute-start | bytes 1806344 | tf_op jit(solution)/shard_map/ppermute | solution.py:47
  98.2 23.5 %collective-permute-start.25 = (bf16[1568,128]{1,0:T(8,128)(2,1)S(1)}, bf16[1568,128]{1,0:T(8,128)(2,1)S(1)}, u32[]{:S(2)}, u32[]{:S(2)}) collective-permute-start(bf16[1568,128]{1,0:T(8,128)(2,1)S(1)} %shard_map.130), channel_id=1, source_target_pairs={{0,64},{8,72},{16,80},{24,88},{32,96},{40,104},{48,112},{56,120},{... | collective-permute-start | bytes 1204232 | tf_op jit(solution)/shard_map/ppermute | solution.py:47
  103.2 13.9 %collective-permute-start.22 = (bf16[784,128]{1,0:T(8,128)(2,1)S(1)}, bf16[784,128]{1,0:T(8,128)(2,1)S(1)}, u32[]{:S(2)}, u32[]{:S(2)}) collective-permute-start(bf16[784,128]{1,0:T(8,128)(2,1)S(1)} %shard_map.128), channel_id=1, source_target_pairs={{0,64},{8,72},{16,80},{24,88},{32,96},{40,104},{48,112},{56,120},{... | collective-permute-start | bytes 602120 | tf_op jit(solution)/shard_map/ppermute | solution.py:47
  105.2 12.8 %collective-permute-start.27 = (bf16[784,128]{1,0:T(8,128)(2,1)S(1)}, bf16[784,128]{1,0:T(8,128)(2,1)S(1)}, u32[]{:S(2)}, u32[]{:S(2)}) collective-permute-start(bf16[784,128]{1,0:T(8,128)(2,1)S(1)} %shard_map.132), channel_id=1, source_target_pairs={{0,56},{8,0},{16,8},{24,16},{32,24},{40,32},{48,40},{56,48},{64,12... | collective-permute-start | bytes 602120 | tf_op jit(solution)/shard_map/ppermute | solution.py:47
  109.1 17.9 %collective-permute-start.26 = (bf16[1568,128]{1,0:T(8,128)(2,1)}, bf16[1568,128]{1,0:T(8,128)(2,1)}, u32[]{:S(2)}, u32[]{:S(2)}) collective-permute-start(bf16[1568,128]{1,0:T(8,128)(2,1)} %shard_map.131), channel_id=1, source_target_pairs={{0,192},{8,200},{16,208},{24,216},{32,224},{40,232},{48,240},{56,2... | collective-permute-start | bytes 1204232 | tf_op jit(solution)/shard_map/ppermute | solution.py:47
  114.3 42.4 %collective-permute-start.18 = (bf16[1312,128]{1,0:T(8,128)(2,1)}, bf16[1312,128]{1,0:T(8,128)(2,1)}, u32[]{:S(2)}, u32[]{:S(2)}) collective-permute-start(bf16[1312,128]{1,0:T(8,128)(2,1)} %get-tuple-element.42), channel_id=1, source_target_pairs={{0,64},{8,72},{16,80},{24,88},{32,96},{40,104},{48,112},{56,120},{... | collective-permute-start | bytes 1007624 | tf_op jit(solution)/shard_map/ppermute | solution.py:47
  117.8 38.9 %collective-permute-start.20 = (bf16[1312,128]{1,0:T(8,128)(2,1)}, bf16[1312,128]{1,0:T(8,128)(2,1)}, u32[]{:S(2)}, u32[]{:S(2)}) collective-permute-start(bf16[1312,128]{1,0:T(8,128)(2,1)} %get-tuple-element.44), channel_id=1, source_target_pairs={{0,8},{8,16},{16,24},{24,32},{32,40},{40,48},{48,56},{56,0},{64,72... | collective-permute-start | bytes 1007624 | tf_op jit(solution)/shard_map/ppermute | solution.py:47
  118.7 37.9 %collective-permute-start.19 = (bf16[1056,128]{1,0:T(8,128)(2,1)}, bf16[1056,128]{1,0:T(8,128)(2,1)}, u32[]{:S(2)}, u32[]{:S(2)}) collective-permute-start(bf16[1056,128]{1,0:T(8,128)(2,1)} %get-tuple-element.43), channel_id=1, source_target_pairs={{0,192},{8,200},{16,208},{24,216},{32,224},{40,232},{48,240},{56,2... | collective-permute-start | bytes 811016 | tf_op jit(solution)/shard_map/ppermute | solution.py:47
  122.5 34.2 %collective-permute-start.21 = (bf16[1056,128]{1,0:T(8,128)(2,1)}, bf16[1056,128]{1,0:T(8,128)(2,1)}, u32[]{:S(2)}, u32[]{:S(2)}) collective-permute-start(bf16[1056,128]{1,0:T(8,128)(2,1)} %get-tuple-element.45), channel_id=1, source_target_pairs={{0,56},{8,0},{16,8},{24,16},{32,24},{40,32},{48,40},{56,48},{64,12... | collective-permute-start | bytes 811016 | tf_op jit(solution)/shard_map/ppermute | solution.py:47
  (31 other events, 200.6 us)
Sparse Core Ops, SparseCore 0:
  9.8 44.2 all-gather.1
